TPU v7x, 512 devices: a whole 4x4x16 slice. The times are simulated.
512 devices in a mesh: dp: 16 (over x_hi, y, core), mp: 32 (over z, x_lo).
Axes of the slice: x: 4 (x_hi: 2, x_lo: 2; x = x_hi * 2 + x_lo), y: 4, z: 16, core: 2. Of those that a mesh axis runs over, the one named last changes fastest.
Arguments:
- activations: bfloat16 [3072, 8192], P('mp', 'dp'), may hold values from -240 to 240
- w_qkv: bfloat16 [3072, 9216], P(None, 'mp'), may hold values from -0.109375 to 0.109375
- w_out: bfloat16 [3072, 3072], P(None, 'mp'), may hold values from -0.875 to 0.875
- d_branch: bfloat16 [3072, 8192], P('mp', 'dp'), may hold values from -0.25 to 0.25
Outputs:
- branch_out: bfloat16 [3072, 8192], P('mp', 'dp')
- grad_qkv: bfloat16 [3072, 9216], P('dp', 'mp')
- grad_out: bfloat16 [3072, 3072], P('dp', 'mp')
All inputs are finite; a program needn't handle non-finite values.
Results may differ from a plain program's by a relative error of at most 0.03.
Values may be sent and summed in bfloat16 or wider, within the bound.
No kernel may reach another device: no remote copies, remote signals or barrier semaphores. Data moves between devices by JAX's collectives and lax.ppermute only.
A program may use at most 64 MiB of HBM per device.

v0:
```python
import jax
import jax.numpy as jnp
from jax import lax
from jax.sharding import PartitionSpec as P

PATCHES = 256


epsilon = 1e-06
highest = lax.Precision.HIGHEST


def normalize_last(values):
    centre = values - jnp.mean(values, -1, keepdims=True)
    inverse = lax.rsqrt(jnp.mean(centre * centre, -1, keepdims=True) + epsilon)
    return (centre * inverse, inverse)


def attend(queries, keys_in, values_in, grad_in):
    query_norm, query_inv = normalize_last(queries.astype(jnp.float32))
    key_norm, key_inv = normalize_last(keys_in.astype(jnp.float32))
    scaling = queries.shape[-1] ** (-0.5)
    scores = jnp.einsum("ipc,iqc->ipq", query_norm, key_norm, precision=highest) * scaling
    exponent = jnp.exp(scores)
    attention = exponent / jnp.sum(exponent, -1, keepdims=True)
    attention_low = lax.optimization_barrier(attention.astype(jnp.bfloat16))
    attention_wide = attention_low.astype(jnp.float32)
    values_wide = values_in.astype(jnp.float32)
    grad_wide = grad_in.astype(jnp.float32)
    heads_out = jnp.einsum("ipq,iqc->ipc", attention_wide, values_wide, precision=highest).astype(
        jnp.bfloat16
    )
    grad_weights = jnp.einsum("ipc,iqc->ipq", grad_wide, values_wide, precision=highest)
    grad_values = jnp.einsum("ipq,ipc->iqc", attention_wide, grad_wide, precision=highest)
    grad_scores = attention * (grad_weights - jnp.sum(grad_weights * attention, -1, keepdims=True))
    grad_qnorm = jnp.einsum("ipq,iqc->ipc", grad_scores, key_norm, precision=highest) * scaling
    grad_knorm = jnp.einsum("ipq,ipc->iqc", grad_scores, query_norm, precision=highest) * scaling
    grad_query = (
        grad_qnorm
        - jnp.mean(grad_qnorm, -1, keepdims=True)
        - query_norm * jnp.mean(grad_qnorm * query_norm, -1, keepdims=True)
    ) * query_inv
    grad_key = (
        grad_knorm
        - jnp.mean(grad_knorm, -1, keepdims=True)
        - key_norm * jnp.mean(grad_knorm * key_norm, -1, keepdims=True)
    ) * key_inv
    grad_proj = jnp.concatenate([grad_query, grad_key, grad_values], -1).astype(jnp.bfloat16)
    return (heads_out, grad_proj)


def on_device(activations, w_qkv, w_out, d_branch):
    features = w_qkv.shape[0]
    head_size = w_out.shape[1]
    tokens = activations.shape[1]
    values = activations.astype(jnp.float32)
    totals = lax.psum((jnp.sum(values, 0), jnp.sum(values * values, 0)), "mp")
    token_mean = totals[0] / features
    variance = totals[1] / features - token_mean * token_mean
    normed = ((values - token_mean) * lax.rsqrt(variance + epsilon)).astype(jnp.bfloat16)
    normed_full = lax.all_gather(normed, "mp", axis=0, tiled=True)
    contract_rows = (((0,), (0,)), ((), ()))
    projected = lax.dot_general(
        normed_full, w_qkv, contract_rows, preferred_element_type=jnp.float32
    ).astype(jnp.bfloat16)
    cot_full = lax.all_gather(d_branch, "mp", axis=0, tiled=True)
    grad_heads = lax.dot_general(
        cot_full, w_out, contract_rows, preferred_element_type=jnp.float32
    ).astype(jnp.bfloat16)
    images = tokens // PATCHES
    shaped = projected.reshape(images, PATCHES, 3 * head_size)
    outputs, grad_proj = attend(
        shaped[..., :head_size],
        shaped[..., head_size : 2 * head_size],
        shaped[..., 2 * head_size :],
        grad_heads.reshape(images, PATCHES, head_size),
    )
    outputs = outputs.reshape(tokens, head_size)
    grad_proj = grad_proj.reshape(tokens, 3 * head_size)
    branch_out = lax.psum_scatter(
        lax.dot_general(
            w_out, outputs, (((1,), (1,)), ((), ())), preferred_element_type=jnp.float32
        ).astype(jnp.bfloat16),
        "mp",
        scatter_dimension=0,
        tiled=True,
    )
    part_qkv = jnp.dot(normed_full, grad_proj, preferred_element_type=jnp.float32)
    part_out = jnp.dot(cot_full, outputs, preferred_element_type=jnp.float32)
    sum_qkv, sum_out = (
        lax.psum_scatter(
            part_qkv.astype(jnp.bfloat16), "dp", scatter_dimension=0, tiled=True
        ).astype(jnp.float32),
        lax.psum_scatter(
            part_out.astype(jnp.bfloat16), "dp", scatter_dimension=0, tiled=True
        ).astype(jnp.float32),
    )
    return (branch_out, sum_qkv.astype(jnp.bfloat16), sum_out.astype(jnp.bfloat16))


def solution(mesh):
    in_specs = (P("mp", "dp"), P(None, "mp"), P(None, "mp"), P("mp", "dp"))
    out_specs = (P("mp", "dp"), P("dp", "mp"), P("dp", "mp"))
    return jax.shard_map(
        on_device, mesh=mesh, in_specs=in_specs, out_specs=out_specs, check_vma=False
    )
```

profile of v0, /device:TPU:12, one launch (start us, length us, event | category | flops | bytes accessed | tf_op | source)
XLA Modules:
  0.0 695.3 jit_solution(16590090724650465133)
XLA Ops:
  7.2 1.1 convert_reduce_fusion
  8.3 70.1 %all-reduce = (f32[512]{0:T(512)S(1)}, f32[512]{0:T(512)S(1)}) all-reduce(f32[512]{0:T(512)S(1)} %get-tuple-element.17, f32[512]{0:T(512)S(1)} %get-tuple-element.16), channel_id=1, replica_groups=mesh['dp'=16,'mp'=32] {'mp'}, use_global_device_ids=true, to_apply=%region_3.0 | all-reduce | flops 1024 | bytes 8192 | tf_op jit(solution)/shard_map/psum | solution.py:57
  78.4 1.6 fusion.35
  80.0 0.7 all-gather.5.cloned.1.call-update
  80.7 131.4 %all-gather.3.cloned.1.call-done = bf16[3072,512]{1,0:T(8,128)(2,1)} async-done(((bf16[96,512]{1,0:T(8,128)(2,1)}), bf16[3072,512]{1,0:T(8,128)(2,1)}) %all-gather.3.cloned.1.call-update) | async-done | bytes 3145744 | tf_op jit(solution)/shard_map/all_gather | solution.py:61
  212.1 3.0 convolution_convert_fusion.3
  215.2 0.2 fusion.61
  215.6 0.7 fusion.2
  216.3 0.3 fusion.11
  216.5 132.1 %all-gather.5.cloned.1.call-done = bf16[3072,512]{1,0:T(8,128)(2,1)} async-done(((bf16[96,512]{1,0:T(8,128)(2,1)}), bf16[3072,512]{1,0:T(8,128)(2,1)}) %all-gather.5.cloned.1.call-update) | async-done | bytes 3145744 | tf_op jit(solution)/shard_map/all_gather | solution.py:66
  348.7 2.5 convolution_convert_fusion.4
  351.2 0.3 multiply_reduce_fusion
  351.5 1.4 fusion.60
  352.9 1.2 fusion.59
  354.1 0.2 fusion.4
  354.3 1.1 fusion.1
  355.4 1.2 copy.54
  356.8 0.2 fusion.3
  357.2 5.2 convolution_convert_fusion.1
  362.4 2.7 fusion
  365.1 4.7 copy.52
  369.8 71.4 %reduce-scatter.12.cloned.1.call-done = bf16[192,96]{1,0:T(8,128)(2,1)} async-done(((bf16[3072,96]{1,0:T(8,128)(2,1)}), bf16[192,96]{1,0:T(8,128)(2,1)}) %reduce-scatter.12.cloned.1.call-update) | async-done | bytes 36880
  441.2 100.6 %reduce-scatter.8.cloned.1.call-done = bf16[192,288]{1,0:T(8,128)(2,1)} async-done(((bf16[3072,288]{1,0:T(8,128)(2,1)}), bf16[192,288]{1,0:T(8,128)(2,1)}) %reduce-scatter.8.cloned.1.call-update) | async-done | bytes 110608 | tf_op jit(solution)/shard_map/reduce_scatter | solution.py:91
  541.8 146.9 %reduce-scatter.10.cloned.1.call-done = bf16[96,512]{1,0:T(8,128)(2,1)} async-done(((bf16[3072,512]{1,0:T(8,128)(2,1)}), bf16[96,512]{1,0:T(8,128)(2,1)}) %reduce-scatter.10.cloned.1.call-update) | async-done | bytes 98320
  (40 shorter events, 0.7 us)
Async XLA Ops:
  7.2 205.0 %copy-start = (bf16[3072,288]{0,1:T(8,128)(2,1)S(1)}, bf16[3072,288]{0,1:T(8,128)(2,1)}, u32[]{:S(2)}) copy-start(bf16[3072,288]{0,1:T(8,128)(2,1)} %param.5) | copy-start | bytes 5308420
  7.2 205.0 %all-gather.3.cloned.1.call-start = ((), (), s32[]{:S(2)}) async-start(), calls=%async_computation.3 | async-start | bytes 3244032 | tf_op jit(solution)/shard_map/all_gather | solution.py:61
  79.9 268.7 %all-gather.5.cloned.1.call-start = ((), (), s32[]{:S(2)}) async-start(), calls=%async_computation.4 | async-start | bytes 3244032 | tf_op jit(solution)/shard_map/all_gather | solution.py:66
  80.7 360.5 %reduce-scatter.12.cloned.1.call-start = ((), (), s32[]{:S(2)}) async-start(), calls=%async_computation.7 | async-start | bytes 835584
  215.1 133.6 %copy-start.2 = (bf16[3072,96]{0,1:T(8,128)(2,1)S(1)}, bf16[3072,96]{0,1:T(8,128)(2,1)}, u32[]{:S(2)}) copy-start(bf16[3072,96]{0,1:T(8,128)(2,1)} %param.6) | copy-start | bytes 1769476
  351.2 3.1 copy-start.1
  354.2 2.5 copy-start.5
  354.3 2.8 copy-start.4
  356.7 185.2 %reduce-scatter.8.cloned.1.call-start = ((), (), s32[]{:S(2)}) async-start(), calls=%async_computation.5 | async-start | bytes 2506752 | tf_op jit(solution)/shard_map/reduce_scatter | solution.py:91
  357.2 5.3 copy-start.3
  362.4 326.4 %reduce-scatter.10.cloned.1.call-start = ((), (), s32[]{:S(2)}) async-start(), calls=%async_computation.6 | async-start | bytes 3244032
Sparse Core Ops, SparseCore 0:
  80.1 132.0 all-gather.2
  214.2 134.4 all-gather.4
  356.8 84.3 reduce-scatter.11
  447.3 94.5 reduce-scatter.7
  545.1 143.6 reduce-scatter.9
where the time goes:
time: 696 us; the launch traced here: 695 us
  waiting for transfers between devices  583 us (84%)
  blocking collectives  70.1 us (10%)
  matrix products  18.3 us (3%)
  between operations  14 us (2%)
    unnamed x7, waiting for transfers between devices  219 us
    all_gather x1, waiting for transfers between devices, on_device(): cot_full = lax.all_gather(d_branch, 'mp', axis=0, tiled=True)  132 us
    all_gather x1, waiting for transfers between devices, on_device(): normed_full = lax.all_gather(normed, 'mp', axis=0, tiled=True)  131 us
    reduce_scatter x1, waiting for transfers between devices, on_device(): lax.psum_scatter(part_qkv.astype(jnp.bfloat16), 'dp', scatter_dimension=0...  101 us
    psum x1, blocking collectives, on_device(): totals = lax.psum((jnp.sum(values, 0), jnp.sum(values * values, 0)), 'mp')  70.1 us
  transfers between devices with their start and end apart: 5, of which 5 were waited for; matrix products, arithmetic and copies ran while one was open for 2% of the time, Pallas kernels for 0%

commit v1 on v0

v1 whole, which is shorter than its diff:
```python
import functools

import jax
import jax.numpy as jnp
from jax import lax
from jax.experimental import pallas as pl
from jax.experimental.pallas import tpu as pltpu
from jax.sharding import Mesh
from jax.sharding import PartitionSpec as P

PATCHES = 256
epsilon = 1e-06
highest = lax.Precision.HIGHEST
low = jnp.bfloat16
wide = jnp.float32


def contract(left, right, left_dim, right_dim, precision=None):
    return lax.dot_general(
        left,
        right,
        (((left_dim,), (right_dim,)), ((), ())),
        precision=precision,
        preferred_element_type=wide,
    )


def normalize_first(values):
    centre = values - jnp.mean(values, 0, keepdims=True)
    inverse = lax.rsqrt(jnp.mean(centre * centre, 0, keepdims=True) + epsilon)
    return (centre * inverse, inverse)


def forward_kernel(
    part, head, gathered, own, other, normed, attention, query, key, inverses, value, heads, branch
):
    features = normed.shape[0]
    blocks = features // part

    def rows_of(block):
        return gathered[pl.ds(pl.multiple_of(2 * part * block, part), part), :].astype(wide)

    zero = jnp.zeros((1, PATCHES), wide)
    total = lax.fori_loop(
        0, blocks, lambda b, t: t + jnp.sum(rows_of(b), 0, keepdims=True), zero
    )
    mean = total / features

    def squares(block, carried):
        centre = rows_of(block) - mean
        return carried + jnp.sum(centre * centre, 0, keepdims=True)

    variance = lax.fori_loop(0, blocks, squares, zero) / features
    scale = lax.rsqrt(variance + epsilon)

    def write(block, carried):
        at = pl.ds(pl.multiple_of(part * block, part), part)
        normed[at, :] = ((rows_of(block) - mean) * scale).astype(low)
        return carried

    lax.fori_loop(0, blocks, write, 0)
    for slot, weights in enumerate((own, other)):
        projected = contract(weights[: 3 * head, :], normed[...], 1, 0).astype(low)
        query_norm, query_inv = normalize_first(projected[:head].astype(wide))
        key_norm, key_inv = normalize_first(projected[head : 2 * head].astype(wide))
        values = projected[2 * head :]
        scores = contract(key_norm, query_norm, 0, 0, highest) * head ** (-0.5)
        exponent = jnp.exp(scores)
        attend = exponent / jnp.sum(exponent, 0, keepdims=True)
        attention[slot] = attend
        query[slot] = query_norm
        key[slot] = key_norm
        inverses[slot, 0:1, :] = query_inv
        inverses[slot, 1:2, :] = key_inv
        value[slot] = values
        heads[slot] = contract(values, attend.astype(low), 1, 0).astype(low)
    both_heads = heads[...].reshape(2 * head, PATCHES)
    step = 512
    for start in range(0, features, step):
        both = jnp.concatenate(
            [own[3 * head :, start : start + step], other[3 * head :, start : start + step]], 0
        )
        branch[start : start + step, :] = contract(both, both_heads, 0, 0).astype(low)


def backward_kernel(
    part,
    head,
    place,
    gathered,
    own,
    other,
    normed,
    attention,
    query,
    key,
    inverses,
    value,
    heads,
    shares,
    cotangent,
):
    features = normed.shape[0]
    blocks = features // part
    for block in range(blocks):
        cotangent[part * block : part * (block + 1), :] = gathered[
            2 * part * block + part : 2 * part * (block + 1), :
        ]
    scaling = head ** (-0.5)
    cores, _, chips, rows, columns = shares.shape
    for slot, weights in enumerate((own, other)):
        grad = contract(weights[...], cotangent[...], 1, 0).astype(low)
        attend = attention[slot]
        query_norm, key_norm = query[slot], key[slot]
        grad_weights = contract(value[slot], grad, 0, 0)
        grad_values = contract(grad, attend.astype(low), 1, 1)
        grad_scores = attend * (grad_weights - jnp.sum(grad_weights * attend, 0, keepdims=True))
        grad_qnorm = contract(key_norm, grad_scores, 1, 0, highest) * scaling
        grad_knorm = contract(query_norm, grad_scores, 1, 1, highest) * scaling
        grad_query = (
            grad_qnorm
            - jnp.mean(grad_qnorm, 0, keepdims=True)
            - query_norm * jnp.mean(grad_qnorm * query_norm, 0, keepdims=True)
        ) * inverses[slot, 0:1, :]
        grad_key = (
            grad_knorm
            - jnp.mean(grad_knorm, 0, keepdims=True)
            - key_norm * jnp.mean(grad_knorm * key_norm, 0, keepdims=True)
        ) * inverses[slot, 1:2, :]
        grad_proj = jnp.concatenate([grad_query, grad_key, grad_values], 0).astype(low)
        tail = jnp.concatenate([grad_proj[256:], jnp.zeros((columns - 3 * head, PATCHES), low)], 0)
        lead = jnp.concatenate([jnp.zeros((3 * head - 256, PATCHES), low), heads[slot]], 0)
        there = place[slot]
        for block in range(cores * chips):
            at = slice(rows * block, rows * (block + 1))
            main = normed[at, :]
            shares[block % cores, there, block // cores, :, :256] = contract(
                main, grad_proj[:256], 1, 1
            ).astype(low)
            shares[block % cores, there, block // cores, :, 256:] = (
                contract(main, tail, 1, 1) + contract(cotangent[at, :], lead, 1, 1)
            ).astype(low)


def on_device(activations, w_qkv, w_out, d_branch):
    part, tokens = activations.shape
    features, head = w_out.shape
    images = tokens // PATCHES
    z, xl, xh, y, core = (lax.axis_size(a) for a in ("z", "xl", "xh", "y", "core"))
    stacked = jnp.stack([activations, d_branch]).reshape(2, part, images, PATCHES)
    mixed = lax.all_to_all(stacked.transpose(2, 0, 1, 3), "xl", 0, 0, tiled=True)
    gathered = lax.all_gather(mixed.reshape(2 * xl * part, PATCHES), "z", axis=0, tiled=True)

    own = jnp.concatenate([w_qkv.T, w_out.T], 0)
    half = own.shape[0] // core
    core_at = lax.axis_index("core")
    swap = [(0, 1), (1, 0)]
    mine = lax.ppermute(lax.dynamic_slice_in_dim(own, core_at * half, half, 0), "xl", swap)
    theirs = lax.ppermute(mine, "core", swap)
    first = core_at == 0
    other = jnp.concatenate([jnp.where(first, mine, theirs), jnp.where(first, theirs, mine)], 0)

    shape = jax.ShapeDtypeStruct
    vmem = pl.BlockSpec(memory_space=pltpu.VMEM)
    kept = (
        shape((features, PATCHES), low),
        shape((2, PATCHES, PATCHES), wide),
        shape((2, head, PATCHES), wide),
        shape((2, head, PATCHES), wide),
        shape((2, 8, PATCHES), wide),
        shape((2, head, PATCHES), low),
        shape((2, head, PATCHES), low),
    )
    *kept, branch = pl.pallas_call(
        functools.partial(forward_kernel, part, head),
        out_shape=kept + (shape((features, PATCHES), low),),
        in_specs=[vmem] * 3,
        out_specs=[vmem] * 8,
        compiler_params=pltpu.CompilerParams(vmem_limit_bytes=40 << 20),
        cost_estimate=pl.CostEstimate(
            flops=2_000_000_000, bytes_accessed=14_000_000, transcendentals=131072
        ),
        name="forward",
    )(gathered, own, other)
    summed = lax.psum_scatter(branch, "z", scatter_dimension=0, tiled=True)

    at = lax.axis_index("xl")
    place = jnp.stack([at, 1 - at]).astype(jnp.int32)
    columns = 4 * head
    rows = features // (core * xh * y)
    shares = pl.pallas_call(
        functools.partial(backward_kernel, part, head),
        out_shape=shape((core, xl, xh * y, rows, columns), low),
        in_specs=[pl.BlockSpec(memory_space=pltpu.SMEM)] + [vmem] * 10,
        out_specs=vmem,
        scratch_shapes=[pltpu.VMEM((features, PATCHES), low)],
        compiler_params=pltpu.CompilerParams(vmem_limit_bytes=40 << 20),
        cost_estimate=pl.CostEstimate(
            flops=2_000_000_000, bytes_accessed=14_000_000, transcendentals=0
        ),
        name="backward",
    )(place, gathered, w_out.T, other[3 * head :], *kept)
    pairs = lax.all_to_all(shares, "core", 0, 0, tiled=True)
    pair_sum = jnp.sum(pairs.astype(wide), 0).astype(low).reshape(xl * xh * y, rows, columns)
    spread = lax.all_to_all(pair_sum, ("xl", "xh", "y"), 0, 0, tiled=True)
    grads = jnp.sum(spread.astype(wide), 0).astype(low)

    swapped = lax.all_to_all(summed.reshape(xl, part, PATCHES), "xl", 0, 0, tiled=True)
    branch_out = swapped.transpose(1, 0, 2).reshape(part, tokens)
    return (branch_out, grads[:, : 3 * head], grads[:, 3 * head :])


def solution(mesh):
    fine = Mesh(mesh.devices.reshape(2, 4, 2, 16, 2), ("xh", "y", "core", "z", "xl"))
    dp, mp = ("xh", "y", "core"), ("z", "xl")
    in_specs = (P(mp, dp), P(None, mp), P(None, mp), P(mp, dp))
    out_specs = (P(mp, dp), P(dp, mp), P(dp, mp))
    return jax.shard_map(
        on_device, mesh=fine, in_specs=in_specs, out_specs=out_specs, check_vma=False
    )
```

time: 696 us -> 199 us (0.29)
  the two profiles are of different devices: /device:TPU:12 before, /device:TPU:16 now
where the time goes in v1:
time: 199 us; the launch traced here: 198 us
  waiting for transfers between devices  78.6 us (39%)
  blocking collectives  53.2 us (27%)
  local copies, waits for them, and re-layouts  20.5 us (10%)
  between operations  14.2 us (7%)
  Pallas kernels  13.1 us (7%)
  other arithmetic  10.8 us (5%)
  starting transfers between devices  7.45 us (4%)
    all_gather x1, waiting for transfers between devices, on_device(): lax.all_gather(mixed.reshape(2 * xl * part, PATCHES), 'z', axis=0, tiled=...  41.8 us
    all_to_all x1, blocking collectives, on_device(): spread = lax.all_to_all(pair_sum, ('xl', 'xh', 'y'), 0, 0, tiled=True)  36.6 us
    ppermute x1, waiting for transfers between devices, on_device(): lax.ppermute(lax.dynamic_slice_in_dim(own, core_at * half, half, 0), 'xl'...  27.4 us
    unnamed x36, local copies, waits for them, and re-layouts  16 us
    all_to_all x1, blocking collectives, on_device(): pairs = lax.all_to_all(shares, 'core', 0, 0, tiled=True)  8.63 us
    all_to_all x1, blocking collectives, on_device(): lax.all_to_all(stacked.transpose(2, 0, 1, 3), 'xl', 0, 0, tiled=True)  8.01 us
    pallas_call x1, Pallas kernels, on_device(): pl.pallas_call(functools.partial(backward_kernel, part, head), out_shape=...  6.9 us
    reduce_scatter x1, waiting for transfers between devices, on_device(): summed = lax.psum_scatter(branch, 'z', scatter_dimension=0, tiled=True)  6.57 us
  transfers between devices with their start and end apart: 5, of which 5 were waited for; matrix products, arithmetic and copies ran while one was open for 6% of the time, Pallas kernels for 3%

profile of v1, /device:TPU:16, one launch (start us, length us, event | category | flops | bytes accessed | tf_op | source)
XLA Modules:
  0.0 197.9 jit_solution(13255329123474650653)
XLA Ops:
  9.3 8.0 %all_to_all.20 = bf16[2,2,96,256]{3,2,1,0:T(8,128)(2,1)} all-to-all(bf16[2,2,96,256]{3,2,1,0:T(8,128)(2,1)S(1)} %maximum_bitcast_fusion), channel_id=1, replica_groups=mesh['xh'=2,'y'=4,'core'=2,'z'=16,'xl'=2] {'xl'}, dimensions={0} | all-to-all | bytes 393216 | tf_op jit(solution)/shard_map/all_to_all | solution.py:151
  17.9 2.1 %collective-permute-start = (bf16[192,3072]{1,0:T(8,128)(2,1)S(1)}, bf16[192,3072]{1,0:T(8,128)(2,1)S(1)}, u32[]{:S(2)}, u32[]{:S(2)}) collective-permute-start(bf16[192,3072]{1,0:T(8,128)(2,1)S(1)} %fusion), channel_id=1, source_target_pairs={{0,1},{1,0},{2,3},{3,2},{4,5},{5,4},{6,7},{7,6},{8,9},{9,8},{10,11... | collective-permute-start | bytes 3538952 | tf_op jit(solution)/shard_map/ppermute | solution.py:158
  20.1 27.4 %collective-permute-done = bf16[192,3072]{1,0:T(8,128)(2,1)S(1)} collective-permute-done((bf16[192,3072]{1,0:T(8,128)(2,1)S(1)}, bf16[192,3072]{1,0:T(8,128)(2,1)S(1)}, u32[]{:S(2)}, u32[]{:S(2)}) %collective-permute-start) | collective-permute-done | bytes 1179680 | tf_op jit(solution)/shard_map/ppermute | solution.py:158
  47.5 1.9 collective-permute-start.1
  49.4 1.6 pad_maximum_fusion.own
  51.0 1.3 collective-permute-done.1
  52.3 1.4 broadcast_select_fusion.1
  54.9 1.6 pad_maximum_fusion.1.other
  56.4 41.8 %all-gather.2.cloned.1.call-done.gathered = bf16[6144,256]{1,0:T(8,128)(2,1)} async-done(((bf16[384,256]{1,0:T(8,128)(2,1)}), bf16[6144,256]{1,0:T(8,128)(2,1)}) %all-gather.2.cloned.1.call-update) | async-done | bytes 3145744 | tf_op jit(solution)/shard_map/all_gather | solution.py:152
  98.2 1.9 copy-done
  100.1 1.7 copy-done.2
  101.7 1.7 copy-done.3
  103.4 6.2 %forward.1 = (bf16[3072,256]{1,0:T(8,128)(2,1)S(1)}, f32[2,256,256]{2,1,0:T(8,128)S(1)}, f32[2,96,256]{2,1,0:T(8,128)S(1)}, f32[2,96,256]{2,1,0:T(8,128)S(1)}, f...) custom-call(bf16[6144,256]{1,0:T(8,128)(2,1)S(1)} %copy-done, ...), custom_call_target="tpu_custom_call" | custom-call | flops 2000000000 | bytes 14000000 | tf_op jit(solution)/shard_map/forward/pallas_call | solution.py:174
  109.7 1.2 copy-done.6
  110.8 1.2 copy-done.7
  116.4 1.4 copy-done.8
  120.6 6.9 %backward.1 = bf16[2,2,8,192,384]{4,3,2,1,0:T(8,128)(2,1)S(1)} custom-call(s32[2]{0:T(128)S(1)} %pad_add_fusion.place, bf16[6144,256]{1,0:T(8,128)(2,1)S(1)} %copy-done.1, bf16[96,3072]{1,0:T(8,128)(2,1)S(1)} %bitcast.15, bf16[96,3072]{1,0:T(8,128)(2,1)S(1)} %slice.12.other, bf16[3072,256]{1,0:T(8,128)(2,1)S(1)} %copy-done.8, f32[2,256,256]{2,1,0:T(8,128)S(1)} %copy-done.10, ...), custom_call_target="tpu_custom_call" | custom-call | flops 2000000000 | bytes 14000000 | tf_op jit(solution)/shard_map/backward/pallas_call | solution.py:191
  127.5 8.6 %all_to_all.21 = bf16[2,2,8,192,384]{4,3,2,1,0:T(8,128)(2,1)} all-to-all(bf16[2,2,8,192,384]{4,3,2,1,0:T(8,128)(2,1)S(1)} %backward.1), channel_id=1, replica_groups=mesh['xh'=2,'y'=4,'core'=2,'z'=16,'xl'=2] {'core'}, dimensions={0} | all-to-all | bytes 9437184 | tf_op jit(solution)/shard_map/all_to_all | solution.py:203
  136.1 3.5 %reduce_sum.24 = bf16[2,8,192,384]{3,2,1,0:T(8,128)(2,1)S(1)} reduce(bf16[2,2,8,192,384]{4,3,2,1,0:T(8,128)(2,1)} %all_to_all.21, bf16[]{:T(256)} %constant.19.clone.1), dimensions={0}, to_apply=%region_1.2 | reduce | flops 1179648 | bytes 7077890 | tf_op jit(solution)/shard_map/reduce_sum | solution.py:204
  139.7 36.6 %all_to_all.22 = bf16[16,192,384]{2,1,0:T(8,128)(2,1)} all-to-all(bf16[16,192,384]{2,1,0:T(8,128)(2,1)S(1)} %bitcast.16), channel_id=1, replica_groups=mesh['xh'=2,'y'=4,'core'=2,'z'=16,'xl'=2] {'xl','xh','y'}, dimensions={0} | all-to-all | bytes 4718592 | tf_op jit(solution)/shard_map/all_to_all | solution.py:205
  176.3 6.6 %reduce-scatter.2.cloned.1.call-done = bf16[192,256]{1,0:T(8,128)(2,1)} async-done(((bf16[3072,256]{1,0:T(8,128)(2,1)}), bf16[192,256]{1,0:T(8,128)(2,1)}) %reduce-scatter.2.cloned.1.call-update) | async-done | bytes 98320 | tf_op jit(solution)/shard_map/reduce_scatter | solution.py:185
  182.8 3.3 %all-to-all-start.1 = ((bf16[2,96,256]{2,1,0:T(8,128)(2,1)}), bf16[2,96,256]{2,1,0:T(8,128)(2,1)S(1)}, u32[]{:S(2)}, u32[]{:S(2)}) async-start(bf16[2,96,256]{2,1,0:T(8,128)(2,1)} %bitcast.22), calls=%async_computation.2 | async-start | bytes 196608 | tf_op jit(solution)/shard_map/all_to_all | solution.py:208
  186.2 2.0 %reduce_sum.25 = bf16[192,384]{1,0:T(8,128)(2,1)S(1)} reduce(bf16[16,192,384]{2,1,0:T(8,128)(2,1)} %all_to_all.22, bf16[]{:T(256)} %constant.19.clone.1), dimensions={0}, to_apply=%region_2.3 | reduce | flops 1105920 | bytes 2506754 | tf_op jit(solution)/shard_map/reduce_sum | solution.py:206
  188.9 1.6 all-to-all-done.1
  (44 shorter events, 12.3 us)
Async XLA Ops:
  7.2 10.2 %copy-start.16 = (bf16[3072,288]{0,1:T(8,128)(2,1)S(1)}, bf16[3072,288]{0,1:T(8,128)(2,1)}, u32[]{:S(2)}) copy-start(bf16[3072,288]{0,1:T(8,128)(2,1)} %param.5) | copy-start | bytes 5308420
  7.2 91.0 %all-gather.2.cloned.1.call-start = ((), (), s32[]{:S(2)}) async-start(), calls=%async_computation.5 | async-start | bytes 3342336 | tf_op jit(solution)/shard_map/all_gather | solution.py:152
  9.2 40.2 %copy-start.4 = (bf16[3072,96]{0,1:T(8,128)(2,1)S(1)}, bf16[3072,96]{0,1:T(8,128)(2,1)}, u32[]{:S(2)}) copy-start(bf16[3072,96]{0,1:T(8,128)(2,1)} %param.6) | copy-start | bytes 1769476
  17.3 165.5 %reduce-scatter.2.cloned.1.call-start = ((), (), s32[]{:S(2)}) async-start(), calls=%async_computation.6 | async-start | bytes 1671168 | tf_op jit(solution)/shard_map/reduce_scatter | solution.py:185
  17.9 29.5 %collective-permute-start = (bf16[192,3072]{1,0:T(8,128)(2,1)S(1)}, bf16[192,3072]{1,0:T(8,128)(2,1)S(1)}, u32[]{:S(2)}, u32[]{:S(2)}) collective-permute-start(bf16[192,3072]{1,0:T(8,128)(2,1)S(1)} %fusion), channel_id=1, source_target_pairs={{0,1},{1,0},{2,3},{3,2},{4,5},{5,4},{6,7},{7,6},{8,9},{9,8},{10,11... | collective-permute-start | bytes 3538952 | tf_op jit(solution)/shard_map/ppermute | solution.py:158
  47.5 4.9 %collective-permute-start.1 = (bf16[192,3072]{1,0:T(8,128)(2,1)S(1)}, bf16[192,3072]{1,0:T(8,128)(2,1)}, u32[]{:S(2)}, u32[]{:S(2)}) collective-permute-start(bf16[192,3072]{1,0:T(8,128)(2,1)S(1)} %collective-permute-done), channel_id=1, source_target_pairs={{0,32},{32,0},{1,33},{33,1},{2,34},{34,2},{3,35},{35,3},{4,36},{36... | collective-permute-start | bytes 3538952 | tf_op jit(solution)/shard_map/ppermute | solution.py:159
  53.8 1.1 copy-start.15
  98.2 1.9 copy-start
  100.1 1.7 copy-start.2
  101.7 1.7 copy-start.3
  103.4 11.9 %copy-start.1 = (bf16[6144,256]{1,0:T(8,128)(2,1)S(1)}, bf16[6144,256]{1,0:T(8,128)(2,1)}, u32[]{:S(2)}) copy-start(bf16[6144,256]{1,0:T(8,128)(2,1)} %all-gather.2.cloned.1.call-done.gathered) | copy-start | bytes 9437188
  109.6 1.2 copy-start.6
  110.8 1.2 copy-start.7
  112.0 0.8 copy-start.9
  112.8 0.6 copy-start.11
  113.4 0.6 copy-start.13
  115.3 1.1 copy-start.5
  116.4 1.4 copy-start.8
  117.8 1.0 copy-start.10
  118.8 0.9 copy-start.12
  119.7 0.9 copy-start.14
  182.8 7.6 %all-to-all-start.1 = ((bf16[2,96,256]{2,1,0:T(8,128)(2,1)}), bf16[2,96,256]{2,1,0:T(8,128)(2,1)S(1)}, u32[]{:S(2)}, u32[]{:S(2)}) async-start(bf16[2,96,256]{2,1,0:T(8,128)(2,1)} %bitcast.22), calls=%async_computation.2 | async-start | bytes 196608 | tf_op jit(solution)/shard_map/all_to_all | solution.py:208
  188.2 2.9 %copy-start.17 = (bf16[192,384]{1,0:T(8,128)(2,1)}, bf16[192,384]{1,0:T(8,128)(2,1)S(1)}, u32[]{:S(2)}) copy-start(bf16[192,384]{1,0:T(8,128)(2,1)S(1)} %reduce_sum.25) | copy-start | bytes 442372
Sparse Core Ops, SparseCore 0:
  17.4 80.7 all-gather.1
  114.2 68.5 reduce-scatter.1

commit v2 on v1

v2 whole, which is shorter than its diff:
```python
import functools

import jax
import jax.numpy as jnp
from jax import lax
from jax.experimental import pallas as pl
from jax.experimental.pallas import tpu as pltpu
from jax.sharding import Mesh
from jax.sharding import PartitionSpec as P

PATCHES = 256
GROUP = 4
epsilon = 1e-06
highest = lax.Precision.HIGHEST
low = jnp.bfloat16
wide = jnp.float32
Z = ("zh", "zl")


def contract(left, right, left_dim, right_dim, precision=None):
    return lax.dot_general(
        left,
        right,
        (((left_dim,), (right_dim,)), ((), ())),
        precision=precision,
        preferred_element_type=wide,
    )


def normalize_first(values):
    centre = values - jnp.mean(values, 0, keepdims=True)
    inverse = lax.rsqrt(jnp.mean(centre * centre, 0, keepdims=True) + epsilon)
    return (centre * inverse, inverse)


def aligned(start, size):
    return pl.ds(pl.multiple_of(start, 16), size)


SETS = ((0, 0, 4), (1, 0, 4), (2, 0, 4), (3, 0, 2), (3, 2, 2))


def forward_kernel(head, place, *refs):
    sets, (qkv_own, out_own, mine, theirs) = refs[:5], refs[5:9]
    normed, attention, query, key, inverses, value, heads = refs[9:16]
    branch_sets = refs[16:21]
    qkv, out, branch, sems = refs[21:]
    features = normed.shape[0]
    block = features // (4 * GROUP)
    core = place[4]
    thirds, quarter = 3 * head // 2, head // 2
    copies = [
        pltpu.make_async_copy(qkv_own, qkv.at[0], sems.at[0]),
        pltpu.make_async_copy(out_own, out.at[0], sems.at[1]),
    ]
    for n, (source, at) in enumerate(((mine, core), (theirs, 1 - core))):
        copies.append(
            pltpu.make_async_copy(
                source.at[pl.ds(0, thirds)], qkv.at[1, aligned(at * thirds, thirds)], sems.at[2 + 2 * n]
            )
        )
        copies.append(
            pltpu.make_async_copy(
                source.at[pl.ds(thirds, quarter)],
                out.at[1, aligned(at * quarter, quarter)],
                sems.at[3 + 2 * n],
            )
        )
    for copy in copies:
        copy.start()

    def over_blocks(body, carried):
        for ref, (which, first, count) in zip(sets, SETS):
            for n in range(count):
                rows = ref[block * n : block * (n + 1), :].astype(wide)
                at = aligned((GROUP * (first + n) + place[which]) * block, block)
                carried = body(rows, at, carried)
        return carried

    def fold(rows):
        return jnp.sum(rows.reshape(block // 8, 8, PATCHES), 0)

    zero = jnp.zeros((8, PATCHES), wide)
    total = over_blocks(lambda rows, at, t: t + fold(rows), zero)
    mean = jnp.sum(total, 0, keepdims=True) / features

    def squares(rows, at, carried):
        centre = rows - mean
        return carried + fold(centre * centre)

    variance = jnp.sum(over_blocks(squares, zero), 0, keepdims=True) / features
    scale = lax.rsqrt(variance + epsilon)

    def write(rows, at, carried):
        normed[at, :] = ((rows - mean) * scale).astype(low)
        return carried

    over_blocks(write, None)
    for copy in copies:
        copy.wait()
    for slot in range(2):
        projected = contract(qkv[slot], normed[...], 1, 0).astype(low)
        query_norm, query_inv = normalize_first(projected[:head].astype(wide))
        key_norm, key_inv = normalize_first(projected[head : 2 * head].astype(wide))
        values = projected[2 * head :]
        scores = contract(key_norm, query_norm, 0, 0, highest) * head ** (-0.5)
        exponent = jnp.exp(scores)
        attend = exponent / jnp.sum(exponent, 0, keepdims=True)
        attention[slot] = attend
        query[slot] = query_norm
        key[slot] = key_norm
        inverses[slot, 0:1, :] = query_inv
        inverses[slot, 1:2, :] = key_inv
        value[slot] = values
        heads[slot] = contract(values, attend.astype(low), 1, 0).astype(low)
    both_heads = heads[...].reshape(2 * head, PATCHES)
    step = 512
    for start in range(0, features, step):
        both = out[:, :, start : start + step].reshape(2 * head, step)
        branch[start : start + step, :] = contract(both, both_heads, 0, 0).astype(low)
    for ref, (which, first, count) in zip(branch_sets, SETS):
        for n in range(count):
            at = aligned((GROUP * (first + n) + place[which]) * block, block)
            ref[block * n : block * (n + 1), :] = branch[at, :]


def backward_kernel(head, place, *refs):
    sets, (out_own, mine, theirs) = refs[:5], refs[5:8]
    normed, attention, query, key, inverses, value, heads = refs[8:15]
    keep, send, cotangent, out, sems = refs[15:]
    core = place[4]
    thirds, quarter = 3 * head // 2, head // 2
    copies = [pltpu.make_async_copy(out_own, out.at[0], sems.at[0])]
    for n, (source, at) in enumerate(((mine, core), (theirs, 1 - core))):
        copies.append(
            pltpu.make_async_copy(
                source.at[pl.ds(thirds, quarter)],
                out.at[1, aligned(at * quarter, quarter)],
                sems.at[1 + n],
            )
        )
    for copy in copies:
        copy.start()
    block = normed.shape[0] // (4 * GROUP)
    for ref, (which, first, count) in zip(sets, SETS):
        for n in range(count):
            at = aligned((GROUP * (first + n) + place[which]) * block, block)
            cotangent[at, :] = ref[block * n : block * (n + 1), :]
    for copy in copies:
        copy.wait()
    scaling = head ** (-0.5)
    _, chips, rows, columns = keep.shape
    for slot in range(2):
        grad = contract(out[slot], cotangent[...], 1, 0).astype(low)
        attend = attention[slot]
        query_norm, key_norm = query[slot], key[slot]
        grad_weights = contract(value[slot], grad, 0, 0)
        grad_values = contract(grad, attend.astype(low), 1, 1)
        grad_scores = attend * (grad_weights - jnp.sum(grad_weights * attend, 0, keepdims=True))
        grad_qnorm = contract(key_norm, grad_scores, 1, 0, highest) * scaling
        grad_knorm = contract(query_norm, grad_scores, 1, 1, highest) * scaling
        grad_query = (
            grad_qnorm
            - jnp.mean(grad_qnorm, 0, keepdims=True)
            - query_norm * jnp.mean(grad_qnorm * query_norm, 0, keepdims=True)
        ) * inverses[slot, 0:1, :]
        grad_key = (
            grad_knorm
            - jnp.mean(grad_knorm, 0, keepdims=True)
            - key_norm * jnp.mean(grad_knorm * key_norm, 0, keepdims=True)
        ) * inverses[slot, 1:2, :]
        grad_proj = jnp.concatenate([grad_query, grad_key, grad_values], 0).astype(low)
        tail = jnp.concatenate([grad_proj[256:], jnp.zeros((columns - 3 * head, PATCHES), low)], 0)
        lead = jnp.concatenate([jnp.zeros((3 * head - 256, PATCHES), low), heads[slot]], 0)
        there = place[5 + slot]
        for ref, owner in ((send, 1 - core), (keep, core)):
            for chip in range(chips):
                at = aligned((2 * chip + owner) * rows, rows)
                main = normed[at, :]
                ref[there, chip, :, :256] = contract(main, grad_proj[:256], 1, 1).astype(low)
                ref[there, chip, :, 256:] = (
                    contract(main, tail, 1, 1) + contract(cotangent[at, :], lead, 1, 1)
                ).astype(low)


def shift(values, by):
    size = lax.axis_size(Z)
    return lax.ppermute(values, Z, [(i, (i + by) % size) for i in range(size)])


def on_device(activations, w_qkv, w_out, d_branch):
    part, tokens = activations.shape
    features, head = w_out.shape
    images = tokens // PATCHES
    zh, xl, xh, y, core = (lax.axis_size(a) for a in ("zh", "xl", "xh", "y", "core"))
    swap = [(0, 1), (1, 0)]
    core_at, xl_at, residue = (lax.axis_index(a) for a in ("core", "xl", "zl"))
    place = jnp.stack(
        [
            residue,
            (residue + 1) % GROUP,
            (residue + 3) % GROUP,
            (residue + 2) % GROUP,
            core_at,
            xl_at,
            1 - xl_at,
        ]
    ).astype(jnp.int32)

    def by_image(values):
        return values.reshape(part, images, PATCHES).transpose(1, 0, 2)

    qkv_own, out_own = w_qkv.T, w_out.T
    thirds, quarter = 3 * head // 2, head // 2
    mine = jnp.concatenate(
        [
            lax.dynamic_slice_in_dim(qkv_own, core_at * thirds, thirds, 0),
            lax.dynamic_slice_in_dim(out_own, core_at * quarter, quarter, 0),
        ],
        0,
    )
    mine = lax.ppermute(mine, "xl", swap)

    def same_residue(values):
        copies = jnp.broadcast_to(by_image(values)[None], (zh, images, part, PATCHES))
        return lax.all_to_all(
            copies.reshape(zh * images, part, PATCHES), ("zh", "xl"), 0, 0, tiled=True
        ).reshape(zh * xl * part, PATCHES)

    def other_residues(same):
        middle = same.shape[0] // 2
        return (
            same,
            shift(same, -1),
            shift(same, 1),
            shift(same[:middle], 2),
            shift(same[middle:], -2),
        )

    same = same_residue(activations)
    mine, d_branch, same = lax.optimization_barrier((mine, d_branch, same))
    sets = other_residues(same)
    theirs = lax.ppermute(mine, "core", swap)
    cotangent_sets = other_residues(same_residue(d_branch))

    shape = jax.ShapeDtypeStruct
    vmem = pl.BlockSpec(memory_space=pltpu.VMEM)
    smem = pl.BlockSpec(memory_space=pltpu.SMEM)
    anywhere = pl.BlockSpec(memory_space=pl.ANY)
    kept = (
        shape((features, PATCHES), low),
        shape((2, PATCHES, PATCHES), wide),
        shape((2, head, PATCHES), wide),
        shape((2, head, PATCHES), wide),
        shape((2, 8, PATCHES), wide),
        shape((2, head, PATCHES), low),
        shape((2, head, PATCHES), low),
    )
    outputs = pl.pallas_call(
        functools.partial(forward_kernel, head),
        out_shape=kept + tuple(shape(s.shape, low) for s in sets),
        in_specs=[smem] + [vmem] * 5 + [anywhere] * 4,
        out_specs=[vmem] * 12,
        scratch_shapes=[
            pltpu.VMEM((2, 3 * head, features), low),
            pltpu.VMEM((2, head, features), low),
            pltpu.VMEM((features, PATCHES), low),
            pltpu.SemaphoreType.DMA((6,)),
        ],
        compiler_params=pltpu.CompilerParams(vmem_limit_bytes=40 << 20),
        cost_estimate=pl.CostEstimate(
            flops=2_000_000_000, bytes_accessed=14_000_000, transcendentals=131072
        ),
        name="forward",
    )(place, *sets, qkv_own, out_own, mine, theirs)
    kept, (b_own, b_plus, b_minus, b_lead, b_tail) = outputs[:7], outputs[7:]
    halves = jnp.concatenate([shift(b_lead, 2), shift(b_tail, -2)], 0)
    terms = (b_own, shift(b_plus, 1), shift(b_minus, -1), halves)
    summed = sum(t.astype(wide) for t in terms).astype(low)
    spread = lax.all_to_all(
        summed.reshape(zh * xl, part, PATCHES), ("zh", "xl"), 0, 0, tiled=True
    ).reshape(zh, xl, part, PATCHES)
    branch_out = jnp.sum(spread.astype(wide), 0).astype(low).transpose(1, 0, 2).reshape(part, tokens)

    columns = 4 * head
    rows = features // (core * xh * y)
    share = shape((xl, xh * y, rows, columns), low)
    keep, send = pl.pallas_call(
        functools.partial(backward_kernel, head),
        out_shape=(share, share),
        in_specs=[smem] + [vmem] * 5 + [anywhere] * 3 + [vmem] * 7,
        out_specs=(vmem, vmem),
        scratch_shapes=[
            pltpu.VMEM((features, PATCHES), low),
            pltpu.VMEM((2, head, features), low),
            pltpu.SemaphoreType.DMA((3,)),
        ],
        compiler_params=pltpu.CompilerParams(vmem_limit_bytes=40 << 20),
        cost_estimate=pl.CostEstimate(
            flops=2_000_000_000, bytes_accessed=14_000_000, transcendentals=0
        ),
        name="backward",
    )(place, *cotangent_sets, out_own, mine, theirs, *kept)
    received = lax.ppermute(send, "core", swap)
    pair_sum = (keep.astype(wide) + received.astype(wide)).astype(low)
    grads = lax.all_to_all(
        pair_sum.reshape(xl * xh * y, rows, columns), ("xl", "xh", "y"), 0, 0, tiled=True
    )
    grads = jnp.sum(grads.astype(wide), 0).astype(low)
    return (branch_out, grads[:, : 3 * head], grads[:, 3 * head :])


def solution(mesh):
    fine = Mesh(mesh.devices.reshape(2, 4, 2, 4, 4, 2), ("xh", "y", "core", "zh", "zl", "xl"))
    dp, mp = ("xh", "y", "core"), ("zh", "zl", "xl")
    in_specs = (P(mp, dp), P(None, mp), P(None, mp), P(mp, dp))
    out_specs = (P(mp, dp), P(dp, mp), P(dp, mp))
    return jax.shard_map(
        on_device, mesh=fine, in_specs=in_specs, out_specs=out_specs, check_vma=False
    )
```

time: 199 us -> 230 us (1.16)
  the two profiles are of different devices: /device:TPU:16 before, /device:TPU:70 now
where the time goes in v2:
time: 230 us; the launch traced here: 229 us
  waiting for transfers between devices  108 us (47%)
  starting transfers between devices  89.9 us (39%)
  Pallas kernels  18.8 us (8%)
  local copies, waits for them, and re-layouts  6.69 us (3%)
  other arithmetic  5.21 us (2%)
    ppermute x12, starting transfers between devices, shift(): return lax.ppermute(values, Z, [(i, (i + by) % size) for i in range(size)])  41.3 us
    ppermute x1, waiting for transfers between devices, on_device(): mine = lax.ppermute(mine, 'xl', swap)  30.4 us
    all_to_all x1, waiting for transfers between devices, on_device(): lax.all_to_all(pair_sum.reshape(xl * xh * y, rows, columns), ('xl', 'xh',...  30 us
    ppermute x12, waiting for transfers between devices, shift(): return lax.ppermute(values, Z, [(i, (i + by) % size) for i in range(size)])  28.2 us
    all_to_all x2, starting transfers between devices, same_residue(): lax.all_to_all(copies.reshape(zh * images, part, PATCHES), ('zh', 'xl'),...  26.6 us
    all_to_all x1, waiting for transfers between devices, on_device(): lax.all_to_all(summed.reshape(zh * xl, part, PATCHES), ('zh', 'xl'), 0, 0...  18.8 us
    pallas_call x1, Pallas kernels, on_device(): pl.pallas_call(functools.partial(backward_kernel, head), out_shape=(share...  10.2 us
    all_to_all x1, starting transfers between devices, on_device(): lax.all_to_all(summed.reshape(zh * xl, part, PATCHES), ('zh', 'xl'), 0, 0...  9.02 us
  transfers between devices with their start and end apart: 19, of which 10 were waited for; matrix products, arithmetic and copies ran while one was open for 4% of the time, Pallas kernels for 4%

profile of v2, /device:TPU:70, one launch (start us, length us, event | category | flops | bytes accessed | tf_op | source)
XLA Modules:
  0.0 229.2 jit_solution(10711801297990473328)
XLA Ops:
  2.5 14.8 %all-to-all-start = ((bf16[8,96,256]{2,1,0:T(8,128)(2,1)}), bf16[8,96,256]{2,1,0:T(8,128)(2,1)S(1)}, u32[]{:S(2)}, u32[]{:S(2)}) async-start(bf16[8,96,256]{2,1,0:T(8,128)(2,1)} %bitcast.10), calls=%async_computation | async-start | bytes 786432 | tf_op jit(solution)/shard_map/all_to_all | solution.py:226
  18.4 2.1 collective-permute-start
  20.5 30.4 %collective-permute-done.refs_7_.refs_6_ = bf16[192,3072]{1,0:T(8,128)(2,1)} collective-permute-done((bf16[192,3072]{1,0:T(8,128)(2,1)S(1)}, bf16[192,3072]{1,0:T(8,128)(2,1)}, u32[]{:S(2)}, u32[]{:S(2)}) %collective-permute-start) | collective-permute-done | bytes 1179680 | tf_op jit(solution)/shard_map/ppermute | solution.py:222
  51.7 11.9 %all-to-all-start.2 = ((bf16[8,96,256]{2,1,0:T(8,128)(2,1)}), bf16[8,96,256]{2,1,0:T(8,128)(2,1)S(1)}, u32[]{:S(2)}, u32[]{:S(2)}) async-start(bf16[8,96,256]{2,1,0:T(8,128)(2,1)} %bitcast.40), calls=%async_computation.2 | async-start | bytes 786432 | tf_op jit(solution)/shard_map/all_to_all | solution.py:226
  66.2 2.4 %collective-permute-start.4 = (bf16[384,256]{1,0:T(8,128)(2,1)S(1)}, bf16[384,256]{1,0:T(8,128)(2,1)S(1)}, u32[]{:S(2)}, u32[]{:S(2)}) collective-permute-start(bf16[384,256]{1,0:T(8,128)(2,1)S(1)} %get-tuple-element.39), channel_id=1, source_target_pairs={{0,28},{2,30},{4,0},{6,2},{8,4},{10,6},{12,8},{14,10},{16,12},{18,... | collective-permute-start | bytes 589832 | tf_op jit(solution)/shard_map/ppermute | solution.py:188
  68.6 5.5 %collective-permute-start.3 = (bf16[384,256]{1,0:T(8,128)(2,1)}, bf16[384,256]{1,0:T(8,128)(2,1)S(1)}, u32[]{:S(2)}, u32[]{:S(2)}) collective-permute-start(bf16[384,256]{1,0:T(8,128)(2,1)} %get-tuple-element.40), channel_id=1, source_target_pairs={{0,4},{2,6},{4,8},{6,10},{8,12},{10,14},{12,16},{14,18},{16,20},{1... | collective-permute-start | bytes 589832 | tf_op jit(solution)/shard_map/ppermute | solution.py:188
  74.2 3.3 %collective-permute-start.2 = (bf16[768,256]{1,0:T(8,128)(2,1)S(1)}, bf16[768,256]{1,0:T(8,128)(2,1)}, u32[]{:S(2)}, u32[]{:S(2)}) collective-permute-start(bf16[768,256]{1,0:T(8,128)(2,1)S(1)} %bitcast.29), channel_id=1, source_target_pairs={{0,2},{2,4},{4,6},{6,8},{8,10},{10,12},{12,14},{14,16},{16,18},{18... | collective-permute-start | bytes 1179656 | tf_op jit(solution)/shard_map/ppermute | solution.py:188
  77.4 2.6 %collective-permute-start.1 = (bf16[768,256]{1,0:T(8,128)(2,1)S(1)}, bf16[768,256]{1,0:T(8,128)(2,1)}, u32[]{:S(2)}, u32[]{:S(2)}) collective-permute-start(bf16[768,256]{1,0:T(8,128)(2,1)S(1)} %bitcast.30), channel_id=1, source_target_pairs={{0,30},{2,0},{4,2},{6,4},{8,6},{10,8},{12,10},{14,12},{16,14},{18,... | collective-permute-start | bytes 1179656 | tf_op jit(solution)/shard_map/ppermute | solution.py:188
  80.0 10.0 %collective-permute-done.4.refs_4_ = bf16[384,256]{1,0:T(8,128)(2,1)S(1)} collective-permute-done((bf16[384,256]{1,0:T(8,128)(2,1)S(1)}, bf16[384,256]{1,0:T(8,128)(2,1)S(1)}, u32[]{:S(2)}, u32[]{:S(2)}) %collective-permute-start.4) | collective-permute-done | bytes 196640 | tf_op jit(solution)/shard_map/ppermute | solution.py:188
  90.4 4.4 %collective-permute-start.11 = (bf16[768,256]{1,0:T(8,128)(2,1)S(1)}, bf16[768,256]{1,0:T(8,128)(2,1)}, u32[]{:S(2)}, u32[]{:S(2)}) collective-permute-start(bf16[768,256]{1,0:T(8,128)(2,1)S(1)} %bitcast.32), channel_id=1, source_target_pairs={{0,2},{2,4},{4,6},{6,8},{8,10},{10,12},{12,14},{14,16},{16,18},{18... | collective-permute-start | bytes 1179656 | tf_op jit(solution)/shard_map/ppermute | solution.py:188
  99.4 4.5 %collective-permute-start.12 = (bf16[384,256]{1,0:T(8,128)(2,1)}, bf16[384,256]{1,0:T(8,128)(2,1)}, u32[]{:S(2)}, u32[]{:S(2)}) collective-permute-start(bf16[384,256]{1,0:T(8,128)(2,1)} %bitcast.20), channel_id=1, source_target_pairs={{0,4},{2,6},{4,8},{6,10},{8,12},{10,14},{12,16},{14,18},{16,20},{1... | collective-permute-start | bytes 589832 | tf_op jit(solution)/shard_map/ppermute | solution.py:188
  103.9 2.4 %collective-permute-start.13 = (bf16[384,256]{1,0:T(8,128)(2,1)}, bf16[384,256]{1,0:T(8,128)(2,1)}, u32[]{:S(2)}, u32[]{:S(2)}) collective-permute-start(bf16[384,256]{1,0:T(8,128)(2,1)} %bitcast.21), channel_id=1, source_target_pairs={{0,28},{2,30},{4,0},{6,2},{8,4},{10,6},{12,8},{14,10},{16,12},{18,... | collective-permute-start | bytes 589832 | tf_op jit(solution)/shard_map/ppermute | solution.py:188
  106.4 8.5 %forward.1 = (bf16[3072,256]{1,0:T(8,128)(2,1)S(1)}, f32[2,256,256]{2,1,0:T(8,128)S(1)}, f32[2,96,256]{2,1,0:T(8,128)S(1)}, f32[2,96,256]{2,1,0:T(8,128)S(1)}, f...) custom-call(s32[7]{0:T(128)S(1)} %stack.31.place, ...), custom_call_target="tpu_custom_call" | custom-call | flops 2000000000 | bytes 14000000 | tf_op jit(solution)/shard_map/forward/pallas_call | solution.py:259
  115.2 2.3 collective-permute-done.13.refs_4_
  117.5 10.2 %backward.1 = (bf16[2,8,192,384]{3,2,1,0:T(8,128)(2,1)S(1)}, bf16[2,8,192,384]{3,2,1,0:T(8,128)(2,1)}) custom-call(s32[7]{0:T(128)S(1)} %stack.31.place, bf16[768,256]{1,0:T(8,128)(2,1)S(1)} %bitcast.34, bf16[768,256]{1,0:T(8,128)(2,1)} %collective-permute-done.10.refs_1_, bf16[768,256]{1,0:T(8,128)(2,1)} %collective-permute-done.11.refs_2_, ...), custom_call_target="tpu_custom_call" | custom-call | flops 2000000000 | bytes 14000000 | tf_op jit(solution)/shard_map/backward/pallas_call | solution.py:288
  131.5 3.9 %collective-permute-start.7 = (bf16[768,256]{1,0:T(8,128)(2,1)S(1)}, bf16[768,256]{1,0:T(8,128)(2,1)S(1)}, u32[]{:S(2)}, u32[]{:S(2)}) collective-permute-start(bf16[768,256]{1,0:T(8,128)(2,1)S(1)} %get-tuple-element.24), channel_id=1, source_target_pairs={{0,30},{2,0},{4,2},{6,4},{8,6},{10,8},{12,10},{14,12},{16,14},{18,... | collective-permute-start | bytes 1179656 | tf_op jit(solution)/shard_map/ppermute | solution.py:188
  135.5 6.6 %collective-permute-start.8 = (bf16[384,256]{1,0:T(8,128)(2,1)S(1)}, bf16[384,256]{1,0:T(8,128)(2,1)S(1)}, u32[]{:S(2)}, u32[]{:S(2)}) collective-permute-start(bf16[384,256]{1,0:T(8,128)(2,1)S(1)} %get-tuple-element.25), channel_id=1, source_target_pairs={{0,4},{2,6},{4,8},{6,10},{8,12},{10,14},{12,16},{14,18},{16,20},{1... | collective-permute-start | bytes 589832 | tf_op jit(solution)/shard_map/ppermute | solution.py:188
  144.0 7.6 %collective-permute-done.8 = bf16[384,256]{1,0:T(8,128)(2,1)S(1)} collective-permute-done((bf16[384,256]{1,0:T(8,128)(2,1)S(1)}, bf16[384,256]{1,0:T(8,128)(2,1)S(1)}, u32[]{:S(2)}, u32[]{:S(2)}) %collective-permute-start.8) | collective-permute-done | bytes 196640 | tf_op jit(solution)/shard_map/ppermute | solution.py:188
  151.6 6.2 %collective-permute-done.9 = bf16[384,256]{1,0:T(8,128)(2,1)S(1)} collective-permute-done((bf16[384,256]{1,0:T(8,128)(2,1)S(1)}, bf16[384,256]{1,0:T(8,128)(2,1)S(1)}, u32[]{:S(2)}, u32[]{:S(2)}) %collective-permute-start.9) | collective-permute-done | bytes 196640 | tf_op jit(solution)/shard_map/ppermute | solution.py:188
  158.7 9.0 %all-to-all-start.1 = ((bf16[8,96,256]{2,1,0:T(8,128)(2,1)}), bf16[8,96,256]{2,1,0:T(8,128)(2,1)S(1)}, u32[]{:S(2)}, u32[]{:S(2)}) async-start(bf16[8,96,256]{2,1,0:T(8,128)(2,1)} %bitcast.14), calls=%async_computation.1 | async-start | bytes 786432 | tf_op jit(solution)/shard_map/all_to_all | solution.py:280
  167.7 3.8 %add_convert_fusion = bf16[2,8,192,384]{3,2,1,0:T(8,128)(2,1)} fusion(bf16[2,8,192,384]{3,2,1,0:T(8,128)(2,1)} %collective-permute-done.14, bf16[2,8,192,384]{3,2,1,0:T(8,128)(2,1)S(1)} %get-tuple-element.35), kind=kLoop, calls=%fused_computation | loop fusion | flops 4718592 | bytes 7077888 | tf_op jit(solution)/shard_map/convert_element_type | solution.py:305
  171.5 18.8 %all-to-all-done.1 = bf16[8,96,256]{2,1,0:T(8,128)(2,1)S(1)} async-done(((bf16[8,96,256]{2,1,0:T(8,128)(2,1)}), bf16[8,96,256]{2,1,0:T(8,128)(2,1)S(1)}, u32[]{:S(2)}, u32[]{:S(2)}) %all-to-all-start.1) | async-done | bytes 393248 | tf_op jit(solution)/shard_map/all_to_all | solution.py:280
  190.3 7.1 %all-to-all-start.3 = ((bf16[16,192,384]{2,1,0:T(8,128)(2,1)}), bf16[16,192,384]{2,1,0:T(8,128)(2,1)S(1)}, u32[]{:S(2)}, u32[]{:S(2)}) async-start(bf16[16,192,384]{2,1,0:T(8,128)(2,1)} %bitcast.38), calls=%async_computation.3 | async-start | bytes 4718592 | tf_op jit(solution)/shard_map/all_to_all | solution.py:306
  198.1 30.0 %all-to-all-done.3 = bf16[16,192,384]{2,1,0:T(8,128)(2,1)S(1)} async-done(((bf16[16,192,384]{2,1,0:T(8,128)(2,1)}), bf16[16,192,384]{2,1,0:T(8,128)(2,1)S(1)}, u32[]{:S(2)}, u32[]{:S(2)}) %all-to-all-start.3) | async-done | bytes 2359328 | tf_op jit(solution)/shard_map/all_to_all | solution.py:306
  (42 shorter events, 20.3 us)
Async XLA Ops:
  0.6 17.6 %copy-start = (bf16[3072,288]{0,1:T(8,128)(2,1)S(1)}, bf16[3072,288]{0,1:T(8,128)(2,1)}, u32[]{:S(2)}) copy-start(bf16[3072,288]{0,1:T(8,128)(2,1)} %param.5) | copy-start | bytes 5308420
  2.5 48.4 %all-to-all-start = ((bf16[8,96,256]{2,1,0:T(8,128)(2,1)}), bf16[8,96,256]{2,1,0:T(8,128)(2,1)S(1)}, u32[]{:S(2)}, u32[]{:S(2)}) async-start(bf16[8,96,256]{2,1,0:T(8,128)(2,1)} %bitcast.10), calls=%async_computation | async-start | bytes 786432 | tf_op jit(solution)/shard_map/all_to_all | solution.py:226
  17.2 33.6 %copy-start.3 = (bf16[96,512]{1,0:T(8,128)(2,1)S(1)}, bf16[96,512]{1,0:T(8,128)(2,1)}, u32[]{:S(2)}) copy-start(bf16[96,512]{1,0:T(8,128)(2,1)} %param.7) | copy-start | bytes 294916
  18.3 88.1 %copy-start.1 = (bf16[3072,96]{0,1:T(8,128)(2,1)S(1)}, bf16[3072,96]{0,1:T(8,128)(2,1)}, u32[]{:S(2)}) copy-start(bf16[3072,96]{0,1:T(8,128)(2,1)} %param.6) | copy-start | bytes 1769476
  18.4 32.4 %collective-permute-start = (bf16[192,3072]{1,0:T(8,128)(2,1)S(1)}, bf16[192,3072]{1,0:T(8,128)(2,1)}, u32[]{:S(2)}, u32[]{:S(2)}) collective-permute-start(bf16[192,3072]{1,0:T(8,128)(2,1)S(1)} %pad_maximum_fusion), channel_id=1, source_target_pairs={{0,1},{1,0},{2,3},{3,2},{4,5},{5,4},{6,7},{7,6},{8,9},{9,8},{10,11... | collective-permute-start | bytes 3538952 | tf_op jit(solution)/shard_map/ppermute | solution.py:222
  51.7 38.7 %all-to-all-start.2 = ((bf16[8,96,256]{2,1,0:T(8,128)(2,1)}), bf16[8,96,256]{2,1,0:T(8,128)(2,1)S(1)}, u32[]{:S(2)}, u32[]{:S(2)}) async-start(bf16[8,96,256]{2,1,0:T(8,128)(2,1)} %bitcast.40), calls=%async_computation.2 | async-start | bytes 786432 | tf_op jit(solution)/shard_map/all_to_all | solution.py:226
  63.6 42.8 %collective-permute-start.5 = (bf16[192,3072]{1,0:T(8,128)(2,1)}, bf16[192,3072]{1,0:T(8,128)(2,1)}, u32[]{:S(2)}, u32[]{:S(2)}) collective-permute-start(bf16[192,3072]{1,0:T(8,128)(2,1)} %collective-permute-done.refs_7_.refs_6_), channel_id=1, source_target_pairs={{0,32},{32,0},{1,33},{33,1},{2,34},{34,2},{3,35},{35,3},{4,36},{36... | collective-permute-start | bytes 3538952 | tf_op jit(solution)/shard_map/ppermute | solution.py:243
  66.2 23.8 %collective-permute-start.4 = (bf16[384,256]{1,0:T(8,128)(2,1)S(1)}, bf16[384,256]{1,0:T(8,128)(2,1)S(1)}, u32[]{:S(2)}, u32[]{:S(2)}) collective-permute-start(bf16[384,256]{1,0:T(8,128)(2,1)S(1)} %get-tuple-element.39), channel_id=1, source_target_pairs={{0,28},{2,30},{4,0},{6,2},{8,4},{10,6},{12,8},{14,10},{16,12},{18,... | collective-permute-start | bytes 589832 | tf_op jit(solution)/shard_map/ppermute | solution.py:188
  68.6 26.1 %collective-permute-start.3 = (bf16[384,256]{1,0:T(8,128)(2,1)}, bf16[384,256]{1,0:T(8,128)(2,1)S(1)}, u32[]{:S(2)}, u32[]{:S(2)}) collective-permute-start(bf16[384,256]{1,0:T(8,128)(2,1)} %get-tuple-element.40), channel_id=1, source_target_pairs={{0,4},{2,6},{4,8},{6,10},{8,12},{10,14},{12,16},{14,18},{16,20},{1... | collective-permute-start | bytes 589832 | tf_op jit(solution)/shard_map/ppermute | solution.py:188
  74.2 25.2 %collective-permute-start.2 = (bf16[768,256]{1,0:T(8,128)(2,1)S(1)}, bf16[768,256]{1,0:T(8,128)(2,1)}, u32[]{:S(2)}, u32[]{:S(2)}) collective-permute-start(bf16[768,256]{1,0:T(8,128)(2,1)S(1)} %bitcast.29), channel_id=1, source_target_pairs={{0,2},{2,4},{4,6},{6,8},{8,10},{10,12},{12,14},{14,16},{16,18},{18... | collective-permute-start | bytes 1179656 | tf_op jit(solution)/shard_map/ppermute | solution.py:188
  77.4 26.4 %collective-permute-start.1 = (bf16[768,256]{1,0:T(8,128)(2,1)S(1)}, bf16[768,256]{1,0:T(8,128)(2,1)}, u32[]{:S(2)}, u32[]{:S(2)}) collective-permute-start(bf16[768,256]{1,0:T(8,128)(2,1)S(1)} %bitcast.30), channel_id=1, source_target_pairs={{0,30},{2,0},{4,2},{6,4},{8,6},{10,8},{12,10},{14,12},{16,14},{18,... | collective-permute-start | bytes 1179656 | tf_op jit(solution)/shard_map/ppermute | solution.py:188
  90.4 27.1 %collective-permute-start.11 = (bf16[768,256]{1,0:T(8,128)(2,1)S(1)}, bf16[768,256]{1,0:T(8,128)(2,1)}, u32[]{:S(2)}, u32[]{:S(2)}) collective-permute-start(bf16[768,256]{1,0:T(8,128)(2,1)S(1)} %bitcast.32), channel_id=1, source_target_pairs={{0,2},{2,4},{4,6},{6,8},{8,10},{10,12},{12,14},{14,16},{16,18},{18... | collective-permute-start | bytes 1179656 | tf_op jit(solution)/shard_map/ppermute | solution.py:188
  94.8 22.7 %collective-permute-start.10 = (bf16[768,256]{1,0:T(8,128)(2,1)S(1)}, bf16[768,256]{1,0:T(8,128)(2,1)}, u32[]{:S(2)}, u32[]{:S(2)}) collective-permute-start(bf16[768,256]{1,0:T(8,128)(2,1)S(1)} %bitcast.33), channel_id=1, source_target_pairs={{0,30},{2,0},{4,2},{6,4},{8,6},{10,8},{12,10},{14,12},{16,14},{18,... | collective-permute-start | bytes 1179656 | tf_op jit(solution)/shard_map/ppermute | solution.py:188
  99.4 15.8 %collective-permute-start.12 = (bf16[384,256]{1,0:T(8,128)(2,1)}, bf16[384,256]{1,0:T(8,128)(2,1)}, u32[]{:S(2)}, u32[]{:S(2)}) collective-permute-start(bf16[384,256]{1,0:T(8,128)(2,1)} %bitcast.20), channel_id=1, source_target_pairs={{0,4},{2,6},{4,8},{6,10},{8,12},{10,14},{12,16},{14,18},{16,20},{1... | collective-permute-start | bytes 589832 | tf_op jit(solution)/shard_map/ppermute | solution.py:188
  103.9 13.6 %collective-permute-start.13 = (bf16[384,256]{1,0:T(8,128)(2,1)}, bf16[384,256]{1,0:T(8,128)(2,1)}, u32[]{:S(2)}, u32[]{:S(2)}) collective-permute-start(bf16[384,256]{1,0:T(8,128)(2,1)} %bitcast.21), channel_id=1, source_target_pairs={{0,28},{2,30},{4,0},{6,2},{8,4},{10,6},{12,8},{14,10},{16,12},{18,... | collective-permute-start | bytes 589832 | tf_op jit(solution)/shard_map/ppermute | solution.py:188
  127.7 40.1 %collective-permute-start.14 = (bf16[2,8,192,384]{3,2,1,0:T(8,128)(2,1)}, bf16[2,8,192,384]{3,2,1,0:T(8,128)(2,1)}, u32[]{:S(2)}, u32[]{:S(2)}) collective-permute-start(bf16[2,8,192,384]{3,2,1,0:T(8,128)(2,1)} %get-tuple-element.36), channel_id=1, source_target_pairs={{0,32},{32,0},{1,33},{33,1},{2,34},{34,2},{3,35},{35,3},{4,36},{36... | collective-permute-start | bytes 7077896 | tf_op jit(solution)/shard_map/ppermute | solution.py:304
  129.6 28.1 %collective-permute-start.6 = (bf16[768,256]{1,0:T(8,128)(2,1)S(1)}, bf16[768,256]{1,0:T(8,128)(2,1)S(1)}, u32[]{:S(2)}, u32[]{:S(2)}) collective-permute-start(bf16[768,256]{1,0:T(8,128)(2,1)S(1)} %get-tuple-element.23), channel_id=1, source_target_pairs={{0,2},{2,4},{4,6},{6,8},{8,10},{10,12},{12,14},{14,16},{16,18},{18... | collective-permute-start | bytes 1179656 | tf_op jit(solution)/shard_map/ppermute | solution.py:188
  131.5 26.2 %collective-permute-start.7 = (bf16[768,256]{1,0:T(8,128)(2,1)S(1)}, bf16[768,256]{1,0:T(8,128)(2,1)S(1)}, u32[]{:S(2)}, u32[]{:S(2)}) collective-permute-start(bf16[768,256]{1,0:T(8,128)(2,1)S(1)} %get-tuple-element.24), channel_id=1, source_target_pairs={{0,30},{2,0},{4,2},{6,4},{8,6},{10,8},{12,10},{14,12},{16,14},{18,... | collective-permute-start | bytes 1179656 | tf_op jit(solution)/shard_map/ppermute | solution.py:188
  135.5 16.1 %collective-permute-start.8 = (bf16[384,256]{1,0:T(8,128)(2,1)S(1)}, bf16[384,256]{1,0:T(8,128)(2,1)S(1)}, u32[]{:S(2)}, u32[]{:S(2)}) collective-permute-start(bf16[384,256]{1,0:T(8,128)(2,1)S(1)} %get-tuple-element.25), channel_id=1, source_target_pairs={{0,4},{2,6},{4,8},{6,10},{8,12},{10,14},{12,16},{14,18},{16,20},{1... | collective-permute-start | bytes 589832 | tf_op jit(solution)/shard_map/ppermute | solution.py:188
  142.1 15.7 %collective-permute-start.9 = (bf16[384,256]{1,0:T(8,128)(2,1)S(1)}, bf16[384,256]{1,0:T(8,128)(2,1)S(1)}, u32[]{:S(2)}, u32[]{:S(2)}) collective-permute-start(bf16[384,256]{1,0:T(8,128)(2,1)S(1)} %get-tuple-element.26), channel_id=1, source_target_pairs={{0,28},{2,30},{4,0},{6,2},{8,4},{10,6},{12,8},{14,10},{16,12},{18,... | collective-permute-start | bytes 589832 | tf_op jit(solution)/shard_map/ppermute | solution.py:188
  158.7 31.6 %all-to-all-start.1 = ((bf16[8,96,256]{2,1,0:T(8,128)(2,1)}), bf16[8,96,256]{2,1,0:T(8,128)(2,1)S(1)}, u32[]{:S(2)}, u32[]{:S(2)}) async-start(bf16[8,96,256]{2,1,0:T(8,128)(2,1)} %bitcast.14), calls=%async_computation.1 | async-start | bytes 786432 | tf_op jit(solution)/shard_map/all_to_all | solution.py:280
  190.3 37.9 %all-to-all-start.3 = ((bf16[16,192,384]{2,1,0:T(8,128)(2,1)}), bf16[16,192,384]{2,1,0:T(8,128)(2,1)S(1)}, u32[]{:S(2)}, u32[]{:S(2)}) async-start(bf16[16,192,384]{2,1,0:T(8,128)(2,1)} %bitcast.38), calls=%async_computation.3 | async-start | bytes 4718592 | tf_op jit(solution)/shard_map/all_to_all | solution.py:306
  228.5 0.7 copy-start.2

commit v3 on v2

--- a/solution.py
+++ b/solution.py
@@ -43,8 +43,7 @@
 def forward_kernel(head, place, *refs):
     sets, (qkv_own, out_own, mine, theirs) = refs[:5], refs[5:9]
     normed, attention, query, key, inverses, value, heads = refs[9:16]
-    branch_sets = refs[16:21]
-    qkv, out, branch, sems = refs[21:]
+    branch, qkv, out, sems = refs[16:]
     features = normed.shape[0]
     block = features // (4 * GROUP)
     core = place[4]
@@ -118,16 +117,11 @@
     for start in range(0, features, step):
         both = out[:, :, start : start + step].reshape(2 * head, step)
         branch[start : start + step, :] = contract(both, both_heads, 0, 0).astype(low)
-    for ref, (which, first, count) in zip(branch_sets, SETS):
-        for n in range(count):
-            at = aligned((GROUP * (first + n) + place[which]) * block, block)
-            ref[block * n : block * (n + 1), :] = branch[at, :]
-
-
-def backward_kernel(head, place, *refs):
-    sets, (out_own, mine, theirs) = refs[:5], refs[5:8]
-    normed, attention, query, key, inverses, value, heads = refs[8:15]
-    keep, send, cotangent, out, sems = refs[15:]
+
+
+def backward_kernel(head, place, cotangent, out_own, mine, theirs, *refs):
+    normed, attention, query, key, inverses, value, heads = refs[:7]
+    shares, out, sems = refs[7:]
     core = place[4]
     thirds, quarter = 3 * head // 2, head // 2
     copies = [pltpu.make_async_copy(out_own, out.at[0], sems.at[0])]
@@ -141,15 +135,10 @@
         )
     for copy in copies:
         copy.start()
-    block = normed.shape[0] // (4 * GROUP)
-    for ref, (which, first, count) in zip(sets, SETS):
-        for n in range(count):
-            at = aligned((GROUP * (first + n) + place[which]) * block, block)
-            cotangent[at, :] = ref[block * n : block * (n + 1), :]
     for copy in copies:
         copy.wait()
     scaling = head ** (-0.5)
-    _, chips, rows, columns = keep.shape
+    cores, _, chips, rows, columns = shares.shape
     for slot in range(2):
         grad = contract(out[slot], cotangent[...], 1, 0).astype(low)
         attend = attention[slot]
@@ -173,12 +162,12 @@
         tail = jnp.concatenate([grad_proj[256:], jnp.zeros((columns - 3 * head, PATCHES), low)], 0)
         lead = jnp.concatenate([jnp.zeros((3 * head - 256, PATCHES), low), heads[slot]], 0)
         there = place[5 + slot]
-        for ref, owner in ((send, 1 - core), (keep, core)):
+        for owner in range(cores):
             for chip in range(chips):
-                at = aligned((2 * chip + owner) * rows, rows)
+                at = slice((2 * chip + owner) * rows, (2 * chip + owner + 1) * rows)
                 main = normed[at, :]
-                ref[there, chip, :, :256] = contract(main, grad_proj[:256], 1, 1).astype(low)
-                ref[there, chip, :, 256:] = (
+                shares[owner, there, chip, :, :256] = contract(main, grad_proj[:256], 1, 1).astype(low)
+                shares[owner, there, chip, :, 256:] = (
                     contract(main, tail, 1, 1) + contract(cotangent[at, :], lead, 1, 1)
                 ).astype(low)
 
@@ -210,6 +199,8 @@
     def by_image(values):
         return values.reshape(part, images, PATCHES).transpose(1, 0, 2)
 
+    mixed = lax.all_to_all(by_image(d_branch), "xl", 0, 0, tiled=True)
+
     qkv_own, out_own = w_qkv.T, w_out.T
     thirds, quarter = 3 * head // 2, head // 2
     mine = jnp.concatenate(
@@ -219,29 +210,23 @@
         ],
         0,
     )
+    mine, activations, mixed = lax.optimization_barrier((mine, activations, mixed))
+    cotangent = lax.all_gather(mixed.reshape(xl * part, PATCHES), Z, axis=0, tiled=True)
     mine = lax.ppermute(mine, "xl", swap)
-
-    def same_residue(values):
-        copies = jnp.broadcast_to(by_image(values)[None], (zh, images, part, PATCHES))
-        return lax.all_to_all(
-            copies.reshape(zh * images, part, PATCHES), ("zh", "xl"), 0, 0, tiled=True
-        ).reshape(zh * xl * part, PATCHES)
-
-    def other_residues(same):
-        middle = same.shape[0] // 2
-        return (
-            same,
-            shift(same, -1),
-            shift(same, 1),
-            shift(same[:middle], 2),
-            shift(same[middle:], -2),
-        )
-
-    same = same_residue(activations)
-    mine, d_branch, same = lax.optimization_barrier((mine, d_branch, same))
-    sets = other_residues(same)
+    copies = jnp.broadcast_to(by_image(activations)[None], (zh, images, part, PATCHES))
+    same = lax.all_to_all(
+        copies.reshape(zh * images, part, PATCHES), ("zh", "xl"), 0, 0, tiled=True
+    ).reshape(zh * xl * part, PATCHES)
+    mine, same = lax.optimization_barrier((mine, same))
     theirs = lax.ppermute(mine, "core", swap)
-    cotangent_sets = other_residues(same_residue(d_branch))
+    middle = zh * xl * part // 2
+    sets = (
+        same,
+        shift(same, -1),
+        shift(same, 1),
+        shift(same[:middle], 2),
+        shift(same[middle:], -2),
+    )
 
     shape = jax.ShapeDtypeStruct
     vmem = pl.BlockSpec(memory_space=pltpu.VMEM)
@@ -258,13 +243,12 @@
     )
     outputs = pl.pallas_call(
         functools.partial(forward_kernel, head),
-        out_shape=kept + tuple(shape(s.shape, low) for s in sets),
+        out_shape=kept + (shape((features, PATCHES), low),),
         in_specs=[smem] + [vmem] * 5 + [anywhere] * 4,
-        out_specs=[vmem] * 12,
+        out_specs=[vmem] * 8,
         scratch_shapes=[
             pltpu.VMEM((2, 3 * head, features), low),
             pltpu.VMEM((2, head, features), low),
-            pltpu.VMEM((features, PATCHES), low),
             pltpu.SemaphoreType.DMA((6,)),
         ],
         compiler_params=pltpu.CompilerParams(vmem_limit_bytes=40 << 20),
@@ -273,40 +257,31 @@
         ),
         name="forward",
     )(place, *sets, qkv_own, out_own, mine, theirs)
-    kept, (b_own, b_plus, b_minus, b_lead, b_tail) = outputs[:7], outputs[7:]
-    halves = jnp.concatenate([shift(b_lead, 2), shift(b_tail, -2)], 0)
-    terms = (b_own, shift(b_plus, 1), shift(b_minus, -1), halves)
-    summed = sum(t.astype(wide) for t in terms).astype(low)
-    spread = lax.all_to_all(
-        summed.reshape(zh * xl, part, PATCHES), ("zh", "xl"), 0, 0, tiled=True
-    ).reshape(zh, xl, part, PATCHES)
-    branch_out = jnp.sum(spread.astype(wide), 0).astype(low).transpose(1, 0, 2).reshape(part, tokens)
-
+    kept, branch = outputs[:7], outputs[7]
+    summed = lax.psum_scatter(branch, Z, scatter_dimension=0, tiled=True)
     columns = 4 * head
     rows = features // (core * xh * y)
-    share = shape((xl, xh * y, rows, columns), low)
-    keep, send = pl.pallas_call(
+    shares = pl.pallas_call(
         functools.partial(backward_kernel, head),
-        out_shape=(share, share),
-        in_specs=[smem] + [vmem] * 5 + [anywhere] * 3 + [vmem] * 7,
-        out_specs=(vmem, vmem),
-        scratch_shapes=[
-            pltpu.VMEM((features, PATCHES), low),
-            pltpu.VMEM((2, head, features), low),
-            pltpu.SemaphoreType.DMA((3,)),
-        ],
+        out_shape=shape((core, xl, xh * y, rows, columns), low),
+        in_specs=[smem, vmem] + [anywhere] * 3 + [vmem] * 7,
+        out_specs=vmem,
+        scratch_shapes=[pltpu.VMEM((2, head, features), low), pltpu.SemaphoreType.DMA((3,))],
         compiler_params=pltpu.CompilerParams(vmem_limit_bytes=40 << 20),
         cost_estimate=pl.CostEstimate(
-            flops=2_000_000_000, bytes_accessed=14_000_000, transcendentals=0
+            flops=1_000_000, bytes_accessed=100_000, transcendentals=0
         ),
         name="backward",
-    )(place, *cotangent_sets, out_own, mine, theirs, *kept)
-    received = lax.ppermute(send, "core", swap)
-    pair_sum = (keep.astype(wide) + received.astype(wide)).astype(low)
+    )(place, cotangent, out_own, mine, theirs, *kept)
+    pairs = lax.all_to_all(shares, "core", 0, 0, tiled=True)
+    pair_sum = jnp.sum(pairs.astype(wide), 0).astype(low)
     grads = lax.all_to_all(
         pair_sum.reshape(xl * xh * y, rows, columns), ("xl", "xh", "y"), 0, 0, tiled=True
     )
+    summed, grads = lax.optimization_barrier((summed, grads))
     grads = jnp.sum(grads.astype(wide), 0).astype(low)
+    swapped = lax.all_to_all(summed.reshape(xl, part, PATCHES), "xl", 0, 0, tiled=True)
+    branch_out = swapped.transpose(1, 0, 2).reshape(part, tokens)
     return (branch_out, grads[:, : 3 * head], grads[:, 3 * head :])
 
 

time: 230 us -> 207 us (0.900)
  the two profiles are of different devices: /device:TPU:70 before, /device:TPU:12 now
where the time goes in v3:
time: 207 us; the launch traced here: 205 us
  waiting for transfers between devices  58.6 us (28%)
  blocking collectives  44.1 us (21%)
  starting transfers between devices  42 us (20%)
  local copies, waits for them, and re-layouts  23.7 us (11%)
  Pallas kernels  17 us (8%)
  between operations  14.3 us (7%)
  other arithmetic  5.61 us (3%)
    all_to_all x1, blocking collectives, on_device(): lax.all_to_all(pair_sum.reshape(xl * xh * y, rows, columns), ('xl', 'xh',...  35.4 us
    ppermute x1, waiting for transfers between devices, on_device(): mine = lax.ppermute(mine, 'xl', swap)  28.4 us
    unnamed x42, local copies, waits for them, and re-layouts  16.9 us
    ppermute x4, waiting for transfers between devices, shift(): return lax.ppermute(values, Z, [(i, (i + by) % size) for i in range(size)])  15.7 us
    all_to_all x1, starting transfers between devices, on_device(): lax.all_to_all(copies.reshape(zh * images, part, PATCHES), ('zh', 'xl'),...  15.1 us
    ppermute x4, starting transfers between devices, shift(): return lax.ppermute(values, Z, [(i, (i + by) % size) for i in range(size)])  14.3 us
    reduce_scatter x1, waiting for transfers between devices, on_device(): summed = lax.psum_scatter(branch, Z, scatter_dimension=0, tiled=True)  11.1 us
    pallas_call x1, Pallas kernels, on_device(): pl.pallas_call(functools.partial(forward_kernel, head), out_shape=kept +...  8.95 us
  transfers between devices with their start and end apart: 11, of which 5 were waited for; matrix products, arithmetic and copies ran while one was open for 5% of the time, Pallas kernels for 8%

profile of v3, /device:TPU:12, one launch (start us, length us, event | category | flops | bytes accessed | tf_op | source)
XLA Modules:
  0.0 205.2 jit_solution(537364453973376060)
XLA Ops:
  7.2 1.5 copy.13
  8.7 3.3 %all-to-all-start = ((bf16[2,96,256]{2,1,0:T(8,128)(2,1)}), bf16[2,96,256]{2,1,0:T(8,128)(2,1)S(1)}, u32[]{:S(2)}, u32[]{:S(2)}) async-start(bf16[2,96,256]{2,1,0:T(8,128)(2,1)} %bitcast.28), calls=%async_computation | async-start | bytes 196608 | tf_op jit(solution)/shard_map/all_to_all | solution.py:202
  14.5 1.9 all-to-all-done
  17.8 15.1 %all-to-all-start.1 = ((bf16[8,96,256]{2,1,0:T(8,128)(2,1)}), bf16[8,96,256]{2,1,0:T(8,128)(2,1)S(1)}, u32[]{:S(2)}, u32[]{:S(2)}) async-start(bf16[8,96,256]{2,1,0:T(8,128)(2,1)} %bitcast.11), calls=%async_computation.1 | async-start | bytes 786432 | tf_op jit(solution)/shard_map/all_to_all | solution.py:217
  33.0 3.9 %collective-permute-start = (bf16[192,3072]{1,0:T(8,128)(2,1)S(1)}, bf16[192,3072]{1,0:T(8,128)(2,1)S(1)}, u32[]{:S(2)}, u32[]{:S(2)}) collective-permute-start(bf16[192,3072]{1,0:T(8,128)(2,1)S(1)} %pad_maximum_fusion), channel_id=1, source_target_pairs={{0,1},{1,0},{2,3},{3,2},{4,5},{5,4},{6,7},{7,6},{8,9},{9,8},{10,11... | collective-permute-start | bytes 3538952 | tf_op jit(solution)/shard_map/ppermute | solution.py:215
  36.9 28.4 %collective-permute-done.refs_7_.mine = bf16[192,3072]{1,0:T(8,128)(2,1)S(1)} collective-permute-done((bf16[192,3072]{1,0:T(8,128)(2,1)S(1)}, bf16[192,3072]{1,0:T(8,128)(2,1)S(1)}, u32[]{:S(2)}, u32[]{:S(2)}) %collective-permute-start) | collective-permute-done | bytes 1179680 | tf_op jit(solution)/shard_map/ppermute | solution.py:215
  65.3 1.9 collective-permute-start.5
  68.2 2.9 %collective-permute-start.2 = (bf16[768,256]{1,0:T(8,128)(2,1)S(1)}, bf16[768,256]{1,0:T(8,128)(2,1)S(1)}, u32[]{:S(2)}, u32[]{:S(2)}) collective-permute-start(bf16[768,256]{1,0:T(8,128)(2,1)S(1)} %bitcast.30), channel_id=1, source_target_pairs={{0,2},{2,4},{4,6},{6,8},{8,10},{10,12},{12,14},{14,16},{16,18},{18... | collective-permute-start | bytes 1179656 | tf_op jit(solution)/shard_map/ppermute | solution.py:177
  71.1 4.6 %collective-permute-start.1 = (bf16[768,256]{1,0:T(8,128)(2,1)S(1)}, bf16[768,256]{1,0:T(8,128)(2,1)S(1)}, u32[]{:S(2)}, u32[]{:S(2)}) collective-permute-start(bf16[768,256]{1,0:T(8,128)(2,1)S(1)} %bitcast.31), channel_id=1, source_target_pairs={{0,30},{2,0},{4,2},{6,4},{8,6},{10,8},{12,10},{14,12},{16,14},{18,... | collective-permute-start | bytes 1179656 | tf_op jit(solution)/shard_map/ppermute | solution.py:177
  76.5 4.9 %collective-permute-start.4 = (bf16[384,256]{1,0:T(8,128)(2,1)}, bf16[384,256]{1,0:T(8,128)(2,1)S(1)}, u32[]{:S(2)}, u32[]{:S(2)}) collective-permute-start(bf16[384,256]{1,0:T(8,128)(2,1)} %get-tuple-element.33), channel_id=1, source_target_pairs={{0,28},{2,30},{4,0},{6,2},{8,4},{10,6},{12,8},{14,10},{16,12},{18,... | collective-permute-start | bytes 589832 | tf_op jit(solution)/shard_map/ppermute | solution.py:177
  81.4 1.9 collective-permute-start.3
  83.4 15.7 %collective-permute-done.4.refs_4_ = bf16[384,256]{1,0:T(8,128)(2,1)S(1)} collective-permute-done((bf16[384,256]{1,0:T(8,128)(2,1)}, bf16[384,256]{1,0:T(8,128)(2,1)S(1)}, u32[]{:S(2)}, u32[]{:S(2)}) %collective-permute-start.4) | collective-permute-done | bytes 196640 | tf_op jit(solution)/shard_map/ppermute | solution.py:177
  102.0 1.3 copy-done.3
  103.3 1.5 copy-done.5
  108.6 9.0 %forward.1 = (bf16[3072,256]{1,0:T(8,128)(2,1)S(1)}, f32[2,256,256]{2,1,0:T(8,128)S(1)}, f32[2,96,256]{2,1,0:T(8,128)S(1)}, f32[2,96,256]{2,1,0:T(8,128)S(1)}, f...) custom-call(s32[7]{0:T(128)S(1)} %stack.31.place, ...), custom_call_target="tpu_custom_call" | custom-call | flops 2000000000 | bytes 14000000 | tf_op jit(solution)/shard_map/forward/pallas_call | solution.py:244
  118.9 1.4 copy-done
  123.4 8.1 %backward.1 = bf16[2,2,8,192,384]{4,3,2,1,0:T(8,128)(2,1)S(1)} custom-call(s32[7]{0:T(128)S(1)} %stack.31.place, bf16[3072,256]{1,0:T(8,128)(2,1)S(1)} %copy-done, bf16[96,3072]{1,0:T(8,128)(2,1)S(1)} %bitcast.35, bf16[192,3072]{1,0:T(8,128)(2,1)S(1)} %copy-done.4, bf16[192,3072]{1,0:T(8,128)(2,1)} %collective-permute-done.5.refs_8_.theirs, ...), custom_call_target="tpu_custom_call" | custom-call | flops 1000000 | bytes 100000 | tf_op jit(solution)/shard_map/backward/pallas_call | solution.py:264
  131.4 8.6 %all_to_all.25 = bf16[2,2,8,192,384]{4,3,2,1,0:T(8,128)(2,1)} all-to-all(bf16[2,2,8,192,384]{4,3,2,1,0:T(8,128)(2,1)S(1)} %backward.1), channel_id=1, replica_groups=mesh['xh'=2,'y'=4,'core'=2,'zh'=4,'zl'=4,'xl'=2] {'core'}, dimensions={0} | all-to-all | bytes 9437184 | tf_op jit(solution)/shard_map/all_to_all | solution.py:276
  140.1 3.5 %reduce_sum.24 = bf16[2,8,192,384]{3,2,1,0:T(8,128)(2,1)S(1)} reduce(bf16[2,2,8,192,384]{4,3,2,1,0:T(8,128)(2,1)} %all_to_all.25, bf16[]{:T(256)} %constant.50.clone.1), dimensions={0}, to_apply=%region_1.2 | reduce | flops 1179648 | bytes 7077890 | tf_op jit(solution)/shard_map/reduce_sum | solution.py:277
  143.6 35.4 %all_to_all.26 = bf16[16,192,384]{2,1,0:T(8,128)(2,1)} all-to-all(bf16[16,192,384]{2,1,0:T(8,128)(2,1)S(1)} %bitcast.37), channel_id=1, replica_groups=mesh['xh'=2,'y'=4,'core'=2,'zh'=4,'zl'=4,'xl'=2] {'xl','xh','y'}, dimensions={0} | all-to-all | bytes 4718592 | tf_op jit(solution)/shard_map/all_to_all | solution.py:278
  179.0 11.1 %reduce-scatter.2.cloned.1.call-done = bf16[192,256]{1,0:T(8,128)(2,1)} async-done(((bf16[3072,256]{1,0:T(8,128)(2,1)}), bf16[192,256]{1,0:T(8,128)(2,1)}) %reduce-scatter.2.cloned.1.call-update) | async-done | bytes 98320 | tf_op jit(solution)/shard_map/reduce_scatter | solution.py:261
  190.1 3.3 %all-to-all-start.4 = ((bf16[2,96,256]{2,1,0:T(8,128)(2,1)}), bf16[2,96,256]{2,1,0:T(8,128)(2,1)S(1)}, u32[]{:S(2)}, u32[]{:S(2)}) async-start(bf16[2,96,256]{2,1,0:T(8,128)(2,1)} %bitcast.43), calls=%async_computation.5 | async-start | bytes 196608 | tf_op jit(solution)/shard_map/all_to_all | solution.py:283
  193.5 2.0 reduce_sum.25
  196.2 1.6 all-to-all-done.4
  (59 shorter events, 18.2 us)
Async XLA Ops:
  8.7 7.6 %all-to-all-start = ((bf16[2,96,256]{2,1,0:T(8,128)(2,1)}), bf16[2,96,256]{2,1,0:T(8,128)(2,1)S(1)}, u32[]{:S(2)}, u32[]{:S(2)}) async-start(bf16[2,96,256]{2,1,0:T(8,128)(2,1)} %bitcast.28), calls=%async_computation | async-start | bytes 196608 | tf_op jit(solution)/shard_map/all_to_all | solution.py:202
  12.1 106.8 %all-gather.2.cloned.1.call-start = ((), (), s32[]{:S(2)}) async-start(), calls=%async_computation.7 | async-start | bytes 1671168 | tf_op jit(solution)/shard_map/all_gather | solution.py:214
  13.1 3.9 %copy-start.20 = (bf16[96,512]{1,0:T(8,128)(2,1)S(1)}, bf16[96,512]{1,0:T(8,128)(2,1)}, u32[]{:S(2)}) copy-start(bf16[96,512]{1,0:T(8,128)(2,1)} %param.4) | copy-start | bytes 294916
  14.5 87.5 %copy-start.1 = (bf16[3072,96]{0,1:T(8,128)(2,1)S(1)}, bf16[3072,96]{0,1:T(8,128)(2,1)}, u32[]{:S(2)}) copy-start(bf16[3072,96]{0,1:T(8,128)(2,1)} %param.6) | copy-start | bytes 1769476
  17.8 47.4 %all-to-all-start.1 = ((bf16[8,96,256]{2,1,0:T(8,128)(2,1)}), bf16[8,96,256]{2,1,0:T(8,128)(2,1)S(1)}, u32[]{:S(2)}, u32[]{:S(2)}) async-start(bf16[8,96,256]{2,1,0:T(8,128)(2,1)} %bitcast.11), calls=%async_computation.1 | async-start | bytes 786432 | tf_op jit(solution)/shard_map/all_to_all | solution.py:217
  32.9 157.2 %reduce-scatter.2.cloned.1.call-start = ((), (), s32[]{:S(2)}) async-start(), calls=%async_computation.6 | async-start | bytes 1671168 | tf_op jit(solution)/shard_map/reduce_scatter | solution.py:261
  33.0 32.3 %collective-permute-start = (bf16[192,3072]{1,0:T(8,128)(2,1)S(1)}, bf16[192,3072]{1,0:T(8,128)(2,1)S(1)}, u32[]{:S(2)}, u32[]{:S(2)}) collective-permute-start(bf16[192,3072]{1,0:T(8,128)(2,1)S(1)} %pad_maximum_fusion), channel_id=1, source_target_pairs={{0,1},{1,0},{2,3},{3,2},{4,5},{5,4},{6,7},{7,6},{8,9},{9,8},{10,11... | collective-permute-start | bytes 3538952 | tf_op jit(solution)/shard_map/ppermute | solution.py:215
  65.3 36.7 %collective-permute-start.5 = (bf16[192,3072]{1,0:T(8,128)(2,1)S(1)}, bf16[192,3072]{1,0:T(8,128)(2,1)}, u32[]{:S(2)}, u32[]{:S(2)}) collective-permute-start(bf16[192,3072]{1,0:T(8,128)(2,1)S(1)} %collective-permute-done.refs_7_.mine), channel_id=1, source_target_pairs={{0,32},{32,0},{1,33},{33,1},{2,34},{34,2},{3,35},{35,3},{4,36},{36... | collective-permute-start | bytes 3538952 | tf_op jit(solution)/shard_map/ppermute | solution.py:221
  67.2 1.1 copy-start.2
  68.2 32.2 %collective-permute-start.2 = (bf16[768,256]{1,0:T(8,128)(2,1)S(1)}, bf16[768,256]{1,0:T(8,128)(2,1)S(1)}, u32[]{:S(2)}, u32[]{:S(2)}) collective-permute-start(bf16[768,256]{1,0:T(8,128)(2,1)S(1)} %bitcast.30), channel_id=1, source_target_pairs={{0,2},{2,4},{4,6},{6,8},{8,10},{10,12},{12,14},{14,16},{16,18},{18... | collective-permute-start | bytes 1179656 | tf_op jit(solution)/shard_map/ppermute | solution.py:177
  71.1 30.1 %collective-permute-start.1 = (bf16[768,256]{1,0:T(8,128)(2,1)S(1)}, bf16[768,256]{1,0:T(8,128)(2,1)S(1)}, u32[]{:S(2)}, u32[]{:S(2)}) collective-permute-start(bf16[768,256]{1,0:T(8,128)(2,1)S(1)} %bitcast.31), channel_id=1, source_target_pairs={{0,30},{2,0},{4,2},{6,4},{8,6},{10,8},{12,10},{14,12},{16,14},{18,... | collective-permute-start | bytes 1179656 | tf_op jit(solution)/shard_map/ppermute | solution.py:177
  76.5 22.6 %collective-permute-start.4 = (bf16[384,256]{1,0:T(8,128)(2,1)}, bf16[384,256]{1,0:T(8,128)(2,1)S(1)}, u32[]{:S(2)}, u32[]{:S(2)}) collective-permute-start(bf16[384,256]{1,0:T(8,128)(2,1)} %get-tuple-element.33), channel_id=1, source_target_pairs={{0,28},{2,30},{4,0},{6,2},{8,4},{10,6},{12,8},{14,10},{16,12},{18,... | collective-permute-start | bytes 589832 | tf_op jit(solution)/shard_map/ppermute | solution.py:177
  81.4 18.4 %collective-permute-start.3 = (bf16[384,256]{1,0:T(8,128)(2,1)S(1)}, bf16[384,256]{1,0:T(8,128)(2,1)S(1)}, u32[]{:S(2)}, u32[]{:S(2)}) collective-permute-start(bf16[384,256]{1,0:T(8,128)(2,1)S(1)} %get-tuple-element.34), channel_id=1, source_target_pairs={{0,4},{2,6},{4,8},{6,10},{8,12},{10,14},{12,16},{14,18},{16,20},{1... | collective-permute-start | bytes 589832 | tf_op jit(solution)/shard_map/ppermute | solution.py:177
  102.0 1.3 copy-start.3
  103.3 1.5 copy-start.5
  104.7 1.0 copy-start.11
  105.7 1.0 copy-start.13
  106.7 0.9 copy-start.15
  107.7 0.9 copy-start.17
  118.9 1.4 copy-start
  120.3 1.3 copy-start.4
  121.6 0.9 copy-start.7
  190.1 7.6 %all-to-all-start.4 = ((bf16[2,96,256]{2,1,0:T(8,128)(2,1)}), bf16[2,96,256]{2,1,0:T(8,128)(2,1)S(1)}, u32[]{:S(2)}, u32[]{:S(2)}) async-start(bf16[2,96,256]{2,1,0:T(8,128)(2,1)} %bitcast.43), calls=%async_computation.5 | async-start | bytes 196608 | tf_op jit(solution)/shard_map/all_to_all | solution.py:283
  195.5 2.9 %copy-start.19 = (bf16[192,384]{1,0:T(8,128)(2,1)}, bf16[192,384]{1,0:T(8,128)(2,1)S(1)}, u32[]{:S(2)}) copy-start(bf16[192,384]{1,0:T(8,128)(2,1)S(1)} %reduce_sum.25) | copy-start | bytes 442372
  (8 other events, 5.7 us)
Sparse Core Ops, SparseCore 0:
  17.1 85.9 all-gather.1
  119.0 71.0 reduce-scatter.1

commit v4 on v3

--- a/solution.py
+++ b/solution.py
@@ -40,63 +40,59 @@
 SETS = ((0, 0, 4), (1, 0, 4), (2, 0, 4), (3, 0, 2), (3, 2, 2))
 
 
+def start_all(pairs, sems, first=0):
+    copies = [
+        pltpu.make_async_copy(source, target, sems.at[first + n])
+        for n, (source, target) in enumerate(pairs)
+    ]
+    for copy in copies:
+        copy.start()
+    return copies
+
+
+def wait_all(copies):
+    for copy in copies:
+        copy.wait()
+
+
+def partner_pieces(mine, theirs, core, first, size):
+    for source, at in ((mine, core), (theirs, 1 - core)):
+        yield source.at[pl.ds(first, size)], aligned(at * size, size)
+
+
 def forward_kernel(head, place, *refs):
-    sets, (qkv_own, out_own, mine, theirs) = refs[:5], refs[5:9]
-    normed, attention, query, key, inverses, value, heads = refs[9:16]
-    branch, qkv, out, sems = refs[16:]
+    gathered, qkv_own, out_own, mine, theirs = refs[:5]
+    results, branch_result = refs[5:12], refs[12]
+    raw, qkv, out, branch = refs[13:17]
+    kept, sems = refs[17:24], refs[24]
+    normed, attention, query, key, inverses, value, heads = kept
     features = normed.shape[0]
     block = features // (4 * GROUP)
     core = place[4]
     thirds, quarter = 3 * head // 2, head // 2
-    copies = [
-        pltpu.make_async_copy(qkv_own, qkv.at[0], sems.at[0]),
-        pltpu.make_async_copy(out_own, out.at[0], sems.at[1]),
-    ]
-    for n, (source, at) in enumerate(((mine, core), (theirs, 1 - core))):
-        copies.append(
-            pltpu.make_async_copy(
-                source.at[pl.ds(0, thirds)], qkv.at[1, aligned(at * thirds, thirds)], sems.at[2 + 2 * n]
-            )
-        )
-        copies.append(
-            pltpu.make_async_copy(
-                source.at[pl.ds(thirds, quarter)],
-                out.at[1, aligned(at * quarter, quarter)],
-                sems.at[3 + 2 * n],
-            )
-        )
-    for copy in copies:
-        copy.start()
-
-    def over_blocks(body, carried):
-        for ref, (which, first, count) in zip(sets, SETS):
-            for n in range(count):
-                rows = ref[block * n : block * (n + 1), :].astype(wide)
-                at = aligned((GROUP * (first + n) + place[which]) * block, block)
-                carried = body(rows, at, carried)
-        return carried
+    rows_in = start_all([(gathered, raw)], sems)
+    weights_in = [(qkv_own, qkv.at[0]), (out_own, out.at[0])]
+    for source, at in partner_pieces(mine, theirs, core, 0, thirds):
+        weights_in.append((source, qkv.at[1, at]))
+    for source, at in partner_pieces(mine, theirs, core, thirds, quarter):
+        weights_in.append((source, out.at[1, at]))
+    weights_in = start_all(weights_in, sems, 1)
+    wait_all(rows_in)
+
+    def rows_of(n):
+        return raw[block * n : block * (n + 1), :].astype(wide)
 
     def fold(rows):
         return jnp.sum(rows.reshape(block // 8, 8, PATCHES), 0)
 
-    zero = jnp.zeros((8, PATCHES), wide)
-    total = over_blocks(lambda rows, at, t: t + fold(rows), zero)
-    mean = jnp.sum(total, 0, keepdims=True) / features
-
-    def squares(rows, at, carried):
-        centre = rows - mean
-        return carried + fold(centre * centre)
-
-    variance = jnp.sum(over_blocks(squares, zero), 0, keepdims=True) / features
-    scale = lax.rsqrt(variance + epsilon)
-
-    def write(rows, at, carried):
-        normed[at, :] = ((rows - mean) * scale).astype(low)
-        return carried
-
-    over_blocks(write, None)
-    for copy in copies:
-        copy.wait()
+    blocks = range(4 * GROUP)
+    mean = jnp.sum(sum(fold(rows_of(n)) for n in blocks), 0, keepdims=True) / features
+    variance = sum(fold((rows_of(n) - mean) * (rows_of(n) - mean)) for n in blocks)
+    scale = lax.rsqrt(jnp.sum(variance, 0, keepdims=True) / features + epsilon)
+    for n in blocks:
+        normed[block * n : block * (n + 1), :] = ((rows_of(n) - mean) * scale).astype(low)
+    results_out = start_all([(normed, results[0])], sems, 7)
+    wait_all(weights_in)
     for slot in range(2):
         projected = contract(qkv[slot], normed[...], 1, 0).astype(low)
         query_norm, query_inv = normalize_first(projected[:head].astype(wide))
@@ -112,35 +108,41 @@
         inverses[slot, 1:2, :] = key_inv
         value[slot] = values
         heads[slot] = contract(values, attend.astype(low), 1, 0).astype(low)
+    results_out += start_all(list(zip(kept[1:], results[1:])), sems, 8)
     both_heads = heads[...].reshape(2 * head, PATCHES)
-    step = 512
-    for start in range(0, features, step):
+    step = 768
+    for n, start in enumerate(range(0, features, step)):
         both = out[:, :, start : start + step].reshape(2 * head, step)
         branch[start : start + step, :] = contract(both, both_heads, 0, 0).astype(low)
-
-
-def backward_kernel(head, place, cotangent, out_own, mine, theirs, *refs):
-    normed, attention, query, key, inverses, value, heads = refs[:7]
-    shares, out, sems = refs[7:]
+        part = pl.ds(start, step)
+        results_out += start_all([(branch.at[part], branch_result.at[part])], sems, 14 + n)
+    wait_all(results_out)
+
+
+def backward_kernel(head, place, *refs):
+    results, sets, (out_own, mine, theirs) = refs[:7], refs[7:12], refs[12:15]
+    shares, cotangent, out = refs[15:18]
+    kept, sems = refs[18:25], refs[25]
+    normed, attention, query, key, inverses, value, heads = kept
     core = place[4]
     thirds, quarter = 3 * head // 2, head // 2
-    copies = [pltpu.make_async_copy(out_own, out.at[0], sems.at[0])]
-    for n, (source, at) in enumerate(((mine, core), (theirs, 1 - core))):
-        copies.append(
-            pltpu.make_async_copy(
-                source.at[pl.ds(thirds, quarter)],
-                out.at[1, aligned(at * quarter, quarter)],
-                sems.at[1 + n],
-            )
-        )
-    for copy in copies:
-        copy.start()
-    for copy in copies:
-        copy.wait()
+    block = cotangent.shape[0] // (4 * GROUP)
+    first_in = [(out_own, out.at[0])]
+    for ref, (which, first, count) in zip(sets, SETS):
+        for n in range(count):
+            at = aligned((GROUP * (first + n) + place[which]) * block, block)
+            first_in.append((ref.at[pl.ds(block * n, block)], cotangent.at[at]))
+    for source, at in partner_pieces(mine, theirs, core, thirds, quarter):
+        first_in.append((source, out.at[1, at]))
+    first_in = start_all(first_in, sems)
+    kept_in = start_all(list(zip(results[1:], kept[1:])) + [(results[0], normed)], sems, 19)
+    wait_all(first_in)
     scaling = head ** (-0.5)
     cores, _, chips, rows, columns = shares.shape
-    for slot in range(2):
-        grad = contract(out[slot], cotangent[...], 1, 0).astype(low)
+    grads = [contract(out[slot], cotangent[...], 1, 0).astype(low) for slot in range(2)]
+    wait_all(kept_in[:-1])
+    rights = []
+    for slot, grad in enumerate(grads):
         attend = attention[slot]
         query_norm, key_norm = query[slot], key[slot]
         grad_weights = contract(value[slot], grad, 0, 0)
@@ -161,12 +163,15 @@
         grad_proj = jnp.concatenate([grad_query, grad_key, grad_values], 0).astype(low)
         tail = jnp.concatenate([grad_proj[256:], jnp.zeros((columns - 3 * head, PATCHES), low)], 0)
         lead = jnp.concatenate([jnp.zeros((3 * head - 256, PATCHES), low), heads[slot]], 0)
+        rights.append((grad_proj[:256], tail, lead))
+    wait_all(kept_in[-1:])
+    for slot, (main_right, tail, lead) in enumerate(rights):
         there = place[5 + slot]
         for owner in range(cores):
             for chip in range(chips):
                 at = slice((2 * chip + owner) * rows, (2 * chip + owner + 1) * rows)
                 main = normed[at, :]
-                shares[owner, there, chip, :, :256] = contract(main, grad_proj[:256], 1, 1).astype(low)
+                shares[owner, there, chip, :, :256] = contract(main, main_right, 1, 1).astype(low)
                 shares[owner, there, chip, :, 256:] = (
                     contract(main, tail, 1, 1) + contract(cotangent[at, :], lead, 1, 1)
                 ).astype(low)
@@ -199,7 +204,7 @@
     def by_image(values):
         return values.reshape(part, images, PATCHES).transpose(1, 0, 2)
 
-    mixed = lax.all_to_all(by_image(d_branch), "xl", 0, 0, tiled=True)
+    mixed = lax.all_to_all(by_image(activations), "xl", 0, 0, tiled=True)
 
     qkv_own, out_own = w_qkv.T, w_out.T
     thirds, quarter = 3 * head // 2, head // 2
@@ -210,16 +215,16 @@
         ],
         0,
     )
-    mine, activations, mixed = lax.optimization_barrier((mine, activations, mixed))
-    cotangent = lax.all_gather(mixed.reshape(xl * part, PATCHES), Z, axis=0, tiled=True)
+    mine, d_branch, mixed = lax.optimization_barrier((mine, d_branch, mixed))
+    gathered = lax.all_gather(mixed.reshape(xl * part, PATCHES), Z, axis=0, tiled=True)
     mine = lax.ppermute(mine, "xl", swap)
-    copies = jnp.broadcast_to(by_image(activations)[None], (zh, images, part, PATCHES))
+    copies = jnp.broadcast_to(by_image(d_branch)[None], (zh, images, part, PATCHES))
     same = lax.all_to_all(
         copies.reshape(zh * images, part, PATCHES), ("zh", "xl"), 0, 0, tiled=True
     ).reshape(zh * xl * part, PATCHES)
+    middle = zh * xl * part // 2
     mine, same = lax.optimization_barrier((mine, same))
     theirs = lax.ppermute(mine, "core", swap)
-    middle = zh * xl * part // 2
     sets = (
         same,
         shift(same, -1),
@@ -227,11 +232,12 @@
         shift(same[:middle], 2),
         shift(same[middle:], -2),
     )
+    gathered, _ = lax.optimization_barrier((gathered, same))
 
     shape = jax.ShapeDtypeStruct
     vmem = pl.BlockSpec(memory_space=pltpu.VMEM)
     smem = pl.BlockSpec(memory_space=pltpu.SMEM)
-    anywhere = pl.BlockSpec(memory_space=pl.ANY)
+    hbm = pl.BlockSpec(memory_space=pltpu.HBM)
     kept = (
         shape((features, PATCHES), low),
         shape((2, PATCHES, PATCHES), wide),
@@ -244,19 +250,22 @@
     outputs = pl.pallas_call(
         functools.partial(forward_kernel, head),
         out_shape=kept + (shape((features, PATCHES), low),),
-        in_specs=[smem] + [vmem] * 5 + [anywhere] * 4,
-        out_specs=[vmem] * 8,
+        in_specs=[smem] + [hbm] * 5,
+        out_specs=[hbm] * 8,
         scratch_shapes=[
+            pltpu.VMEM((features, PATCHES), low),
             pltpu.VMEM((2, 3 * head, features), low),
             pltpu.VMEM((2, head, features), low),
-            pltpu.SemaphoreType.DMA((6,)),
-        ],
+            pltpu.VMEM((features, PATCHES), low),
+        ]
+        + [pltpu.VMEM(k.shape, k.dtype) for k in kept]
+        + [pltpu.SemaphoreType.DMA((18,))],
         compiler_params=pltpu.CompilerParams(vmem_limit_bytes=40 << 20),
         cost_estimate=pl.CostEstimate(
             flops=2_000_000_000, bytes_accessed=14_000_000, transcendentals=131072
         ),
         name="forward",
-    )(place, *sets, qkv_own, out_own, mine, theirs)
+    )(place, gathered, qkv_own, out_own, mine, theirs)
     kept, branch = outputs[:7], outputs[7]
     summed = lax.psum_scatter(branch, Z, scatter_dimension=0, tiled=True)
     columns = 4 * head
@@ -264,15 +273,20 @@
     shares = pl.pallas_call(
         functools.partial(backward_kernel, head),
         out_shape=shape((core, xl, xh * y, rows, columns), low),
-        in_specs=[smem, vmem] + [anywhere] * 3 + [vmem] * 7,
+        in_specs=[smem] + [hbm] * 15,
         out_specs=vmem,
-        scratch_shapes=[pltpu.VMEM((2, head, features), low), pltpu.SemaphoreType.DMA((3,))],
+        scratch_shapes=[
+            pltpu.VMEM((features, PATCHES), low),
+            pltpu.VMEM((2, head, features), low),
+        ]
+        + [pltpu.VMEM(k.shape, k.dtype) for k in kept]
+        + [pltpu.SemaphoreType.DMA((26,))],
         compiler_params=pltpu.CompilerParams(vmem_limit_bytes=40 << 20),
         cost_estimate=pl.CostEstimate(
             flops=1_000_000, bytes_accessed=100_000, transcendentals=0
         ),
         name="backward",
-    )(place, cotangent, out_own, mine, theirs, *kept)
+    )(place, *kept, *sets, out_own, mine, theirs)
     pairs = lax.all_to_all(shares, "core", 0, 0, tiled=True)
     pair_sum = jnp.sum(pairs.astype(wide), 0).astype(low)
     grads = lax.all_to_all(

time: 207 us -> 216 us (1.043)
  the two profiles are of different devices: /device:TPU:12 before, /device:TPU:32 now
where the time goes in v4:
time: 216 us; the launch traced here: 215 us
  waiting for transfers between devices  73.9 us (34%)
  blocking collectives  46 us (21%)
  starting transfers between devices  39.9 us (18%)
  Pallas kernels  18.2 us (8%)
  local copies, waits for them, and re-layouts  16.2 us (8%)
  between operations  14.2 us (7%)
  other arithmetic  6.63 us (3%)
    all_to_all x1, blocking collectives, on_device(): lax.all_to_all(pair_sum.reshape(xl * xh * y, rows, columns), ('xl', 'xh',...  37.3 us
    all_gather x1, waiting for transfers between devices, on_device(): lax.all_gather(mixed.reshape(xl * part, PATCHES), Z, axis=0, tiled=True)  30.8 us
    ppermute x1, waiting for transfers between devices, on_device(): mine = lax.ppermute(mine, 'xl', swap)  28.8 us
    all_to_all x1, starting transfers between devices, on_device(): lax.all_to_all(copies.reshape(zh * images, part, PATCHES), ('zh', 'xl'),...  14.8 us
    ppermute x4, starting transfers between devices, shift(): return lax.ppermute(values, Z, [(i, (i + by) % size) for i in range(size)])  12.6 us
    ppermute x4, waiting for transfers between devices, shift(): return lax.ppermute(values, Z, [(i, (i + by) % size) for i in range(size)])  11.8 us
    unnamed x26, local copies, waits for them, and re-layouts  10.2 us
    pallas_call x1, Pallas kernels, on_device(): pl.pallas_call(functools.partial(backward_kernel, head), out_shape=shape(...  9.46 us
  transfers between devices with their start and end apart: 11, of which 6 were waited for; matrix products, arithmetic and copies ran while one was open for 5% of the time, Pallas kernels for 4%

profile of v4, /device:TPU:32, one launch (start us, length us, event | category | flops | bytes accessed | tf_op | source)
XLA Modules:
  0.0 215.1 jit_solution(13812031607698838763)
XLA Ops:
  7.2 1.5 copy.13
  8.7 3.3 %all-to-all-start = ((bf16[2,96,256]{2,1,0:T(8,128)(2,1)}), bf16[2,96,256]{2,1,0:T(8,128)(2,1)S(1)}, u32[]{:S(2)}, u32[]{:S(2)}) async-start(bf16[2,96,256]{2,1,0:T(8,128)(2,1)} %bitcast.28), calls=%async_computation | async-start | bytes 196608 | tf_op jit(solution)/shard_map/all_to_all | solution.py:207
  17.8 14.8 %all-to-all-start.1 = ((bf16[8,96,256]{2,1,0:T(8,128)(2,1)}), bf16[8,96,256]{2,1,0:T(8,128)(2,1)S(1)}, u32[]{:S(2)}, u32[]{:S(2)}) async-start(bf16[8,96,256]{2,1,0:T(8,128)(2,1)} %bitcast.12), calls=%async_computation.1 | async-start | bytes 786432 | tf_op jit(solution)/shard_map/all_to_all | solution.py:222
  32.6 3.9 %collective-permute-start = (bf16[192,3072]{1,0:T(8,128)(2,1)}, bf16[192,3072]{1,0:T(8,128)(2,1)S(1)}, u32[]{:S(2)}, u32[]{:S(2)}) collective-permute-start(bf16[192,3072]{1,0:T(8,128)(2,1)} %pad_maximum_fusion), channel_id=1, source_target_pairs={{0,1},{1,0},{2,3},{3,2},{4,5},{5,4},{6,7},{7,6},{8,9},{9,8},{10,11... | collective-permute-start | bytes 3538952 | tf_op jit(solution)/shard_map/ppermute | solution.py:220
  36.5 28.8 %collective-permute-done.refs_3_.refs_13_ = bf16[192,3072]{1,0:T(8,128)(2,1)S(1)} collective-permute-done((bf16[192,3072]{1,0:T(8,128)(2,1)}, bf16[192,3072]{1,0:T(8,128)(2,1)S(1)}, u32[]{:S(2)}, u32[]{:S(2)}) %collective-permute-start) | collective-permute-done | bytes 1179680 | tf_op jit(solution)/shard_map/ppermute | solution.py:220
  65.3 1.9 collective-permute-start.1
  68.4 30.8 %all-gather.2.cloned.1.call-done.refs_0_ = bf16[3072,256]{1,0:T(8,128)(2,1)} async-done(((bf16[192,256]{1,0:T(8,128)(2,1)}), bf16[3072,256]{1,0:T(8,128)(2,1)}) %all-gather.2.cloned.1.call-update) | async-done | bytes 1572880 | tf_op jit(solution)/shard_map/all_gather | solution.py:219
  99.2 1.3 copy-done.2
  100.5 1.5 copy-done.4
  101.9 1.4 copy-done.9
  103.3 8.8 %forward.1 = (bf16[3072,256]{1,0:T(8,128)(2,1)S(1)}, f32[2,256,256]{2,1,0:T(8,128)S(1)}, f32[2,96,256]{2,1,0:T(8,128)S(1)}, f32[2,96,256]{2,1,0:T(8,128)S(1)}, f...) custom-call(s32[7]{0:T(128)S(1)} %stack.31.place, ...), custom_call_target="tpu_custom_call" | custom-call | flops 2000000000 | bytes 14000000 | tf_op jit(solution)/shard_map/forward/pallas_call | solution.py:250
  113.4 2.8 %collective-permute-start.3 = (bf16[768,256]{1,0:T(8,128)(2,1)S(1)}, bf16[768,256]{1,0:T(8,128)(2,1)S(1)}, u32[]{:S(2)}, u32[]{:S(2)}) collective-permute-start(bf16[768,256]{1,0:T(8,128)(2,1)S(1)} %bitcast.30), channel_id=1, source_target_pairs={{0,2},{2,4},{4,6},{6,8},{8,10},{10,12},{12,14},{14,16},{16,18},{18... | collective-permute-start | bytes 1179656 | tf_op jit(solution)/shard_map/ppermute | solution.py:182
  116.3 3.0 %collective-permute-start.2 = (bf16[768,256]{1,0:T(8,128)(2,1)S(1)}, bf16[768,256]{1,0:T(8,128)(2,1)S(1)}, u32[]{:S(2)}, u32[]{:S(2)}) collective-permute-start(bf16[768,256]{1,0:T(8,128)(2,1)S(1)} %bitcast.31), channel_id=1, source_target_pairs={{0,30},{2,0},{4,2},{6,4},{8,6},{10,8},{12,10},{14,12},{16,14},{18,... | collective-permute-start | bytes 1179656 | tf_op jit(solution)/shard_map/ppermute | solution.py:182
  119.3 4.6 %collective-permute-start.5 = (bf16[384,256]{1,0:T(8,128)(2,1)S(1)}, bf16[384,256]{1,0:T(8,128)(2,1)S(1)}, u32[]{:S(2)}, u32[]{:S(2)}) collective-permute-start(bf16[384,256]{1,0:T(8,128)(2,1)S(1)} %get-tuple-element.35), channel_id=1, source_target_pairs={{0,28},{2,30},{4,0},{6,2},{8,4},{10,6},{12,8},{14,10},{16,12},{18,... | collective-permute-start | bytes 589832 | tf_op jit(solution)/shard_map/ppermute | solution.py:182
  123.9 2.2 %collective-permute-start.4 = (bf16[384,256]{1,0:T(8,128)(2,1)S(1)}, bf16[384,256]{1,0:T(8,128)(2,1)S(1)}, u32[]{:S(2)}, u32[]{:S(2)}) collective-permute-start(bf16[384,256]{1,0:T(8,128)(2,1)S(1)} %get-tuple-element.36), channel_id=1, source_target_pairs={{0,4},{2,6},{4,8},{6,10},{8,12},{10,14},{12,16},{14,18},{16,20},{1... | collective-permute-start | bytes 589832 | tf_op jit(solution)/shard_map/ppermute | solution.py:182
  126.1 7.6 %collective-permute-done.5.refs_11_ = bf16[384,256]{1,0:T(8,128)(2,1)S(1)} collective-permute-done((bf16[384,256]{1,0:T(8,128)(2,1)S(1)}, bf16[384,256]{1,0:T(8,128)(2,1)S(1)}, u32[]{:S(2)}, u32[]{:S(2)}) %collective-permute-start.5) | collective-permute-done | bytes 196640 | tf_op jit(solution)/shard_map/ppermute | solution.py:182
  133.7 4.2 %collective-permute-done.4.refs_10_ = bf16[384,256]{1,0:T(8,128)(2,1)S(1)} collective-permute-done((bf16[384,256]{1,0:T(8,128)(2,1)S(1)}, bf16[384,256]{1,0:T(8,128)(2,1)S(1)}, u32[]{:S(2)}, u32[]{:S(2)}) %collective-permute-start.4) | collective-permute-done | bytes 196640 | tf_op jit(solution)/shard_map/ppermute | solution.py:182
  141.0 9.5 %backward.1 = bf16[2,2,8,192,384]{4,3,2,1,0:T(8,128)(2,1)S(1)} custom-call(s32[7]{0:T(128)S(1)} %stack.31.place, bf16[3072,256]{1,0:T(8,128)(2,1)S(1)} %get-tuple-element.26.refs_0_, f32[2,256,256]{2,1,0:T(8,128)S(1)} %get-tuple-element.27.refs_1_, f32[2,96,256]{2,1,0:T(8,128)S(1)} %get-tuple-element.28.refs_2_, ...), custom_call_target="tpu_custom_call" | custom-call | flops 1000000 | bytes 100000 | tf_op jit(solution)/shard_map/backward/pallas_call | solution.py:273
  150.5 8.6 %all_to_all.25 = bf16[2,2,8,192,384]{4,3,2,1,0:T(8,128)(2,1)} all-to-all(bf16[2,2,8,192,384]{4,3,2,1,0:T(8,128)(2,1)S(1)} %backward.1), channel_id=1, replica_groups=mesh['xh'=2,'y'=4,'core'=2,'zh'=4,'zl'=4,'xl'=2] {'core'}, dimensions={0} | all-to-all | bytes 9437184 | tf_op jit(solution)/shard_map/all_to_all | solution.py:290
  159.1 3.5 %reduce_sum.24 = bf16[2,8,192,384]{3,2,1,0:T(8,128)(2,1)S(1)} reduce(bf16[2,2,8,192,384]{4,3,2,1,0:T(8,128)(2,1)} %all_to_all.25, bf16[]{:T(256)} %constant.50.clone.1), dimensions={0}, to_apply=%region_1.2 | reduce | flops 1179648 | bytes 7077890 | tf_op jit(solution)/shard_map/reduce_sum | solution.py:291
  162.6 37.3 %all_to_all.26 = bf16[16,192,384]{2,1,0:T(8,128)(2,1)} all-to-all(bf16[16,192,384]{2,1,0:T(8,128)(2,1)S(1)} %bitcast.37), channel_id=1, replica_groups=mesh['xh'=2,'y'=4,'core'=2,'zh'=4,'zl'=4,'xl'=2] {'xl','xh','y'}, dimensions={0} | all-to-all | bytes 4718592 | tf_op jit(solution)/shard_map/all_to_all | solution.py:292
  200.0 3.3 %all-to-all-start.4 = ((bf16[2,96,256]{2,1,0:T(8,128)(2,1)}), bf16[2,96,256]{2,1,0:T(8,128)(2,1)S(1)}, u32[]{:S(2)}, u32[]{:S(2)}) async-start(bf16[2,96,256]{2,1,0:T(8,128)(2,1)} %bitcast.43), calls=%async_computation.5 | async-start | bytes 196608 | tf_op jit(solution)/shard_map/all_to_all | solution.py:297
  203.3 2.0 reduce_sum.25
  206.0 1.6 all-to-all-done.4
  (43 shorter events, 12.6 us)
Async XLA Ops:
  8.7 7.6 %all-to-all-start = ((bf16[2,96,256]{2,1,0:T(8,128)(2,1)}), bf16[2,96,256]{2,1,0:T(8,128)(2,1)S(1)}, u32[]{:S(2)}, u32[]{:S(2)}) async-start(bf16[2,96,256]{2,1,0:T(8,128)(2,1)} %bitcast.28), calls=%async_computation | async-start | bytes 196608 | tf_op jit(solution)/shard_map/all_to_all | solution.py:207
  12.1 87.1 %all-gather.2.cloned.1.call-start = ((), (), s32[]{:S(2)}) async-start(), calls=%async_computation.6 | async-start | bytes 1671168 | tf_op jit(solution)/shard_map/all_gather | solution.py:219
  13.1 3.9 %copy-start.12 = (bf16[96,512]{1,0:T(8,128)(2,1)S(1)}, bf16[96,512]{1,0:T(8,128)(2,1)}, u32[]{:S(2)}) copy-start(bf16[96,512]{1,0:T(8,128)(2,1)} %param.7) | copy-start | bytes 294916
  14.4 84.8 %copy-start = (bf16[3072,96]{0,1:T(8,128)(2,1)S(1)}, bf16[3072,96]{0,1:T(8,128)(2,1)}, u32[]{:S(2)}) copy-start(bf16[3072,96]{0,1:T(8,128)(2,1)} %param.6) | copy-start | bytes 1769476
  16.3 0.6 copy-start.10
  17.8 47.5 %all-to-all-start.1 = ((bf16[8,96,256]{2,1,0:T(8,128)(2,1)}), bf16[8,96,256]{2,1,0:T(8,128)(2,1)S(1)}, u32[]{:S(2)}, u32[]{:S(2)}) async-start(bf16[8,96,256]{2,1,0:T(8,128)(2,1)} %bitcast.12), calls=%async_computation.1 | async-start | bytes 786432 | tf_op jit(solution)/shard_map/all_to_all | solution.py:222
  32.6 167.4 %reduce-scatter.2.cloned.1.call-start = ((), (), s32[]{:S(2)}) async-start(), calls=%async_computation.7 | async-start | bytes 1671168 | tf_op jit(solution)/shard_map/reduce_scatter | solution.py:270
  32.6 32.7 %collective-permute-start = (bf16[192,3072]{1,0:T(8,128)(2,1)}, bf16[192,3072]{1,0:T(8,128)(2,1)S(1)}, u32[]{:S(2)}, u32[]{:S(2)}) collective-permute-start(bf16[192,3072]{1,0:T(8,128)(2,1)} %pad_maximum_fusion), channel_id=1, source_target_pairs={{0,1},{1,0},{2,3},{3,2},{4,5},{5,4},{6,7},{7,6},{8,9},{9,8},{10,11... | collective-permute-start | bytes 3538952 | tf_op jit(solution)/shard_map/ppermute | solution.py:220
  65.3 33.9 %collective-permute-start.1 = (bf16[192,3072]{1,0:T(8,128)(2,1)S(1)}, bf16[192,3072]{1,0:T(8,128)(2,1)}, u32[]{:S(2)}, u32[]{:S(2)}) collective-permute-start(bf16[192,3072]{1,0:T(8,128)(2,1)S(1)} %collective-permute-done.refs_3_.refs_13_), channel_id=1, source_target_pairs={{0,32},{32,0},{1,33},{33,1},{2,34},{34,2},{3,35},{35,3},{4,36},{36... | collective-permute-start | bytes 3538952 | tf_op jit(solution)/shard_map/ppermute | solution.py:227
  67.2 1.0 copy-start.1
  99.2 1.3 copy-start.2
  100.5 1.5 copy-start.4
  101.9 1.4 copy-start.9
  112.1 0.6 copy-start.5
  112.8 0.6 copy-start.7
  113.4 24.5 %collective-permute-start.3 = (bf16[768,256]{1,0:T(8,128)(2,1)S(1)}, bf16[768,256]{1,0:T(8,128)(2,1)S(1)}, u32[]{:S(2)}, u32[]{:S(2)}) collective-permute-start(bf16[768,256]{1,0:T(8,128)(2,1)S(1)} %bitcast.30), channel_id=1, source_target_pairs={{0,2},{2,4},{4,6},{6,8},{8,10},{10,12},{12,14},{14,16},{16,18},{18... | collective-permute-start | bytes 1179656 | tf_op jit(solution)/shard_map/ppermute | solution.py:182
  116.3 21.6 %collective-permute-start.2 = (bf16[768,256]{1,0:T(8,128)(2,1)S(1)}, bf16[768,256]{1,0:T(8,128)(2,1)S(1)}, u32[]{:S(2)}, u32[]{:S(2)}) collective-permute-start(bf16[768,256]{1,0:T(8,128)(2,1)S(1)} %bitcast.31), channel_id=1, source_target_pairs={{0,30},{2,0},{4,2},{6,4},{8,6},{10,8},{12,10},{14,12},{16,14},{18,... | collective-permute-start | bytes 1179656 | tf_op jit(solution)/shard_map/ppermute | solution.py:182
  119.3 14.3 %collective-permute-start.5 = (bf16[384,256]{1,0:T(8,128)(2,1)S(1)}, bf16[384,256]{1,0:T(8,128)(2,1)S(1)}, u32[]{:S(2)}, u32[]{:S(2)}) collective-permute-start(bf16[384,256]{1,0:T(8,128)(2,1)S(1)} %get-tuple-element.35), channel_id=1, source_target_pairs={{0,28},{2,30},{4,0},{6,2},{8,4},{10,6},{12,8},{14,10},{16,12},{18,... | collective-permute-start | bytes 589832 | tf_op jit(solution)/shard_map/ppermute | solution.py:182
  123.9 14.0 %collective-permute-start.4 = (bf16[384,256]{1,0:T(8,128)(2,1)S(1)}, bf16[384,256]{1,0:T(8,128)(2,1)S(1)}, u32[]{:S(2)}, u32[]{:S(2)}) collective-permute-start(bf16[384,256]{1,0:T(8,128)(2,1)S(1)} %get-tuple-element.36), channel_id=1, source_target_pairs={{0,4},{2,6},{4,8},{6,10},{8,12},{10,14},{12,16},{14,18},{16,20},{1... | collective-permute-start | bytes 589832 | tf_op jit(solution)/shard_map/ppermute | solution.py:182
  137.9 1.3 copy-start.3
  139.2 0.9 copy-start.6
  140.1 0.9 copy-start.8
  200.0 7.6 %all-to-all-start.4 = ((bf16[2,96,256]{2,1,0:T(8,128)(2,1)}), bf16[2,96,256]{2,1,0:T(8,128)(2,1)S(1)}, u32[]{:S(2)}, u32[]{:S(2)}) async-start(bf16[2,96,256]{2,1,0:T(8,128)(2,1)} %bitcast.43), calls=%async_computation.5 | async-start | bytes 196608 | tf_op jit(solution)/shard_map/all_to_all | solution.py:297
  205.3 2.9 %copy-start.11 = (bf16[192,384]{1,0:T(8,128)(2,1)}, bf16[192,384]{1,0:T(8,128)(2,1)S(1)}, u32[]{:S(2)}) copy-start(bf16[192,384]{1,0:T(8,128)(2,1)S(1)} %reduce_sum.25) | copy-start | bytes 442372
Sparse Core Ops, SparseCore 0:
  17.1 82.0 all-gather.1
  113.6 68.6 reduce-scatter.1

commit v5 on v4

--- a/solution.py
+++ b/solution.py
@@ -61,22 +61,27 @@
 
 
 def forward_kernel(head, place, *refs):
-    gathered, qkv_own, out_own, mine, theirs = refs[:5]
-    results, branch_result = refs[5:12], refs[12]
-    raw, qkv, out, branch = refs[13:17]
-    kept, sems = refs[17:24], refs[24]
+    sets, (qkv_own, out_own, mine, theirs) = refs[:5], refs[5:9]
+    results, branch_result = refs[9:16], refs[16]
+    raw, qkv, out, branch = refs[17:21]
+    kept, sems = refs[21:28], refs[28]
     normed, attention, query, key, inverses, value, heads = kept
     features = normed.shape[0]
     block = features // (4 * GROUP)
     core = place[4]
     thirds, quarter = 3 * head // 2, head // 2
-    rows_in = start_all([(gathered, raw)], sems)
+    rows_in = []
+    for ref, (which, first, count) in zip(sets, SETS):
+        for n in range(count):
+            at = aligned((GROUP * (first + n) + place[which]) * block, block)
+            rows_in.append((ref.at[pl.ds(block * n, block)], raw.at[at]))
+    rows_in = start_all(rows_in, sems)
     weights_in = [(qkv_own, qkv.at[0]), (out_own, out.at[0])]
     for source, at in partner_pieces(mine, theirs, core, 0, thirds):
         weights_in.append((source, qkv.at[1, at]))
     for source, at in partner_pieces(mine, theirs, core, thirds, quarter):
         weights_in.append((source, out.at[1, at]))
-    weights_in = start_all(weights_in, sems, 1)
+    weights_in = start_all(weights_in, sems, 16)
     wait_all(rows_in)
 
     def rows_of(n):
@@ -91,7 +96,7 @@
     scale = lax.rsqrt(jnp.sum(variance, 0, keepdims=True) / features + epsilon)
     for n in blocks:
         normed[block * n : block * (n + 1), :] = ((rows_of(n) - mean) * scale).astype(low)
-    results_out = start_all([(normed, results[0])], sems, 7)
+    results_out = start_all([(normed, results[0])], sems, 22)
     wait_all(weights_in)
     for slot in range(2):
         projected = contract(qkv[slot], normed[...], 1, 0).astype(low)
@@ -108,34 +113,29 @@
         inverses[slot, 1:2, :] = key_inv
         value[slot] = values
         heads[slot] = contract(values, attend.astype(low), 1, 0).astype(low)
-    results_out += start_all(list(zip(kept[1:], results[1:])), sems, 8)
+    results_out += start_all(list(zip(kept[1:], results[1:])), sems, 23)
     both_heads = heads[...].reshape(2 * head, PATCHES)
     step = 768
     for n, start in enumerate(range(0, features, step)):
         both = out[:, :, start : start + step].reshape(2 * head, step)
         branch[start : start + step, :] = contract(both, both_heads, 0, 0).astype(low)
         part = pl.ds(start, step)
-        results_out += start_all([(branch.at[part], branch_result.at[part])], sems, 14 + n)
+        results_out += start_all([(branch.at[part], branch_result.at[part])], sems, 29 + n)
     wait_all(results_out)
 
 
 def backward_kernel(head, place, *refs):
-    results, sets, (out_own, mine, theirs) = refs[:7], refs[7:12], refs[12:15]
-    shares, cotangent, out = refs[15:18]
-    kept, sems = refs[18:25], refs[25]
+    results, cotangent_in, out_own, mine, theirs = refs[:7], refs[7], refs[8], refs[9], refs[10]
+    shares, cotangent, out = refs[11:14]
+    kept, sems = refs[14:21], refs[21]
     normed, attention, query, key, inverses, value, heads = kept
     core = place[4]
     thirds, quarter = 3 * head // 2, head // 2
-    block = cotangent.shape[0] // (4 * GROUP)
-    first_in = [(out_own, out.at[0])]
-    for ref, (which, first, count) in zip(sets, SETS):
-        for n in range(count):
-            at = aligned((GROUP * (first + n) + place[which]) * block, block)
-            first_in.append((ref.at[pl.ds(block * n, block)], cotangent.at[at]))
+    first_in = [(cotangent_in, cotangent), (out_own, out.at[0])]
     for source, at in partner_pieces(mine, theirs, core, thirds, quarter):
         first_in.append((source, out.at[1, at]))
     first_in = start_all(first_in, sems)
-    kept_in = start_all(list(zip(results[1:], kept[1:])) + [(results[0], normed)], sems, 19)
+    kept_in = start_all(list(zip(results[1:], kept[1:])) + [(results[0], normed)], sems, 4)
     wait_all(first_in)
     scaling = head ** (-0.5)
     cores, _, chips, rows, columns = shares.shape
@@ -201,10 +201,8 @@
         ]
     ).astype(jnp.int32)
 
-    def by_image(values):
-        return values.reshape(part, images, PATCHES).transpose(1, 0, 2)
-
-    mixed = lax.all_to_all(by_image(activations), "xl", 0, 0, tiled=True)
+    stacked = jnp.stack([activations, d_branch]).reshape(2, part, images, PATCHES)
+    mixed = lax.all_to_all(stacked.transpose(2, 0, 1, 3), "xl", 0, 0, tiled=True)
 
     qkv_own, out_own = w_qkv.T, w_out.T
     thirds, quarter = 3 * head // 2, head // 2
@@ -215,16 +213,15 @@
         ],
         0,
     )
-    mine, d_branch, mixed = lax.optimization_barrier((mine, d_branch, mixed))
-    gathered = lax.all_gather(mixed.reshape(xl * part, PATCHES), Z, axis=0, tiled=True)
+    mine, mixed = lax.optimization_barrier((mine, mixed))
+    chunk = xl * part
+    cotangent = lax.all_gather(mixed[:, 1].reshape(chunk, PATCHES), Z, axis=0, tiled=True)
     mine = lax.ppermute(mine, "xl", swap)
-    copies = jnp.broadcast_to(by_image(d_branch)[None], (zh, images, part, PATCHES))
-    same = lax.all_to_all(
-        copies.reshape(zh * images, part, PATCHES), ("zh", "xl"), 0, 0, tiled=True
-    ).reshape(zh * xl * part, PATCHES)
-    middle = zh * xl * part // 2
+    copies = jnp.broadcast_to(mixed[:, 0].reshape(1, chunk, PATCHES), (zh, chunk, PATCHES))
+    same = lax.all_to_all(copies, "zh", 0, 0, tiled=True).reshape(zh * chunk, PATCHES)
     mine, same = lax.optimization_barrier((mine, same))
     theirs = lax.ppermute(mine, "core", swap)
+    middle = zh * chunk // 2
     sets = (
         same,
         shift(same, -1),
@@ -232,7 +229,6 @@
         shift(same[:middle], 2),
         shift(same[middle:], -2),
     )
-    gathered, _ = lax.optimization_barrier((gathered, same))
 
     shape = jax.ShapeDtypeStruct
     vmem = pl.BlockSpec(memory_space=pltpu.VMEM)
@@ -250,7 +246,7 @@
     outputs = pl.pallas_call(
         functools.partial(forward_kernel, head),
         out_shape=kept + (shape((features, PATCHES), low),),
-        in_specs=[smem] + [hbm] * 5,
+        in_specs=[smem] + [hbm] * 9,
         out_specs=[hbm] * 8,
         scratch_shapes=[
             pltpu.VMEM((features, PATCHES), low),
@@ -259,13 +255,13 @@
             pltpu.VMEM((features, PATCHES), low),
         ]
         + [pltpu.VMEM(k.shape, k.dtype) for k in kept]
-        + [pltpu.SemaphoreType.DMA((18,))],
-        compiler_params=pltpu.CompilerParams(vmem_limit_bytes=40 << 20),
+        + [pltpu.SemaphoreType.DMA((33,))],
+        compiler_params=pltpu.CompilerParams(vmem_limit_bytes=60 << 20),
         cost_estimate=pl.CostEstimate(
             flops=2_000_000_000, bytes_accessed=14_000_000, transcendentals=131072
         ),
         name="forward",
-    )(place, gathered, qkv_own, out_own, mine, theirs)
+    )(place, *sets, qkv_own, out_own, mine, theirs)
     kept, branch = outputs[:7], outputs[7]
     summed = lax.psum_scatter(branch, Z, scatter_dimension=0, tiled=True)
     columns = 4 * head
@@ -273,20 +269,20 @@
     shares = pl.pallas_call(
         functools.partial(backward_kernel, head),
         out_shape=shape((core, xl, xh * y, rows, columns), low),
-        in_specs=[smem] + [hbm] * 15,
+        in_specs=[smem] + [hbm] * 11,
         out_specs=vmem,
         scratch_shapes=[
             pltpu.VMEM((features, PATCHES), low),
             pltpu.VMEM((2, head, features), low),
         ]
         + [pltpu.VMEM(k.shape, k.dtype) for k in kept]
-        + [pltpu.SemaphoreType.DMA((26,))],
-        compiler_params=pltpu.CompilerParams(vmem_limit_bytes=40 << 20),
+        + [pltpu.SemaphoreType.DMA((11,))],
+        compiler_params=pltpu.CompilerParams(vmem_limit_bytes=60 << 20),
         cost_estimate=pl.CostEstimate(
             flops=1_000_000, bytes_accessed=100_000, transcendentals=0
         ),
         name="backward",
-    )(place, *kept, *sets, out_own, mine, theirs)
+    )(place, *kept, cotangent, out_own, mine, theirs)
     pairs = lax.all_to_all(shares, "core", 0, 0, tiled=True)
     pair_sum = jnp.sum(pairs.astype(wide), 0).astype(low)
     grads = lax.all_to_all(

time: 216 us -> 195 us (0.903)
  the two profiles are of different devices: /device:TPU:32 before, /device:TPU:8 now
where the time goes in v5:
time: 195 us; the launch traced here: 194 us
  waiting for transfers between devices  56.5 us (29%)
  blocking collectives  49.6 us (25%)
  starting transfers between devices  40.8 us (21%)
  Pallas kernels  18.8 us (10%)
  between operations  14.3 us (7%)
  local copies, waits for them, and re-layouts  8.4 us (4%)
  other arithmetic  5.87 us (3%)
    all_to_all x1, blocking collectives, on_device(): lax.all_to_all(pair_sum.reshape(xl * xh * y, rows, columns), ('xl', 'xh',...  36.9 us
    all_to_all x1, waiting for transfers between devices, on_device(): lax.all_to_all(copies, 'zh', 0, 0, tiled=True).reshape(zh * chunk, PATCHES)  20.7 us
    ppermute x4, waiting for transfers between devices, shift(): return lax.ppermute(values, Z, [(i, (i + by) % size) for i in range(size)])  16.6 us
    all_to_all x1, starting transfers between devices, on_device(): lax.all_to_all(copies, 'zh', 0, 0, tiled=True).reshape(zh * chunk, PATCHES)  15.1 us
    ppermute x4, starting transfers between devices, shift(): return lax.ppermute(values, Z, [(i, (i + by) % size) for i in range(size)])  14.9 us
    all_to_all x1, blocking collectives, on_device(): pairs = lax.all_to_all(shares, 'core', 0, 0, tiled=True)  12.7 us
    pallas_call x1, Pallas kernels, on_device(): pl.pallas_call(functools.partial(backward_kernel, head), out_shape=shape(...  9.8 us
    pallas_call x1, Pallas kernels, on_device(): pl.pallas_call(functools.partial(forward_kernel, head), out_shape=kept +...  8.98 us
  transfers between devices with their start and end apart: 11, of which 6 were waited for; matrix products, arithmetic and copies ran while one was open for 5% of the time, Pallas kernels for 10%

profile of v5, /device:TPU:8, one launch (start us, length us, event | category | flops | bytes accessed | tf_op | source)
XLA Modules:
  0.0 194.3 jit_solution(14220496653719125519)
XLA Ops:
  7.2 1.0 stack.41
  8.2 0.9 stack.42
  10.1 3.4 %all-to-all-start = ((bf16[2,2,96,256]{3,2,1,0:T(8,128)(2,1)}), bf16[2,2,96,256]{3,2,1,0:T(8,128)(2,1)S(1)}, u32[]{:S(2)}, u32[]{:S(2)}) async-start(bf16[2,2,96,256]{3,2,1,0:T(8,128)(2,1)} %copy.11), calls=%async_computation | async-start | bytes 393216 | tf_op jit(solution)/shard_map/all_to_all | solution.py:205
  13.6 1.2 dynamic-slice_bitcast_fusion
  14.9 3.4 %all-to-all-done = bf16[2,2,96,256]{3,2,1,0:T(8,128)(2,1)S(1)} async-done(((bf16[2,2,96,256]{3,2,1,0:T(8,128)(2,1)}), bf16[2,2,96,256]{3,2,1,0:T(8,128)(2,1)S(1)}, u32[]{:S(2)}, u32[]{:S(2)}) %all-to-all-start) | async-done | bytes 196640 | tf_op jit(solution)/shard_map/all_to_all | solution.py:205
  19.8 15.1 %all-to-all-start.1 = ((bf16[4,192,256]{2,1,0:T(8,128)(2,1)}), bf16[4,192,256]{2,1,0:T(8,128)(2,1)S(1)}, u32[]{:S(2)}, u32[]{:S(2)}) async-start(bf16[4,192,256]{2,1,0:T(8,128)(2,1)} %broadcast_in_dim.8), calls=%async_computation.1 | async-start | bytes 786432 | tf_op jit(solution)/shard_map/all_to_all | solution.py:221
  34.9 2.1 %collective-permute-start = (bf16[192,3072]{1,0:T(8,128)(2,1)S(1)}, bf16[192,3072]{1,0:T(8,128)(2,1)S(1)}, u32[]{:S(2)}, u32[]{:S(2)}) collective-permute-start(bf16[192,3072]{1,0:T(8,128)(2,1)S(1)} %pad_maximum_fusion), channel_id=1, source_target_pairs={{0,1},{1,0},{2,3},{3,2},{4,5},{5,4},{6,7},{7,6},{8,9},{9,8},{10,11... | collective-permute-start | bytes 3538952 | tf_op jit(solution)/shard_map/ppermute | solution.py:219
  37.0 20.7 %all-to-all-done.1 = bf16[4,192,256]{2,1,0:T(8,128)(2,1)S(1)} async-done(((bf16[4,192,256]{2,1,0:T(8,128)(2,1)}), bf16[4,192,256]{2,1,0:T(8,128)(2,1)S(1)}, u32[]{:S(2)}, u32[]{:S(2)}) %all-to-all-start.1) | async-done | bytes 393248 | tf_op jit(solution)/shard_map/all_to_all | solution.py:221
  57.7 5.3 %collective-permute-done.refs_7_.refs_9_ = bf16[192,3072]{1,0:T(8,128)(2,1)S(1)} collective-permute-done((bf16[192,3072]{1,0:T(8,128)(2,1)S(1)}, bf16[192,3072]{1,0:T(8,128)(2,1)S(1)}, u32[]{:S(2)}, u32[]{:S(2)}) %collective-permute-start) | collective-permute-done | bytes 1179680 | tf_op jit(solution)/shard_map/ppermute | solution.py:219
  63.0 1.9 collective-permute-start.5
  64.9 3.6 %collective-permute-start.2 = (bf16[768,256]{1,0:T(8,128)(2,1)S(1)}, bf16[768,256]{1,0:T(8,128)(2,1)S(1)}, u32[]{:S(2)}, u32[]{:S(2)}) collective-permute-start(bf16[768,256]{1,0:T(8,128)(2,1)S(1)} %bitcast.25), channel_id=1, source_target_pairs={{0,2},{2,4},{4,6},{6,8},{8,10},{10,12},{12,14},{14,16},{16,18},{18... | collective-permute-start | bytes 1179656 | tf_op jit(solution)/shard_map/ppermute | solution.py:182
  68.5 4.6 %collective-permute-start.1 = (bf16[768,256]{1,0:T(8,128)(2,1)S(1)}, bf16[768,256]{1,0:T(8,128)(2,1)}, u32[]{:S(2)}, u32[]{:S(2)}) collective-permute-start(bf16[768,256]{1,0:T(8,128)(2,1)S(1)} %bitcast.26), channel_id=1, source_target_pairs={{0,30},{2,0},{4,2},{6,4},{8,6},{10,8},{12,10},{14,12},{16,14},{18,... | collective-permute-start | bytes 1179656 | tf_op jit(solution)/shard_map/ppermute | solution.py:182
  73.1 4.4 %collective-permute-start.4 = (bf16[384,256]{1,0:T(8,128)(2,1)S(1)}, bf16[384,256]{1,0:T(8,128)(2,1)}, u32[]{:S(2)}, u32[]{:S(2)}) collective-permute-start(bf16[384,256]{1,0:T(8,128)(2,1)S(1)} %get-tuple-element.31), channel_id=1, source_target_pairs={{0,28},{2,30},{4,0},{6,2},{8,4},{10,6},{12,8},{14,10},{16,12},{18,... | collective-permute-start | bytes 589832 | tf_op jit(solution)/shard_map/ppermute | solution.py:182
  77.5 2.4 %collective-permute-start.3 = (bf16[384,256]{1,0:T(8,128)(2,1)S(1)}, bf16[384,256]{1,0:T(8,128)(2,1)}, u32[]{:S(2)}, u32[]{:S(2)}) collective-permute-start(bf16[384,256]{1,0:T(8,128)(2,1)S(1)} %get-tuple-element.32), channel_id=1, source_target_pairs={{0,4},{2,6},{4,8},{6,10},{8,12},{10,14},{12,16},{14,18},{16,20},{1... | collective-permute-start | bytes 589832 | tf_op jit(solution)/shard_map/ppermute | solution.py:182
  80.5 16.6 %collective-permute-done.4.refs_4_ = bf16[384,256]{1,0:T(8,128)(2,1)} collective-permute-done((bf16[384,256]{1,0:T(8,128)(2,1)S(1)}, bf16[384,256]{1,0:T(8,128)(2,1)}, u32[]{:S(2)}, u32[]{:S(2)}) %collective-permute-start.4) | collective-permute-done | bytes 196640 | tf_op jit(solution)/shard_map/ppermute | solution.py:182
  98.3 9.0 %forward.1 = (bf16[3072,256]{1,0:T(8,128)(2,1)}, f32[2,256,256]{2,1,0:T(8,128)}, f32[2,96,256]{2,1,0:T(8,128)}, f32[2,96,256]{2,1,0:T(8,128)}, f32[2,8,256]{2,1,...) custom-call(s32[7]{0:T(128)} %stack.40.place, ...), custom_call_target="tpu_custom_call" | custom-call | flops 2000000000 | bytes 14000000 | tf_op jit(solution)/shard_map/forward/pallas_call | solution.py:246
  107.4 9.8 %backward.1 = bf16[2,2,8,192,384]{4,3,2,1,0:T(8,128)(2,1)} custom-call(s32[7]{0:T(128)} %stack.40.place, bf16[3072,256]{1,0:T(8,128)(2,1)} %get-tuple-element.22.refs_0_, f32[2,256,256]{2,1,0:T(8,128)} %get-tuple-element.23.refs_1_, f32[2,96,256]{2,1,0:T(8,128)} %get-tuple-element.24.refs_2_, f32[2,96,256]{2,1,0:T(8,128)} %get-tuple-element.25.refs_3_, ...), custom_call_target="tpu_custom_call" | custom-call | flops 1000000 | bytes 100000 | tf_op jit(solution)/shard_map/backward/pallas_call | solution.py:269
  117.2 12.7 %all_to_all.25 = bf16[2,2,8,192,384]{4,3,2,1,0:T(8,128)(2,1)} all-to-all(bf16[2,2,8,192,384]{4,3,2,1,0:T(8,128)(2,1)} %backward.1), channel_id=1, replica_groups=mesh['xh'=2,'y'=4,'core'=2,'zh'=4,'zl'=4,'xl'=2] {'core'}, dimensions={0} | all-to-all | bytes 9437184 | tf_op jit(solution)/shard_map/all_to_all | solution.py:286
  129.9 3.5 %reduce_sum.24 = bf16[2,8,192,384]{3,2,1,0:T(8,128)(2,1)S(1)} reduce(bf16[2,2,8,192,384]{4,3,2,1,0:T(8,128)(2,1)} %all_to_all.25, bf16[]{:T(256)} %constant.50.clone.1), dimensions={0}, to_apply=%region_1.2 | reduce | flops 1179648 | bytes 7077890 | tf_op jit(solution)/shard_map/reduce_sum | solution.py:287
  133.4 36.9 %all_to_all.26 = bf16[16,192,384]{2,1,0:T(8,128)(2,1)} all-to-all(bf16[16,192,384]{2,1,0:T(8,128)(2,1)S(1)} %bitcast.24), channel_id=1, replica_groups=mesh['xh'=2,'y'=4,'core'=2,'zh'=4,'zl'=4,'xl'=2] {'xl','xh','y'}, dimensions={0} | all-to-all | bytes 4718592 | tf_op jit(solution)/shard_map/all_to_all | solution.py:288
  170.3 8.8 %reduce-scatter.2.cloned.1.call-done = bf16[192,256]{1,0:T(8,128)(2,1)} async-done(((bf16[3072,256]{1,0:T(8,128)(2,1)}), bf16[192,256]{1,0:T(8,128)(2,1)}) %reduce-scatter.2.cloned.1.call-update) | async-done | bytes 98320 | tf_op jit(solution)/shard_map/reduce_scatter | solution.py:266
  179.1 3.3 %all-to-all-start.4 = ((bf16[2,96,256]{2,1,0:T(8,128)(2,1)}), bf16[2,96,256]{2,1,0:T(8,128)(2,1)S(1)}, u32[]{:S(2)}, u32[]{:S(2)}) async-start(bf16[2,96,256]{2,1,0:T(8,128)(2,1)} %bitcast.36), calls=%async_computation.5 | async-start | bytes 196608 | tf_op jit(solution)/shard_map/all_to_all | solution.py:293
  182.5 2.0 %reduce_sum.25 = bf16[192,384]{1,0:T(8,128)(2,1)S(1)} reduce(bf16[16,192,384]{2,1,0:T(8,128)(2,1)} %all_to_all.26, bf16[]{:T(256)} %constant.50.clone.1), dimensions={0}, to_apply=%region_2.3 | reduce | flops 1105920 | bytes 2506754 | tf_op jit(solution)/shard_map/reduce_sum | solution.py:292
  185.2 1.6 all-to-all-done.4
  (31 shorter events, 5.7 us)
Async XLA Ops:
  7.2 6.4 %copy-start.1 = (bf16[3072,96]{0,1:T(8,128)(2,1)S(1)}, bf16[3072,96]{0,1:T(8,128)(2,1)}, u32[]{:S(2)}) copy-start(bf16[3072,96]{0,1:T(8,128)(2,1)} %param.6) | copy-start | bytes 1769476
  10.1 8.2 %all-to-all-start = ((bf16[2,2,96,256]{3,2,1,0:T(8,128)(2,1)}), bf16[2,2,96,256]{3,2,1,0:T(8,128)(2,1)S(1)}, u32[]{:S(2)}, u32[]{:S(2)}) async-start(bf16[2,2,96,256]{3,2,1,0:T(8,128)(2,1)} %copy.11), calls=%async_computation | async-start | bytes 393216 | tf_op jit(solution)/shard_map/all_to_all | solution.py:205
  13.5 93.8 %all-gather.2.cloned.1.call-start = ((), (), s32[]{:S(2)}) async-start(), calls=%async_computation.7 | async-start | bytes 1671168 | tf_op jit(solution)/shard_map/all_gather | solution.py:218
  19.8 37.9 %all-to-all-start.1 = ((bf16[4,192,256]{2,1,0:T(8,128)(2,1)}), bf16[4,192,256]{2,1,0:T(8,128)(2,1)S(1)}, u32[]{:S(2)}, u32[]{:S(2)}) async-start(bf16[4,192,256]{2,1,0:T(8,128)(2,1)} %broadcast_in_dim.8), calls=%async_computation.1 | async-start | bytes 786432 | tf_op jit(solution)/shard_map/all_to_all | solution.py:221
  34.9 144.3 %reduce-scatter.2.cloned.1.call-start = ((), (), s32[]{:S(2)}) async-start(), calls=%async_computation.6 | async-start | bytes 1671168 | tf_op jit(solution)/shard_map/reduce_scatter | solution.py:266
  34.9 28.2 %collective-permute-start = (bf16[192,3072]{1,0:T(8,128)(2,1)S(1)}, bf16[192,3072]{1,0:T(8,128)(2,1)S(1)}, u32[]{:S(2)}, u32[]{:S(2)}) collective-permute-start(bf16[192,3072]{1,0:T(8,128)(2,1)S(1)} %pad_maximum_fusion), channel_id=1, source_target_pairs={{0,1},{1,0},{2,3},{3,2},{4,5},{5,4},{6,7},{7,6},{8,9},{9,8},{10,11... | collective-permute-start | bytes 3538952 | tf_op jit(solution)/shard_map/ppermute | solution.py:219
  57.7 39.5 %copy-start = (bf16[4,192,256]{2,1,0:T(8,128)(2,1)}, bf16[4,192,256]{2,1,0:T(8,128)(2,1)S(1)}, u32[]{:S(2)}) copy-start(bf16[4,192,256]{2,1,0:T(8,128)(2,1)S(1)} %all-to-all-done.1) | copy-start | bytes 1179652
  63.0 34.2 %copy-start.2 = (bf16[192,3072]{1,0:T(8,128)(2,1)}, bf16[192,3072]{1,0:T(8,128)(2,1)S(1)}, u32[]{:S(2)}) copy-start(bf16[192,3072]{1,0:T(8,128)(2,1)S(1)} %collective-permute-done.refs_7_.refs_9_) | copy-start | bytes 3538948
  63.0 34.2 %collective-permute-start.5 = (bf16[192,3072]{1,0:T(8,128)(2,1)S(1)}, bf16[192,3072]{1,0:T(8,128)(2,1)S(1)}, u32[]{:S(2)}, u32[]{:S(2)}) collective-permute-start(bf16[192,3072]{1,0:T(8,128)(2,1)S(1)} %collective-permute-done.refs_7_.refs_9_), channel_id=1, source_target_pairs={{0,32},{32,0},{1,33},{33,1},{2,34},{34,2},{3,35},{35,3},{4,36},{36... | collective-permute-start | bytes 3538952 | tf_op jit(solution)/shard_map/ppermute | solution.py:223
  64.9 32.2 %collective-permute-start.2 = (bf16[768,256]{1,0:T(8,128)(2,1)S(1)}, bf16[768,256]{1,0:T(8,128)(2,1)S(1)}, u32[]{:S(2)}, u32[]{:S(2)}) collective-permute-start(bf16[768,256]{1,0:T(8,128)(2,1)S(1)} %bitcast.25), channel_id=1, source_target_pairs={{0,2},{2,4},{4,6},{6,8},{8,10},{10,12},{12,14},{14,16},{16,18},{18... | collective-permute-start | bytes 1179656 | tf_op jit(solution)/shard_map/ppermute | solution.py:182
  68.5 28.7 %collective-permute-start.1 = (bf16[768,256]{1,0:T(8,128)(2,1)S(1)}, bf16[768,256]{1,0:T(8,128)(2,1)}, u32[]{:S(2)}, u32[]{:S(2)}) collective-permute-start(bf16[768,256]{1,0:T(8,128)(2,1)S(1)} %bitcast.26), channel_id=1, source_target_pairs={{0,30},{2,0},{4,2},{6,4},{8,6},{10,8},{12,10},{14,12},{16,14},{18,... | collective-permute-start | bytes 1179656 | tf_op jit(solution)/shard_map/ppermute | solution.py:182
  73.1 24.0 %collective-permute-start.4 = (bf16[384,256]{1,0:T(8,128)(2,1)S(1)}, bf16[384,256]{1,0:T(8,128)(2,1)}, u32[]{:S(2)}, u32[]{:S(2)}) collective-permute-start(bf16[384,256]{1,0:T(8,128)(2,1)S(1)} %get-tuple-element.31), channel_id=1, source_target_pairs={{0,28},{2,30},{4,0},{6,2},{8,4},{10,6},{12,8},{14,10},{16,12},{18,... | collective-permute-start | bytes 589832 | tf_op jit(solution)/shard_map/ppermute | solution.py:182
  77.5 19.6 %collective-permute-start.3 = (bf16[384,256]{1,0:T(8,128)(2,1)S(1)}, bf16[384,256]{1,0:T(8,128)(2,1)}, u32[]{:S(2)}, u32[]{:S(2)}) collective-permute-start(bf16[384,256]{1,0:T(8,128)(2,1)S(1)} %get-tuple-element.32), channel_id=1, source_target_pairs={{0,4},{2,6},{4,8},{6,10},{8,12},{10,14},{12,16},{14,18},{16,20},{1... | collective-permute-start | bytes 589832 | tf_op jit(solution)/shard_map/ppermute | solution.py:182
  97.2 0.7 copy-start.5
  97.2 1.1 copy-start.3
  179.1 7.6 %all-to-all-start.4 = ((bf16[2,96,256]{2,1,0:T(8,128)(2,1)}), bf16[2,96,256]{2,1,0:T(8,128)(2,1)S(1)}, u32[]{:S(2)}, u32[]{:S(2)}) async-start(bf16[2,96,256]{2,1,0:T(8,128)(2,1)} %bitcast.36), calls=%async_computation.5 | async-start | bytes 196608 | tf_op jit(solution)/shard_map/all_to_all | solution.py:293
  184.5 2.9 %copy-start.4 = (bf16[192,384]{1,0:T(8,128)(2,1)}, bf16[192,384]{1,0:T(8,128)(2,1)S(1)}, u32[]{:S(2)}) copy-start(bf16[192,384]{1,0:T(8,128)(2,1)S(1)} %reduce_sum.25) | copy-start | bytes 442372
Sparse Core Ops, SparseCore 0:
  19.1 86.0 all-gather.1
  108.0 71.0 reduce-scatter.1

commit v6 on v5

--- a/solution.py
+++ b/solution.py
@@ -60,7 +60,14 @@
         yield source.at[pl.ds(first, size)], aligned(at * size, size)
 
 
-def forward_kernel(head, place, *refs):
+def rows_from(sets, place, target, part, which_array):
+    for ref, (which, first, count) in zip(sets, SETS):
+        for n in range(2 * count):
+            at = ((GROUP * (first + n // 2) + place[which]) * 2 + n % 2) * part
+            yield ref.at[pl.ds((2 * n + which_array) * part, part)], target.at[aligned(at, part)]
+
+
+def forward_kernel(part, head, place, *refs):
     sets, (qkv_own, out_own, mine, theirs) = refs[:5], refs[5:9]
     results, branch_result = refs[9:16], refs[16]
     raw, qkv, out, branch = refs[17:21]
@@ -70,18 +77,13 @@
     block = features // (4 * GROUP)
     core = place[4]
     thirds, quarter = 3 * head // 2, head // 2
-    rows_in = []
-    for ref, (which, first, count) in zip(sets, SETS):
-        for n in range(count):
-            at = aligned((GROUP * (first + n) + place[which]) * block, block)
-            rows_in.append((ref.at[pl.ds(block * n, block)], raw.at[at]))
-    rows_in = start_all(rows_in, sems)
+    rows_in = start_all(rows_from(sets, place, raw, part, 0), sems)
     weights_in = [(qkv_own, qkv.at[0]), (out_own, out.at[0])]
     for source, at in partner_pieces(mine, theirs, core, 0, thirds):
         weights_in.append((source, qkv.at[1, at]))
     for source, at in partner_pieces(mine, theirs, core, thirds, quarter):
         weights_in.append((source, out.at[1, at]))
-    weights_in = start_all(weights_in, sems, 16)
+    weights_in = start_all(weights_in, sems, 32)
     wait_all(rows_in)
 
     def rows_of(n):
@@ -96,7 +98,7 @@
     scale = lax.rsqrt(jnp.sum(variance, 0, keepdims=True) / features + epsilon)
     for n in blocks:
         normed[block * n : block * (n + 1), :] = ((rows_of(n) - mean) * scale).astype(low)
-    results_out = start_all([(normed, results[0])], sems, 22)
+    results_out = start_all([(normed, results[0])], sems, 38)
     wait_all(weights_in)
     for slot in range(2):
         projected = contract(qkv[slot], normed[...], 1, 0).astype(low)
@@ -113,29 +115,29 @@
         inverses[slot, 1:2, :] = key_inv
         value[slot] = values
         heads[slot] = contract(values, attend.astype(low), 1, 0).astype(low)
-    results_out += start_all(list(zip(kept[1:], results[1:])), sems, 23)
+    results_out += start_all(list(zip(kept[1:], results[1:])), sems, 39)
     both_heads = heads[...].reshape(2 * head, PATCHES)
     step = 768
     for n, start in enumerate(range(0, features, step)):
         both = out[:, :, start : start + step].reshape(2 * head, step)
         branch[start : start + step, :] = contract(both, both_heads, 0, 0).astype(low)
         part = pl.ds(start, step)
-        results_out += start_all([(branch.at[part], branch_result.at[part])], sems, 29 + n)
+        results_out += start_all([(branch.at[part], branch_result.at[part])], sems, 45 + n)
     wait_all(results_out)
 
 
-def backward_kernel(head, place, *refs):
-    results, cotangent_in, out_own, mine, theirs = refs[:7], refs[7], refs[8], refs[9], refs[10]
-    shares, cotangent, out = refs[11:14]
-    kept, sems = refs[14:21], refs[21]
+def backward_kernel(part, head, place, *refs):
+    results, sets, (out_own, mine, theirs) = refs[:7], refs[7:12], refs[12:15]
+    shares, cotangent, out = refs[15:18]
+    kept, sems = refs[18:25], refs[25]
     normed, attention, query, key, inverses, value, heads = kept
     core = place[4]
     thirds, quarter = 3 * head // 2, head // 2
-    first_in = [(cotangent_in, cotangent), (out_own, out.at[0])]
+    first_in = [(out_own, out.at[0])]
     for source, at in partner_pieces(mine, theirs, core, thirds, quarter):
         first_in.append((source, out.at[1, at]))
-    first_in = start_all(first_in, sems)
-    kept_in = start_all(list(zip(results[1:], kept[1:])) + [(results[0], normed)], sems, 4)
+    first_in = start_all([*rows_from(sets, place, cotangent, part, 1), *first_in], sems)
+    kept_in = start_all(list(zip(results[1:], kept[1:])) + [(results[0], normed)], sems, 35)
     wait_all(first_in)
     scaling = head ** (-0.5)
     cores, _, chips, rows, columns = shares.shape
@@ -214,14 +216,11 @@
         0,
     )
     mine, mixed = lax.optimization_barrier((mine, mixed))
-    chunk = xl * part
-    cotangent = lax.all_gather(mixed[:, 1].reshape(chunk, PATCHES), Z, axis=0, tiled=True)
     mine = lax.ppermute(mine, "xl", swap)
-    copies = jnp.broadcast_to(mixed[:, 0].reshape(1, chunk, PATCHES), (zh, chunk, PATCHES))
-    same = lax.all_to_all(copies, "zh", 0, 0, tiled=True).reshape(zh * chunk, PATCHES)
+    same = lax.all_gather(mixed.reshape(xl * 2 * part, PATCHES), "zh", axis=0, tiled=True)
     mine, same = lax.optimization_barrier((mine, same))
     theirs = lax.ppermute(mine, "core", swap)
-    middle = zh * chunk // 2
+    middle = same.shape[0] // 2
     sets = (
         same,
         shift(same, -1),
@@ -244,7 +243,7 @@
         shape((2, head, PATCHES), low),
     )
     outputs = pl.pallas_call(
-        functools.partial(forward_kernel, head),
+        functools.partial(forward_kernel, part, head),
         out_shape=kept + (shape((features, PATCHES), low),),
         in_specs=[smem] + [hbm] * 9,
         out_specs=[hbm] * 8,
@@ -255,7 +254,7 @@
             pltpu.VMEM((features, PATCHES), low),
         ]
         + [pltpu.VMEM(k.shape, k.dtype) for k in kept]
-        + [pltpu.SemaphoreType.DMA((33,))],
+        + [pltpu.SemaphoreType.DMA((49,))],
         compiler_params=pltpu.CompilerParams(vmem_limit_bytes=60 << 20),
         cost_estimate=pl.CostEstimate(
             flops=2_000_000_000, bytes_accessed=14_000_000, transcendentals=131072
@@ -267,22 +266,22 @@
     columns = 4 * head
     rows = features // (core * xh * y)
     shares = pl.pallas_call(
-        functools.partial(backward_kernel, head),
+        functools.partial(backward_kernel, part, head),
         out_shape=shape((core, xl, xh * y, rows, columns), low),
-        in_specs=[smem] + [hbm] * 11,
+        in_specs=[smem] + [hbm] * 15,
         out_specs=vmem,
         scratch_shapes=[
             pltpu.VMEM((features, PATCHES), low),
             pltpu.VMEM((2, head, features), low),
         ]
         + [pltpu.VMEM(k.shape, k.dtype) for k in kept]
-        + [pltpu.SemaphoreType.DMA((11,))],
+        + [pltpu.SemaphoreType.DMA((42,))],
         compiler_params=pltpu.CompilerParams(vmem_limit_bytes=60 << 20),
         cost_estimate=pl.CostEstimate(
             flops=1_000_000, bytes_accessed=100_000, transcendentals=0
         ),
         name="backward",
-    )(place, *kept, cotangent, out_own, mine, theirs)
+    )(place, *kept, *sets, out_own, mine, theirs)
     pairs = lax.all_to_all(shares, "core", 0, 0, tiled=True)
     pair_sum = jnp.sum(pairs.astype(wide), 0).astype(low)
     grads = lax.all_to_all(

time: 195 us -> 201 us (1.031)
  blocking collectives: 49.6 us -> 89.5 us
  waiting for transfers between devices: 56.5 us -> 38.3 us
  starting transfers between devices: 40.8 us -> 25.5 us
    all_gather x0 -> x1, blocking collectives: none -> 39.7 us  [on_device(): lax.all_gather(mixed.reshape(xl * 2 * part, PATCHES), 'zh', axis=0, tiled...]
    all_to_all x1 -> x0, waiting for transfers between devices: 20.7 us -> none  [on_device(): lax.all_to_all(copies, 'zh', 0, 0, tiled=True).reshape(zh * chunk, PATCHES)]
    all_to_all x1 -> x0, starting transfers between devices: 15.1 us -> none  [on_device(): lax.all_to_all(copies, 'zh', 0, 0, tiled=True).reshape(zh * chunk, PATCHES)]
    ppermute x4, waiting for transfers between devices: 16.6 us -> 22.9 us  [shift(): return lax.ppermute(values, Z, [(i, (i + by) % size) for i in range(size)])]
    ppermute x1, waiting for transfers between devices: 5.33 us -> 0.01 us  [on_device(): mine = lax.ppermute(mine, 'xl', swap)]
  transfers between devices with their start and end apart: 11 -> 9, of which waited for: 6 -> 5; matrix products, arithmetic and copies ran while one was open for 5% -> 4% of each run, Pallas kernels for 10% -> 5%
where the time goes in v6:
time: 201 us; the launch traced here: 200 us
  blocking collectives  89.5 us (45%)
  waiting for transfers between devices  38.3 us (19%)
  starting transfers between devices  25.5 us (13%)
  Pallas kernels  19.3 us (10%)
  between operations  14.2 us (7%)
  local copies, waits for them, and re-layouts  7.09 us (4%)
  other arithmetic  6.3 us (3%)
    all_gather x1, blocking collectives, on_device(): lax.all_gather(mixed.reshape(xl * 2 * part, PATCHES), 'zh', axis=0, tiled...  39.7 us
    all_to_all x1, blocking collectives, on_device(): lax.all_to_all(pair_sum.reshape(xl * xh * y, rows, columns), ('xl', 'xh',...  37 us
    ppermute x4, waiting for transfers between devices, shift(): return lax.ppermute(values, Z, [(i, (i + by) % size) for i in range(size)])  22.9 us
    ppermute x4, starting transfers between devices, shift(): return lax.ppermute(values, Z, [(i, (i + by) % size) for i in range(size)])  14.6 us
    all_to_all x1, blocking collectives, on_device(): pairs = lax.all_to_all(shares, 'core', 0, 0, tiled=True)  12.7 us
    pallas_call x1, Pallas kernels, on_device(): pl.pallas_call(functools.partial(backward_kernel, part, head), out_shape=...  10.2 us
    reduce_scatter x1, waiting for transfers between devices, on_device(): summed = lax.psum_scatter(branch, Z, scatter_dimension=0, tiled=True)  10.2 us
    pallas_call x1, Pallas kernels, on_device(): pl.pallas_call(functools.partial(forward_kernel, part, head), out_shape=k...  9.11 us
  transfers between devices with their start and end apart: 9, of which 5 were waited for; matrix products, arithmetic and copies ran while one was open for 4% of the time, Pallas kernels for 5%

profile of v6, /device:TPU:8, one launch (start us, length us, event | category | flops | bytes accessed | tf_op | source)
XLA Modules:
  0.0 200.2 jit_solution(12922937100543086278)
XLA Ops:
  7.2 1.0 stack.42
  9.9 3.4 %all-to-all-start = ((bf16[2,2,96,256]{3,2,1,0:T(8,128)(2,1)}), bf16[2,2,96,256]{3,2,1,0:T(8,128)(2,1)S(1)}, u32[]{:S(2)}, u32[]{:S(2)}) async-start(bf16[2,2,96,256]{3,2,1,0:T(8,128)(2,1)} %maximum_bitcast_fusion), calls=%async_computation | async-start | bytes 393216 | tf_op jit(solution)/shard_map/all_to_all | solution.py:207
  13.4 1.0 dynamic-slice_bitcast_fusion.1
  14.5 3.6 %all-to-all-done = bf16[2,2,96,256]{3,2,1,0:T(8,128)(2,1)S(1)} async-done(((bf16[2,2,96,256]{3,2,1,0:T(8,128)(2,1)}), bf16[2,2,96,256]{3,2,1,0:T(8,128)(2,1)S(1)}, u32[]{:S(2)}, u32[]{:S(2)}) %all-to-all-start) | async-done | bytes 196640 | tf_op jit(solution)/shard_map/all_to_all | solution.py:207
  18.1 2.1 %collective-permute-start = (bf16[192,3072]{1,0:T(8,128)(2,1)S(1)}, bf16[192,3072]{1,0:T(8,128)(2,1)S(1)}, u32[]{:S(2)}, u32[]{:S(2)}) collective-permute-start(bf16[192,3072]{1,0:T(8,128)(2,1)S(1)} %pad_maximum_fusion), channel_id=1, source_target_pairs={{0,1},{1,0},{2,3},{3,2},{4,5},{5,4},{6,7},{7,6},{8,9},{9,8},{10,11... | collective-permute-start | bytes 3538952 | tf_op jit(solution)/shard_map/ppermute | solution.py:219
  20.3 39.7 %all_gather.3.refs_0_.refs_7_ = bf16[1536,256]{1,0:T(8,128)(2,1)S(1)} all-gather(bf16[384,256]{1,0:T(8,128)(2,1)S(1)} %bitcast.26), channel_id=1, replica_groups=mesh['xh'=2,'y'=4,'core'=2,'zh'=4,'zl'=4,'xl'=2] {'zh'}, dimensions={0}, use_global_device_ids=true | all-gather | bytes 983040 | tf_op jit(solution)/shard_map/all_gather | solution.py:220
  59.9 1.9 collective-permute-start.5
  61.9 4.8 %collective-permute-start.1 = (bf16[1536,256]{1,0:T(8,128)(2,1)S(1)}, bf16[1536,256]{1,0:T(8,128)(2,1)}, u32[]{:S(2)}, u32[]{:S(2)}) collective-permute-start(bf16[1536,256]{1,0:T(8,128)(2,1)S(1)} %all_gather.3.refs_0_.refs_7_), channel_id=1, source_target_pairs={{0,30},{2,0},{4,2},{6,4},{8,6},{10,8},{12,10},{14,12},{16,14},{18,... | collective-permute-start | bytes 2359304 | tf_op jit(solution)/shard_map/ppermute | solution.py:184
  66.6 1.9 collective-permute-start.2
  68.6 1.0 fusion
  69.5 2.3 %collective-permute-start.3 = (bf16[768,256]{1,0:T(8,128)(2,1)}, bf16[768,256]{1,0:T(8,128)(2,1)S(1)}, u32[]{:S(2)}, u32[]{:S(2)}) collective-permute-start(bf16[768,256]{1,0:T(8,128)(2,1)} %get-tuple-element.32), channel_id=1, source_target_pairs={{0,4},{2,6},{4,8},{6,10},{8,12},{10,14},{12,16},{14,18},{16,20},{1... | collective-permute-start | bytes 1179656 | tf_op jit(solution)/shard_map/ppermute | solution.py:184
  71.8 5.7 %collective-permute-start.4 = (bf16[768,256]{1,0:T(8,128)(2,1)}, bf16[768,256]{1,0:T(8,128)(2,1)}, u32[]{:S(2)}, u32[]{:S(2)}) collective-permute-start(bf16[768,256]{1,0:T(8,128)(2,1)} %get-tuple-element.31), channel_id=1, source_target_pairs={{0,28},{2,30},{4,0},{6,2},{8,4},{10,6},{12,8},{14,10},{16,12},{18,... | collective-permute-start | bytes 1179656 | tf_op jit(solution)/shard_map/ppermute | solution.py:184
  78.1 20.6 %collective-permute-done.3.refs_3_.refs_10_ = bf16[768,256]{1,0:T(8,128)(2,1)S(1)} collective-permute-done((bf16[768,256]{1,0:T(8,128)(2,1)}, bf16[768,256]{1,0:T(8,128)(2,1)S(1)}, u32[]{:S(2)}, u32[]{:S(2)}) %collective-permute-start.3) | collective-permute-done | bytes 393248 | tf_op jit(solution)/shard_map/ppermute | solution.py:184
  98.7 2.3 %collective-permute-done.4.refs_4_.refs_11_ = bf16[768,256]{1,0:T(8,128)(2,1)} collective-permute-done((bf16[768,256]{1,0:T(8,128)(2,1)}, bf16[768,256]{1,0:T(8,128)(2,1)}, u32[]{:S(2)}, u32[]{:S(2)}) %collective-permute-start.4) | collective-permute-done | bytes 393248 | tf_op jit(solution)/shard_map/ppermute | solution.py:184
  101.1 1.1 copy-done.2
  102.2 9.1 %forward.1 = (bf16[3072,256]{1,0:T(8,128)(2,1)}, f32[2,256,256]{2,1,0:T(8,128)}, f32[2,96,256]{2,1,0:T(8,128)}, f32[2,96,256]{2,1,0:T(8,128)}, f32[2,8,256]{2,1,...) custom-call(s32[7]{0:T(128)} %stack.40.place, ...), custom_call_target="tpu_custom_call" | custom-call | flops 2000000000 | bytes 14000000 | tf_op jit(solution)/shard_map/forward/pallas_call | solution.py:245
  111.3 10.2 %backward.1 = bf16[2,2,8,192,384]{4,3,2,1,0:T(8,128)(2,1)} custom-call(s32[7]{0:T(128)} %stack.40.place, bf16[3072,256]{1,0:T(8,128)(2,1)} %get-tuple-element.22.refs_0_, f32[2,256,256]{2,1,0:T(8,128)} %get-tuple-element.23.refs_1_, f32[2,96,256]{2,1,0:T(8,128)} %get-tuple-element.24.refs_2_, f32[2,96,256]{2,1,0:T(8,128)} %get-tuple-element.25.refs_3_, ...), custom_call_target="tpu_custom_call" | custom-call | flops 1000000 | bytes 100000 | tf_op jit(solution)/shard_map/backward/pallas_call | solution.py:268
  121.6 12.7 %all_to_all.20 = bf16[2,2,8,192,384]{4,3,2,1,0:T(8,128)(2,1)} all-to-all(bf16[2,2,8,192,384]{4,3,2,1,0:T(8,128)(2,1)} %backward.1), channel_id=1, replica_groups=mesh['xh'=2,'y'=4,'core'=2,'zh'=4,'zl'=4,'xl'=2] {'core'}, dimensions={0} | all-to-all | bytes 9437184 | tf_op jit(solution)/shard_map/all_to_all | solution.py:285
  134.3 3.5 %reduce_sum.24 = bf16[2,8,192,384]{3,2,1,0:T(8,128)(2,1)S(1)} reduce(bf16[2,2,8,192,384]{4,3,2,1,0:T(8,128)(2,1)} %all_to_all.20, bf16[]{:T(256)} %constant.50.clone.1), dimensions={0}, to_apply=%region_1.2 | reduce | flops 1179648 | bytes 7077890 | tf_op jit(solution)/shard_map/reduce_sum | solution.py:286
  137.8 37.0 %all_to_all.21 = bf16[16,192,384]{2,1,0:T(8,128)(2,1)} all-to-all(bf16[16,192,384]{2,1,0:T(8,128)(2,1)S(1)} %bitcast.22), channel_id=1, replica_groups=mesh['xh'=2,'y'=4,'core'=2,'zh'=4,'zl'=4,'xl'=2] {'xl','xh','y'}, dimensions={0} | all-to-all | bytes 4718592 | tf_op jit(solution)/shard_map/all_to_all | solution.py:287
  174.9 10.2 %reduce-scatter.2.cloned.1.call-done = bf16[192,256]{1,0:T(8,128)(2,1)} async-done(((bf16[3072,256]{1,0:T(8,128)(2,1)}), bf16[192,256]{1,0:T(8,128)(2,1)}) %reduce-scatter.2.cloned.1.call-update) | async-done | bytes 98320 | tf_op jit(solution)/shard_map/reduce_scatter | solution.py:265
  185.1 3.3 %all-to-all-start.3 = ((bf16[2,96,256]{2,1,0:T(8,128)(2,1)}), bf16[2,96,256]{2,1,0:T(8,128)(2,1)S(1)}, u32[]{:S(2)}, u32[]{:S(2)}) async-start(bf16[2,96,256]{2,1,0:T(8,128)(2,1)} %bitcast.29), calls=%async_computation.4 | async-start | bytes 196608 | tf_op jit(solution)/shard_map/all_to_all | solution.py:292
  188.4 2.0 reduce_sum.25
  191.1 1.6 all-to-all-done.3
  (26 shorter events, 3.9 us)
Async XLA Ops:
  7.2 7.2 %copy-start.3 = (bf16[3072,288]{0,1:T(8,128)(2,1)S(1)}, bf16[3072,288]{0,1:T(8,128)(2,1)}, u32[]{:S(2)}) copy-start(bf16[3072,288]{0,1:T(8,128)(2,1)} %param.5) | copy-start | bytes 5308420
  9.9 8.2 %all-to-all-start = ((bf16[2,2,96,256]{3,2,1,0:T(8,128)(2,1)}), bf16[2,2,96,256]{3,2,1,0:T(8,128)(2,1)S(1)}, u32[]{:S(2)}, u32[]{:S(2)}) async-start(bf16[2,2,96,256]{3,2,1,0:T(8,128)(2,1)} %maximum_bitcast_fusion), calls=%async_computation | async-start | bytes 393216 | tf_op jit(solution)/shard_map/all_to_all | solution.py:207
  13.3 171.8 %reduce-scatter.2.cloned.1.call-start = ((), (), s32[]{:S(2)}) async-start(), calls=%async_computation.5 | async-start | bytes 1671168 | tf_op jit(solution)/shard_map/reduce_scatter | solution.py:265
  18.1 41.8 %collective-permute-start = (bf16[192,3072]{1,0:T(8,128)(2,1)S(1)}, bf16[192,3072]{1,0:T(8,128)(2,1)S(1)}, u32[]{:S(2)}, u32[]{:S(2)}) collective-permute-start(bf16[192,3072]{1,0:T(8,128)(2,1)S(1)} %pad_maximum_fusion), channel_id=1, source_target_pairs={{0,1},{1,0},{2,3},{3,2},{4,5},{5,4},{6,7},{7,6},{8,9},{9,8},{10,11... | collective-permute-start | bytes 3538952 | tf_op jit(solution)/shard_map/ppermute | solution.py:219
  59.9 41.1 %copy-start = (bf16[1536,256]{1,0:T(8,128)(2,1)}, bf16[1536,256]{1,0:T(8,128)(2,1)S(1)}, u32[]{:S(2)}) copy-start(bf16[1536,256]{1,0:T(8,128)(2,1)S(1)} %all_gather.3.refs_0_.refs_7_) | copy-start | bytes 2359300
  59.9 41.1 %copy-start.1 = (bf16[192,3072]{1,0:T(8,128)(2,1)}, bf16[192,3072]{1,0:T(8,128)(2,1)S(1)}, u32[]{:S(2)}) copy-start(bf16[192,3072]{1,0:T(8,128)(2,1)S(1)} %collective-permute-done.refs_7_.refs_13_) | copy-start | bytes 3538948
  59.9 41.1 %collective-permute-start.5 = (bf16[192,3072]{1,0:T(8,128)(2,1)S(1)}, bf16[192,3072]{1,0:T(8,128)(2,1)S(1)}, u32[]{:S(2)}, u32[]{:S(2)}) collective-permute-start(bf16[192,3072]{1,0:T(8,128)(2,1)S(1)} %collective-permute-done.refs_7_.refs_13_), channel_id=1, source_target_pairs={{0,32},{32,0},{1,33},{33,1},{2,34},{34,2},{3,35},{35,3},{4,36},{36... | collective-permute-start | bytes 3538952 | tf_op jit(solution)/shard_map/ppermute | solution.py:222
  61.9 39.2 %collective-permute-start.1 = (bf16[1536,256]{1,0:T(8,128)(2,1)S(1)}, bf16[1536,256]{1,0:T(8,128)(2,1)}, u32[]{:S(2)}, u32[]{:S(2)}) collective-permute-start(bf16[1536,256]{1,0:T(8,128)(2,1)S(1)} %all_gather.3.refs_0_.refs_7_), channel_id=1, source_target_pairs={{0,30},{2,0},{4,2},{6,4},{8,6},{10,8},{12,10},{14,12},{16,14},{18,... | collective-permute-start | bytes 2359304 | tf_op jit(solution)/shard_map/ppermute | solution.py:184
  66.6 34.4 %collective-permute-start.2 = (bf16[1536,256]{1,0:T(8,128)(2,1)S(1)}, bf16[1536,256]{1,0:T(8,128)(2,1)}, u32[]{:S(2)}, u32[]{:S(2)}) collective-permute-start(bf16[1536,256]{1,0:T(8,128)(2,1)S(1)} %all_gather.3.refs_0_.refs_7_), channel_id=1, source_target_pairs={{0,2},{2,4},{4,6},{6,8},{8,10},{10,12},{12,14},{14,16},{16,18},{18... | collective-permute-start | bytes 2359304 | tf_op jit(solution)/shard_map/ppermute | solution.py:184
  69.5 29.2 %collective-permute-start.3 = (bf16[768,256]{1,0:T(8,128)(2,1)}, bf16[768,256]{1,0:T(8,128)(2,1)S(1)}, u32[]{:S(2)}, u32[]{:S(2)}) collective-permute-start(bf16[768,256]{1,0:T(8,128)(2,1)} %get-tuple-element.32), channel_id=1, source_target_pairs={{0,4},{2,6},{4,8},{6,10},{8,12},{10,14},{12,16},{14,18},{16,20},{1... | collective-permute-start | bytes 1179656 | tf_op jit(solution)/shard_map/ppermute | solution.py:184
  71.8 29.2 %collective-permute-start.4 = (bf16[768,256]{1,0:T(8,128)(2,1)}, bf16[768,256]{1,0:T(8,128)(2,1)}, u32[]{:S(2)}, u32[]{:S(2)}) collective-permute-start(bf16[768,256]{1,0:T(8,128)(2,1)} %get-tuple-element.31), channel_id=1, source_target_pairs={{0,28},{2,30},{4,0},{6,2},{8,4},{10,6},{12,8},{14,10},{16,12},{18,... | collective-permute-start | bytes 1179656 | tf_op jit(solution)/shard_map/ppermute | solution.py:184
  98.7 2.3 %copy-start.4 = (bf16[768,256]{1,0:T(8,128)(2,1)}, bf16[768,256]{1,0:T(8,128)(2,1)S(1)}, u32[]{:S(2)}) copy-start(bf16[768,256]{1,0:T(8,128)(2,1)S(1)} %collective-permute-done.3.refs_3_.refs_10_) | copy-start | bytes 1179652
  101.1 1.1 copy-start.2
  185.1 7.6 %all-to-all-start.3 = ((bf16[2,96,256]{2,1,0:T(8,128)(2,1)}), bf16[2,96,256]{2,1,0:T(8,128)(2,1)S(1)}, u32[]{:S(2)}, u32[]{:S(2)}) async-start(bf16[2,96,256]{2,1,0:T(8,128)(2,1)} %bitcast.29), calls=%async_computation.4 | async-start | bytes 196608 | tf_op jit(solution)/shard_map/all_to_all | solution.py:292
  190.4 2.9 %copy-start.5 = (bf16[192,384]{1,0:T(8,128)(2,1)}, bf16[192,384]{1,0:T(8,128)(2,1)S(1)}, u32[]{:S(2)}) copy-start(bf16[192,384]{1,0:T(8,128)(2,1)S(1)} %reduce_sum.25) | copy-start | bytes 442372
Sparse Core Ops, SparseCore 0:
  111.5 73.5 reduce-scatter.1

commit v7 on v4

--- a/solution.py
+++ b/solution.py
@@ -9,7 +9,6 @@
 from jax.sharding import PartitionSpec as P
 
 PATCHES = 256
-GROUP = 4
 epsilon = 1e-06
 highest = lax.Precision.HIGHEST
 low = jnp.bfloat16
@@ -35,9 +34,6 @@
 
 def aligned(start, size):
     return pl.ds(pl.multiple_of(start, 16), size)
-
-
-SETS = ((0, 0, 4), (1, 0, 4), (2, 0, 4), (3, 0, 2), (3, 2, 2))
 
 
 def start_all(pairs, sems, first=0):
@@ -67,10 +63,9 @@
     kept, sems = refs[17:24], refs[24]
     normed, attention, query, key, inverses, value, heads = kept
     features = normed.shape[0]
-    block = features // (4 * GROUP)
-    core = place[4]
+    core = place[0]
     thirds, quarter = 3 * head // 2, head // 2
-    rows_in = start_all([(gathered, raw)], sems)
+    rows_in = start_all([(gathered.at[:, 0], raw)], sems)
     weights_in = [(qkv_own, qkv.at[0]), (out_own, out.at[0])]
     for source, at in partner_pieces(mine, theirs, core, 0, thirds):
         weights_in.append((source, qkv.at[1, at]))
@@ -79,18 +74,20 @@
     weights_in = start_all(weights_in, sems, 1)
     wait_all(rows_in)
 
+    blocks, part, _ = raw.shape
+
     def rows_of(n):
-        return raw[block * n : block * (n + 1), :].astype(wide)
+        return raw[n].astype(wide)
 
     def fold(rows):
-        return jnp.sum(rows.reshape(block // 8, 8, PATCHES), 0)
-
-    blocks = range(4 * GROUP)
+        return jnp.sum(rows.reshape(part // 8, 8, PATCHES), 0)
+
+    blocks = range(blocks)
     mean = jnp.sum(sum(fold(rows_of(n)) for n in blocks), 0, keepdims=True) / features
     variance = sum(fold((rows_of(n) - mean) * (rows_of(n) - mean)) for n in blocks)
     scale = lax.rsqrt(jnp.sum(variance, 0, keepdims=True) / features + epsilon)
     for n in blocks:
-        normed[block * n : block * (n + 1), :] = ((rows_of(n) - mean) * scale).astype(low)
+        normed[part * n : part * (n + 1), :] = ((rows_of(n) - mean) * scale).astype(low)
     results_out = start_all([(normed, results[0])], sems, 7)
     wait_all(weights_in)
     for slot in range(2):
@@ -120,26 +117,22 @@
 
 
 def backward_kernel(head, place, *refs):
-    results, sets, (out_own, mine, theirs) = refs[:7], refs[7:12], refs[12:15]
-    shares, cotangent, out = refs[15:18]
-    kept, sems = refs[18:25], refs[25]
+    results, gathered, out_own, mine, theirs = refs[:7], refs[7], refs[8], refs[9], refs[10]
+    shares, cotangent, out = refs[11:14]
+    kept, sems = refs[14:21], refs[21]
     normed, attention, query, key, inverses, value, heads = kept
-    core = place[4]
+    core = place[0]
     thirds, quarter = 3 * head // 2, head // 2
-    block = cotangent.shape[0] // (4 * GROUP)
-    first_in = [(out_own, out.at[0])]
-    for ref, (which, first, count) in zip(sets, SETS):
-        for n in range(count):
-            at = aligned((GROUP * (first + n) + place[which]) * block, block)
-            first_in.append((ref.at[pl.ds(block * n, block)], cotangent.at[at]))
+    first_in = [(gathered.at[:, 1], cotangent), (out_own, out.at[0])]
     for source, at in partner_pieces(mine, theirs, core, thirds, quarter):
         first_in.append((source, out.at[1, at]))
     first_in = start_all(first_in, sems)
-    kept_in = start_all(list(zip(results[1:], kept[1:])) + [(results[0], normed)], sems, 19)
+    kept_in = start_all(list(zip(results[1:], kept[1:])) + [(results[0], normed)], sems, 4)
     wait_all(first_in)
     scaling = head ** (-0.5)
     cores, _, chips, rows, columns = shares.shape
-    grads = [contract(out[slot], cotangent[...], 1, 0).astype(low) for slot in range(2)]
+    cotangent = cotangent[...].reshape(normed.shape)
+    grads = [contract(out[slot], cotangent, 1, 0).astype(low) for slot in range(2)]
     wait_all(kept_in[:-1])
     rights = []
     for slot, grad in enumerate(grads):
@@ -166,7 +159,7 @@
         rights.append((grad_proj[:256], tail, lead))
     wait_all(kept_in[-1:])
     for slot, (main_right, tail, lead) in enumerate(rights):
-        there = place[5 + slot]
+        there = place[1 + slot]
         for owner in range(cores):
             for chip in range(chips):
                 at = slice((2 * chip + owner) * rows, (2 * chip + owner + 1) * rows)
@@ -177,34 +170,20 @@
                 ).astype(low)
 
 
-def shift(values, by):
-    size = lax.axis_size(Z)
-    return lax.ppermute(values, Z, [(i, (i + by) % size) for i in range(size)])
-
-
 def on_device(activations, w_qkv, w_out, d_branch):
     part, tokens = activations.shape
     features, head = w_out.shape
     images = tokens // PATCHES
     zh, xl, xh, y, core = (lax.axis_size(a) for a in ("zh", "xl", "xh", "y", "core"))
     swap = [(0, 1), (1, 0)]
-    core_at, xl_at, residue = (lax.axis_index(a) for a in ("core", "xl", "zl"))
-    place = jnp.stack(
-        [
-            residue,
-            (residue + 1) % GROUP,
-            (residue + 3) % GROUP,
-            (residue + 2) % GROUP,
-            core_at,
-            xl_at,
-            1 - xl_at,
-        ]
-    ).astype(jnp.int32)
-
-    def by_image(values):
-        return values.reshape(part, images, PATCHES).transpose(1, 0, 2)
-
-    mixed = lax.all_to_all(by_image(activations), "xl", 0, 0, tiled=True)
+    core_at, xl_at = lax.axis_index("core"), lax.axis_index("xl")
+    place = jnp.stack([core_at, xl_at, 1 - xl_at]).astype(jnp.int32)
+
+    cut = [slice(n * PATCHES, (n + 1) * PATCHES) for n in range(images)]
+    both = jnp.concatenate([v[:, c] for c in cut for v in (activations, d_branch)], 0)
+    mixed = lax.all_to_all(both.reshape(images, 2 * part, PATCHES), "xl", 0, 0, tiled=True)
+    gathered = lax.all_gather(mixed.reshape(xl * 2 * part, PATCHES), Z, axis=0, tiled=True)
+    gathered = gathered.reshape(features // part, 2, part, PATCHES)
 
     qkv_own, out_own = w_qkv.T, w_out.T
     thirds, quarter = 3 * head // 2, head // 2
@@ -215,24 +194,9 @@
         ],
         0,
     )
-    mine, d_branch, mixed = lax.optimization_barrier((mine, d_branch, mixed))
-    gathered = lax.all_gather(mixed.reshape(xl * part, PATCHES), Z, axis=0, tiled=True)
+    mine, mixed = lax.optimization_barrier((mine, mixed))
     mine = lax.ppermute(mine, "xl", swap)
-    copies = jnp.broadcast_to(by_image(d_branch)[None], (zh, images, part, PATCHES))
-    same = lax.all_to_all(
-        copies.reshape(zh * images, part, PATCHES), ("zh", "xl"), 0, 0, tiled=True
-    ).reshape(zh * xl * part, PATCHES)
-    middle = zh * xl * part // 2
-    mine, same = lax.optimization_barrier((mine, same))
     theirs = lax.ppermute(mine, "core", swap)
-    sets = (
-        same,
-        shift(same, -1),
-        shift(same, 1),
-        shift(same[:middle], 2),
-        shift(same[middle:], -2),
-    )
-    gathered, _ = lax.optimization_barrier((gathered, same))
 
     shape = jax.ShapeDtypeStruct
     vmem = pl.BlockSpec(memory_space=pltpu.VMEM)
@@ -253,14 +217,14 @@
         in_specs=[smem] + [hbm] * 5,
         out_specs=[hbm] * 8,
         scratch_shapes=[
-            pltpu.VMEM((features, PATCHES), low),
+            pltpu.VMEM((features // part, part, PATCHES), low),
             pltpu.VMEM((2, 3 * head, features), low),
             pltpu.VMEM((2, head, features), low),
             pltpu.VMEM((features, PATCHES), low),
         ]
         + [pltpu.VMEM(k.shape, k.dtype) for k in kept]
         + [pltpu.SemaphoreType.DMA((18,))],
-        compiler_params=pltpu.CompilerParams(vmem_limit_bytes=40 << 20),
+        compiler_params=pltpu.CompilerParams(vmem_limit_bytes=60 << 20),
         cost_estimate=pl.CostEstimate(
             flops=2_000_000_000, bytes_accessed=14_000_000, transcendentals=131072
         ),
@@ -273,20 +237,20 @@
     shares = pl.pallas_call(
         functools.partial(backward_kernel, head),
         out_shape=shape((core, xl, xh * y, rows, columns), low),
-        in_specs=[smem] + [hbm] * 15,
+        in_specs=[smem] + [hbm] * 11,
         out_specs=vmem,
         scratch_shapes=[
-            pltpu.VMEM((features, PATCHES), low),
+            pltpu.VMEM((features // part, part, PATCHES), low),
             pltpu.VMEM((2, head, features), low),
         ]
         + [pltpu.VMEM(k.shape, k.dtype) for k in kept]
-        + [pltpu.SemaphoreType.DMA((26,))],
-        compiler_params=pltpu.CompilerParams(vmem_limit_bytes=40 << 20),
+        + [pltpu.SemaphoreType.DMA((11,))],
+        compiler_params=pltpu.CompilerParams(vmem_limit_bytes=60 << 20),
         cost_estimate=pl.CostEstimate(
             flops=1_000_000, bytes_accessed=100_000, transcendentals=0
         ),
         name="backward",
-    )(place, *kept, *sets, out_own, mine, theirs)
+    )(place, *kept, gathered, out_own, mine, theirs)
     pairs = lax.all_to_all(shares, "core", 0, 0, tiled=True)
     pair_sum = jnp.sum(pairs.astype(wide), 0).astype(low)
     grads = lax.all_to_all(

time: 216 us -> 190 us (0.88)
  the two profiles are of different devices: /device:TPU:32 before, /device:TPU:12 now
where the time goes in v7:
time: 190 us
  waiting for transfers between devices  84 us (44%)
  blocking collectives  55.8 us (29%)
  Pallas kernels  18.5 us (10%)
  between operations  14.2 us (7%)
  starting transfers between devices  7.45 us (4%)
  other arithmetic  6.27 us (3%)
  local copies, waits for them, and re-layouts  3.43 us (2%)
    all_gather x1, waiting for transfers between devices, on_device(): lax.all_gather(mixed.reshape(xl * 2 * part, PATCHES), Z, axis=0, tiled=True)  46.5 us
    all_to_all x1, blocking collectives, on_device(): lax.all_to_all(pair_sum.reshape(xl * xh * y, rows, columns), ('xl', 'xh',...  35.1 us
    ppermute x1, waiting for transfers between devices, on_device(): mine = lax.ppermute(mine, 'xl', swap)  26.3 us
    all_to_all x1, blocking collectives, on_device(): pairs = lax.all_to_all(shares, 'core', 0, 0, tiled=True)  12.7 us
    pallas_call x1, Pallas kernels, on_device(): pl.pallas_call(functools.partial(backward_kernel, head), out_shape=shape(...  9.81 us
    pallas_call x1, Pallas kernels, on_device(): pl.pallas_call(functools.partial(forward_kernel, head), out_shape=kept +...  8.71 us
    all_to_all x1, blocking collectives, on_device(): lax.all_to_all(both.reshape(images, 2 * part, PATCHES), 'xl', 0, 0, tiled...  7.89 us
    reduce_scatter x1, waiting for transfers between devices, on_device(): summed = lax.psum_scatter(branch, Z, scatter_dimension=0, tiled=True)  7.45 us
  transfers between devices with their start and end apart: 5, of which 5 were waited for; matrix products, arithmetic and copies ran while one was open for 4% of the time, Pallas kernels for 5%

profile of v7, /device:TPU:12, one launch (start us, length us, event | category | flops | bytes accessed | tf_op | source)
XLA Modules:
  0.0 189.6 jit_solution(9683739204895091732)
XLA Ops:
  7.2 0.0 all-gather.2.cloned.1.call-start
  7.2 1.0 fusion
  8.3 7.9 %all_to_all.20 = bf16[2,192,256]{2,1,0:T(8,128)(2,1)} all-to-all(bf16[2,192,256]{2,1,0:T(8,128)(2,1)S(1)} %bitcast.25), channel_id=1, replica_groups=mesh['xh'=2,'y'=4,'core'=2,'zh'=4,'zl'=4,'xl'=2] {'xl'}, dimensions={0} | all-to-all | bytes 393216 | tf_op jit(solution)/shard_map/all_to_all | solution.py:184
  16.2 0.0 reduce-scatter.2.cloned.1.call-start
  16.2 1.0 dynamic-slice_bitcast_fusion.1
  17.2 0.1 dynamic-slice_bitcast_fusion
  17.3 0.1 pad_maximum_fusion
  17.4 2.1 %collective-permute-start = (bf16[192,3072]{1,0:T(8,128)(2,1)S(1)}, bf16[192,3072]{1,0:T(8,128)(2,1)S(1)}, u32[]{:S(2)}, u32[]{:S(2)}) collective-permute-start(bf16[192,3072]{1,0:T(8,128)(2,1)S(1)} %pad_maximum_fusion), channel_id=1, source_target_pairs={{0,1},{1,0},{2,3},{3,2},{4,5},{5,4},{6,7},{7,6},{8,9},{9,8},{10,11... | collective-permute-start | bytes 3538952 | tf_op jit(solution)/shard_map/ppermute | solution.py:198
  19.5 26.3 %collective-permute-done.refs_3_.refs_9_ = bf16[192,3072]{1,0:T(8,128)(2,1)S(1)} collective-permute-done((bf16[192,3072]{1,0:T(8,128)(2,1)S(1)}, bf16[192,3072]{1,0:T(8,128)(2,1)S(1)}, u32[]{:S(2)}, u32[]{:S(2)}) %collective-permute-start) | collective-permute-done | bytes 1179680 | tf_op jit(solution)/shard_map/ppermute | solution.py:198
  45.8 1.9 %collective-permute-start.1 = (bf16[192,3072]{1,0:T(8,128)(2,1)S(1)}, bf16[192,3072]{1,0:T(8,128)(2,1)S(1)}, u32[]{:S(2)}, u32[]{:S(2)}) collective-permute-start(bf16[192,3072]{1,0:T(8,128)(2,1)S(1)} %collective-permute-done.refs_3_.refs_9_), channel_id=1, source_target_pairs={{0,32},{32,0},{1,33},{33,1},{2,34},{34,2},{3,35},{35,3},{4,36},{36... | collective-permute-start | bytes 3538952 | tf_op jit(solution)/shard_map/ppermute | solution.py:199
  47.8 0.7 pad_add_fusion.place
  48.4 2.2 %collective-permute-done.1.refs_4_.refs_10_ = bf16[192,3072]{1,0:T(8,128)(2,1)S(1)} collective-permute-done((bf16[192,3072]{1,0:T(8,128)(2,1)S(1)}, bf16[192,3072]{1,0:T(8,128)(2,1)S(1)}, u32[]{:S(2)}, u32[]{:S(2)}) %collective-permute-start.1) | collective-permute-done | bytes 1179680 | tf_op jit(solution)/shard_map/ppermute | solution.py:199
  50.6 46.5 %all-gather.2.cloned.1.call-done = bf16[6144,256]{1,0:T(8,128)(2,1)} async-done(((bf16[384,256]{1,0:T(8,128)(2,1)}), bf16[6144,256]{1,0:T(8,128)(2,1)}) %all-gather.2.cloned.1.call-update) | async-done | bytes 3145744 | tf_op jit(solution)/shard_map/all_gather | solution.py:185
  97.1 8.7 %forward.1 = (bf16[3072,256]{1,0:T(8,128)(2,1)}, f32[2,256,256]{2,1,0:T(8,128)}, f32[2,96,256]{2,1,0:T(8,128)}, f32[2,96,256]{2,1,0:T(8,128)}, f32[2,8,256]{2,1,...) custom-call(s32[3]{0:T(128)} %pad_add_fusion.place, ...), custom_call_target="tpu_custom_call" | custom-call | flops 2000000000 | bytes 14000000 | tf_op jit(solution)/shard_map/forward/pallas_call | solution.py:214
  105.8 9.8 %backward.1 = bf16[2,2,8,192,384]{4,3,2,1,0:T(8,128)(2,1)} custom-call(s32[3]{0:T(128)} %pad_add_fusion.place, bf16[3072,256]{1,0:T(8,128)(2,1)} %get-tuple-element.16.refs_0_, f32[2,256,256]{2,1,0:T(8,128)} %get-tuple-element.17.refs_1_, f32[2,96,256]{2,1,0:T(8,128)} %get-tuple-element.18.refs_2_, f32[2,96,256]{2,1,0:T(8,128)} %get-tuple-element.19.refs_3_, ...), custom_call_target="tpu_custom_call" | custom-call | flops 1000000 | bytes 100000 | tf_op jit(solution)/shard_map/backward/pallas_call | solution.py:237
  115.6 12.7 %all_to_all.21 = bf16[2,2,8,192,384]{4,3,2,1,0:T(8,128)(2,1)} all-to-all(bf16[2,2,8,192,384]{4,3,2,1,0:T(8,128)(2,1)} %backward.1), channel_id=1, replica_groups=mesh['xh'=2,'y'=4,'core'=2,'zh'=4,'zl'=4,'xl'=2] {'core'}, dimensions={0} | all-to-all | bytes 9437184 | tf_op jit(solution)/shard_map/all_to_all | solution.py:254
  128.4 3.5 %reduce_sum.24 = bf16[2,8,192,384]{3,2,1,0:T(8,128)(2,1)S(1)} reduce(bf16[2,2,8,192,384]{4,3,2,1,0:T(8,128)(2,1)} %all_to_all.21, bf16[]{:T(256)} %constant.23.clone.1), dimensions={0}, to_apply=%region_1.0 | reduce | flops 1179648 | bytes 7077890 | tf_op jit(solution)/shard_map/reduce_sum | solution.py:255
  131.9 35.1 %all_to_all.22 = bf16[16,192,384]{2,1,0:T(8,128)(2,1)} all-to-all(bf16[16,192,384]{2,1,0:T(8,128)(2,1)S(1)} %bitcast.20), channel_id=1, replica_groups=mesh['xh'=2,'y'=4,'core'=2,'zh'=4,'zl'=4,'xl'=2] {'xl','xh','y'}, dimensions={0} | all-to-all | bytes 4718592 | tf_op jit(solution)/shard_map/all_to_all | solution.py:256
  167.0 7.4 %reduce-scatter.2.cloned.1.call-done = bf16[192,256]{1,0:T(8,128)(2,1)} async-done(((bf16[3072,256]{1,0:T(8,128)(2,1)}), bf16[192,256]{1,0:T(8,128)(2,1)}) %reduce-scatter.2.cloned.1.call-update) | async-done | bytes 98320 | tf_op jit(solution)/shard_map/reduce_scatter | solution.py:234
  174.5 3.3 %all-to-all-start.3 = ((bf16[2,96,256]{2,1,0:T(8,128)(2,1)}), bf16[2,96,256]{2,1,0:T(8,128)(2,1)S(1)}, u32[]{:S(2)}, u32[]{:S(2)}) async-start(bf16[2,96,256]{2,1,0:T(8,128)(2,1)} %bitcast.28), calls=%async_computation.4 | async-start | bytes 196608 | tf_op jit(solution)/shard_map/all_to_all | solution.py:261
  177.8 2.0 %reduce_sum.25 = bf16[192,384]{1,0:T(8,128)(2,1)S(1)} reduce(bf16[16,192,384]{2,1,0:T(8,128)(2,1)} %all_to_all.22, bf16[]{:T(256)} %constant.23.clone.1), dimensions={0}, to_apply=%region_2.0 | reduce | flops 1105920 | bytes 2506754 | tf_op jit(solution)/shard_map/reduce_sum | solution.py:260
  179.8 0.7 slice.25
  180.5 1.6 all-to-all-done.3
  182.1 0.6 copy.8
  (11 shorter events, 0.1 us)
Async XLA Ops:
  7.2 10.0 %copy-start.2 = (bf16[3072,288]{0,1:T(8,128)(2,1)S(1)}, bf16[3072,288]{0,1:T(8,128)(2,1)}, u32[]{:S(2)}) copy-start(bf16[3072,288]{0,1:T(8,128)(2,1)} %param.5) | copy-start | bytes 5308420
  7.2 89.9 %all-gather.2.cloned.1.call-start = ((), (), s32[]{:S(2)}) async-start(), calls=%async_computation.5 | async-start | bytes 3342336 | tf_op jit(solution)/shard_map/all_gather | solution.py:185
  16.2 158.3 %reduce-scatter.2.cloned.1.call-start = ((), (), s32[]{:S(2)}) async-start(), calls=%async_computation.6 | async-start | bytes 1671168 | tf_op jit(solution)/shard_map/reduce_scatter | solution.py:234
  17.4 28.5 %collective-permute-start = (bf16[192,3072]{1,0:T(8,128)(2,1)S(1)}, bf16[192,3072]{1,0:T(8,128)(2,1)S(1)}, u32[]{:S(2)}, u32[]{:S(2)}) collective-permute-start(bf16[192,3072]{1,0:T(8,128)(2,1)S(1)} %pad_maximum_fusion), channel_id=1, source_target_pairs={{0,1},{1,0},{2,3},{3,2},{4,5},{5,4},{6,7},{7,6},{8,9},{9,8},{10,11... | collective-permute-start | bytes 3538952 | tf_op jit(solution)/shard_map/ppermute | solution.py:198
  45.8 51.3 %copy-start = (bf16[192,3072]{1,0:T(8,128)(2,1)}, bf16[192,3072]{1,0:T(8,128)(2,1)S(1)}, u32[]{:S(2)}) copy-start(bf16[192,3072]{1,0:T(8,128)(2,1)S(1)} %collective-permute-done.refs_3_.refs_9_) | copy-start | bytes 3538948
  45.8 4.7 %collective-permute-start.1 = (bf16[192,3072]{1,0:T(8,128)(2,1)S(1)}, bf16[192,3072]{1,0:T(8,128)(2,1)S(1)}, u32[]{:S(2)}, u32[]{:S(2)}) collective-permute-start(bf16[192,3072]{1,0:T(8,128)(2,1)S(1)} %collective-permute-done.refs_3_.refs_9_), channel_id=1, source_target_pairs={{0,32},{32,0},{1,33},{33,1},{2,34},{34,2},{3,35},{35,3},{4,36},{36... | collective-permute-start | bytes 3538952 | tf_op jit(solution)/shard_map/ppermute | solution.py:199
  50.6 46.5 %copy-start.1 = (bf16[192,3072]{1,0:T(8,128)(2,1)}, bf16[192,3072]{1,0:T(8,128)(2,1)S(1)}, u32[]{:S(2)}) copy-start(bf16[192,3072]{1,0:T(8,128)(2,1)S(1)} %collective-permute-done.1.refs_4_.refs_10_) | copy-start | bytes 3538948
  174.5 7.6 %all-to-all-start.3 = ((bf16[2,96,256]{2,1,0:T(8,128)(2,1)}), bf16[2,96,256]{2,1,0:T(8,128)(2,1)S(1)}, u32[]{:S(2)}, u32[]{:S(2)}) async-start(bf16[2,96,256]{2,1,0:T(8,128)(2,1)} %bitcast.28), calls=%async_computation.4 | async-start | bytes 196608 | tf_op jit(solution)/shard_map/all_to_all | solution.py:261
  179.8 2.9 %copy-start.3 = (bf16[192,384]{1,0:T(8,128)(2,1)}, bf16[192,384]{1,0:T(8,128)(2,1)S(1)}, u32[]{:S(2)}) copy-start(bf16[192,384]{1,0:T(8,128)(2,1)S(1)} %reduce_sum.25) | copy-start | bytes 442372
Sparse Core Ops, SparseCore 0:
  16.3 80.7 all-gather.1
  106.0 68.4 reduce-scatter.1

commit v8 on v5

--- a/solution.py
+++ b/solution.py
@@ -201,8 +201,10 @@
         ]
     ).astype(jnp.int32)
 
-    stacked = jnp.stack([activations, d_branch]).reshape(2, part, images, PATCHES)
-    mixed = lax.all_to_all(stacked.transpose(2, 0, 1, 3), "xl", 0, 0, tiled=True)
+    cut = [slice(n * PATCHES, (n + 1) * PATCHES) for n in range(images)]
+    both = jnp.concatenate([v[:, c] for c in cut for v in (activations, d_branch)], 0)
+    both = both.reshape(images, 2, part, PATCHES)
+    mixed = lax.all_to_all(both, "xl", 0, 0, tiled=True)
 
     qkv_own, out_own = w_qkv.T, w_out.T
     thirds, quarter = 3 * head // 2, head // 2
@@ -217,8 +219,7 @@
     chunk = xl * part
     cotangent = lax.all_gather(mixed[:, 1].reshape(chunk, PATCHES), Z, axis=0, tiled=True)
     mine = lax.ppermute(mine, "xl", swap)
-    copies = jnp.broadcast_to(mixed[:, 0].reshape(1, chunk, PATCHES), (zh, chunk, PATCHES))
-    same = lax.all_to_all(copies, "zh", 0, 0, tiled=True).reshape(zh * chunk, PATCHES)
+    same = lax.all_gather(mixed[:, 0].reshape(chunk, PATCHES), "zh", axis=0, tiled=True)
     mine, same = lax.optimization_barrier((mine, same))
     theirs = lax.ppermute(mine, "core", swap)
     middle = zh * chunk // 2

time: 195 us -> 186 us (0.954)
  blocking collectives: 49.6 us -> 80.4 us
  waiting for transfers between devices: 56.5 us -> 33.2 us
  starting transfers between devices: 40.8 us -> 26.9 us
  local copies, waits for them, and re-layouts: 8.4 us -> 5.86 us
    all_gather x0 -> x1, blocking collectives: none -> 30.4 us  [on_device(): lax.all_gather(mixed[:, 0].reshape(chunk, PATCHES), 'zh', axis=0, tiled=T...]
    all_to_all x2 -> x1, waiting for transfers between devices: 24.1 us -> 3.59 us  [on_device(): mixed = lax.all_to_all(both, 'xl', 0, 0, tiled=True)]
    all_to_all x2 -> x1, starting transfers between devices: 18.5 us -> 3.43 us  [on_device(): mixed = lax.all_to_all(both, 'xl', 0, 0, tiled=True)]
    ppermute x1, waiting for transfers between devices: 5.33 us -> 0.01 us  [on_device(): mine = lax.ppermute(mine, 'xl', swap)]
    all_gather x1, waiting for transfers between devices: 0.02 us -> 2.92 us  [on_device(): lax.all_gather(mixed[:, 1].reshape(chunk, PATCHES), Z, axis=0, tiled=True)]
  transfers between devices with their start and end apart: 11 -> 10, of which waited for: 6 -> 5; matrix products, arithmetic and copies ran while one was open for 5% -> 4% of each run, Pallas kernels for 10% -> 10%
where the time goes in v8:
time: 186 us
  blocking collectives  80.4 us (43%)
  waiting for transfers between devices  33.2 us (18%)
  starting transfers between devices  26.9 us (14%)
  Pallas kernels  18.8 us (10%)
  between operations  14.3 us (8%)
  other arithmetic  6.27 us (3%)
  local copies, waits for them, and re-layouts  5.86 us (3%)
    all_to_all x1, blocking collectives, on_device(): lax.all_to_all(pair_sum.reshape(xl * xh * y, rows, columns), ('xl', 'xh',...  37.2 us
    all_gather x1, blocking collectives, on_device(): lax.all_gather(mixed[:, 0].reshape(chunk, PATCHES), 'zh', axis=0, tiled=T...  30.4 us
    ppermute x4, waiting for transfers between devices, shift(): return lax.ppermute(values, Z, [(i, (i + by) % size) for i in range(size)])  17 us
    ppermute x4, starting transfers between devices, shift(): return lax.ppermute(values, Z, [(i, (i + by) % size) for i in range(size)])  16 us
    all_to_all x1, blocking collectives, on_device(): pairs = lax.all_to_all(shares, 'core', 0, 0, tiled=True)  12.8 us
    pallas_call x1, Pallas kernels, on_device(): pl.pallas_call(functools.partial(backward_kernel, head), out_shape=shape(...  9.79 us
    pallas_call x1, Pallas kernels, on_device(): pl.pallas_call(functools.partial(forward_kernel, head), out_shape=kept +...  8.98 us
    reduce_scatter x1, waiting for transfers between devices, on_device(): summed = lax.psum_scatter(branch, Z, scatter_dimension=0, tiled=True)  8.08 us
  transfers between devices with their start and end apart: 10, of which 5 were waited for; matrix products, arithmetic and copies ran while one was open for 4% of the time, Pallas kernels for 10%

profile of v8, /device:TPU:8, one launch (start us, length us, event | category | flops | bytes accessed | tf_op | source)
XLA Modules:
  0.0 185.6 jit_solution(5551255513149966186)
XLA Ops:
  7.2 1.0 fusion.2
  8.9 3.4 %all-to-all-start = ((bf16[2,2,96,256]{3,2,1,0:T(8,128)(2,1)}), bf16[2,2,96,256]{3,2,1,0:T(8,128)(2,1)S(1)}, u32[]{:S(2)}, u32[]{:S(2)}) async-start(bf16[2,2,96,256]{3,2,1,0:T(8,128)(2,1)} %bitcast.9), calls=%async_computation | async-start | bytes 393216 | tf_op jit(solution)/shard_map/all_to_all | solution.py:207
  12.4 1.0 dynamic-slice_bitcast_fusion.1
  13.5 3.6 %all-to-all-done = bf16[2,2,96,256]{3,2,1,0:T(8,128)(2,1)S(1)} async-done(((bf16[2,2,96,256]{3,2,1,0:T(8,128)(2,1)}), bf16[2,2,96,256]{3,2,1,0:T(8,128)(2,1)S(1)}, u32[]{:S(2)}, u32[]{:S(2)}) %all-to-all-start) | async-done | bytes 196640 | tf_op jit(solution)/shard_map/all_to_all | solution.py:207
  17.9 2.1 %collective-permute-start = (bf16[192,3072]{1,0:T(8,128)(2,1)S(1)}, bf16[192,3072]{1,0:T(8,128)(2,1)S(1)}, u32[]{:S(2)}, u32[]{:S(2)}) collective-permute-start(bf16[192,3072]{1,0:T(8,128)(2,1)S(1)} %pad_maximum_fusion), channel_id=1, source_target_pairs={{0,1},{1,0},{2,3},{3,2},{4,5},{5,4},{6,7},{7,6},{8,9},{9,8},{10,11... | collective-permute-start | bytes 3538952 | tf_op jit(solution)/shard_map/ppermute | solution.py:221
  20.0 30.4 %all_gather.6.refs_0_ = bf16[768,256]{1,0:T(8,128)(2,1)S(1)} all-gather(bf16[192,256]{1,0:T(8,128)(2,1)S(1)} %bitcast.28), channel_id=1, replica_groups=mesh['xh'=2,'y'=4,'core'=2,'zh'=4,'zl'=4,'xl'=2] {'zh'}, dimensions={0}, use_global_device_ids=true | all-gather | bytes 491520 | tf_op jit(solution)/shard_map/all_gather | solution.py:222
  50.4 1.9 %collective-permute-start.5 = (bf16[192,3072]{1,0:T(8,128)(2,1)S(1)}, bf16[192,3072]{1,0:T(8,128)(2,1)S(1)}, u32[]{:S(2)}, u32[]{:S(2)}) collective-permute-start(bf16[192,3072]{1,0:T(8,128)(2,1)S(1)} %collective-permute-done.refs_7_.refs_9_), channel_id=1, source_target_pairs={{0,32},{32,0},{1,33},{33,1},{2,34},{34,2},{3,35},{35,3},{4,36},{36... | collective-permute-start | bytes 3538952 | tf_op jit(solution)/shard_map/ppermute | solution.py:224
  52.3 2.8 %collective-permute-start.2 = (bf16[768,256]{1,0:T(8,128)(2,1)S(1)}, bf16[768,256]{1,0:T(8,128)(2,1)S(1)}, u32[]{:S(2)}, u32[]{:S(2)}) collective-permute-start(bf16[768,256]{1,0:T(8,128)(2,1)S(1)} %all_gather.6.refs_0_), channel_id=1, source_target_pairs={{0,2},{2,4},{4,6},{6,8},{8,10},{10,12},{12,14},{14,16},{16,18},{18... | collective-permute-start | bytes 1179656 | tf_op jit(solution)/shard_map/ppermute | solution.py:182
  55.1 6.5 %collective-permute-start.1 = (bf16[768,256]{1,0:T(8,128)(2,1)S(1)}, bf16[768,256]{1,0:T(8,128)(2,1)}, u32[]{:S(2)}, u32[]{:S(2)}) collective-permute-start(bf16[768,256]{1,0:T(8,128)(2,1)S(1)} %all_gather.6.refs_0_), channel_id=1, source_target_pairs={{0,30},{2,0},{4,2},{6,4},{8,6},{10,8},{12,10},{14,12},{16,14},{18,... | collective-permute-start | bytes 1179656 | tf_op jit(solution)/shard_map/ppermute | solution.py:182
  61.6 4.4 %collective-permute-start.4 = (bf16[384,256]{1,0:T(8,128)(2,1)S(1)}, bf16[384,256]{1,0:T(8,128)(2,1)}, u32[]{:S(2)}, u32[]{:S(2)}) collective-permute-start(bf16[384,256]{1,0:T(8,128)(2,1)S(1)} %get-tuple-element.31), channel_id=1, source_target_pairs={{0,28},{2,30},{4,0},{6,2},{8,4},{10,6},{12,8},{14,10},{16,12},{18,... | collective-permute-start | bytes 589832 | tf_op jit(solution)/shard_map/ppermute | solution.py:182
  66.0 2.4 %collective-permute-start.3 = (bf16[384,256]{1,0:T(8,128)(2,1)S(1)}, bf16[384,256]{1,0:T(8,128)(2,1)}, u32[]{:S(2)}, u32[]{:S(2)}) collective-permute-start(bf16[384,256]{1,0:T(8,128)(2,1)S(1)} %get-tuple-element.32), channel_id=1, source_target_pairs={{0,4},{2,6},{4,8},{6,10},{8,12},{10,14},{12,16},{14,18},{16,20},{1... | collective-permute-start | bytes 589832 | tf_op jit(solution)/shard_map/ppermute | solution.py:182
  69.0 17.0 %collective-permute-done.4.refs_4_ = bf16[384,256]{1,0:T(8,128)(2,1)} collective-permute-done((bf16[384,256]{1,0:T(8,128)(2,1)S(1)}, bf16[384,256]{1,0:T(8,128)(2,1)}, u32[]{:S(2)}, u32[]{:S(2)}) %collective-permute-start.4) | collective-permute-done | bytes 196640 | tf_op jit(solution)/shard_map/ppermute | solution.py:182
  86.0 0.7 copy-done.5
  87.2 9.0 %forward.1 = (bf16[3072,256]{1,0:T(8,128)(2,1)}, f32[2,256,256]{2,1,0:T(8,128)}, f32[2,96,256]{2,1,0:T(8,128)}, f32[2,96,256]{2,1,0:T(8,128)}, f32[2,8,256]{2,1,...) custom-call(s32[7]{0:T(128)} %stack.31.place, ...), custom_call_target="tpu_custom_call" | custom-call | flops 2000000000 | bytes 14000000 | tf_op jit(solution)/shard_map/forward/pallas_call | solution.py:247
  96.2 2.9 %all-gather.2.cloned.1.call-done.refs_7_ = bf16[3072,256]{1,0:T(8,128)(2,1)} async-done(((bf16[192,256]{1,0:T(8,128)(2,1)}), bf16[3072,256]{1,0:T(8,128)(2,1)}) %all-gather.2.cloned.1.call-update) | async-done | bytes 1572880 | tf_op jit(solution)/shard_map/all_gather | solution.py:220
  99.1 9.8 %backward.1 = bf16[2,2,8,192,384]{4,3,2,1,0:T(8,128)(2,1)} custom-call(s32[7]{0:T(128)} %stack.31.place, bf16[3072,256]{1,0:T(8,128)(2,1)} %get-tuple-element.22.refs_0_, f32[2,256,256]{2,1,0:T(8,128)} %get-tuple-element.23.refs_1_, f32[2,96,256]{2,1,0:T(8,128)} %get-tuple-element.24.refs_2_, f32[2,96,256]{2,1,0:T(8,128)} %get-tuple-element.25.refs_3_, ...), custom_call_target="tpu_custom_call" | custom-call | flops 1000000 | bytes 100000 | tf_op jit(solution)/shard_map/backward/pallas_call | solution.py:270
  108.9 12.8 %all_to_all.20 = bf16[2,2,8,192,384]{4,3,2,1,0:T(8,128)(2,1)} all-to-all(bf16[2,2,8,192,384]{4,3,2,1,0:T(8,128)(2,1)} %backward.1), channel_id=1, replica_groups=mesh['xh'=2,'y'=4,'core'=2,'zh'=4,'zl'=4,'xl'=2] {'core'}, dimensions={0} | all-to-all | bytes 9437184 | tf_op jit(solution)/shard_map/all_to_all | solution.py:287
  121.6 3.5 %reduce_sum.24 = bf16[2,8,192,384]{3,2,1,0:T(8,128)(2,1)S(1)} reduce(bf16[2,2,8,192,384]{4,3,2,1,0:T(8,128)(2,1)} %all_to_all.20, bf16[]{:T(256)} %constant.50.clone.1), dimensions={0}, to_apply=%region_1.2 | reduce | flops 1179648 | bytes 7077890 | tf_op jit(solution)/shard_map/reduce_sum | solution.py:288
  125.2 37.2 %all_to_all.21 = bf16[16,192,384]{2,1,0:T(8,128)(2,1)} all-to-all(bf16[16,192,384]{2,1,0:T(8,128)(2,1)S(1)} %bitcast.22), channel_id=1, replica_groups=mesh['xh'=2,'y'=4,'core'=2,'zh'=4,'zl'=4,'xl'=2] {'xl','xh','y'}, dimensions={0} | all-to-all | bytes 4718592 | tf_op jit(solution)/shard_map/all_to_all | solution.py:289
  162.4 8.1 %reduce-scatter.2.cloned.1.call-done = bf16[192,256]{1,0:T(8,128)(2,1)} async-done(((bf16[3072,256]{1,0:T(8,128)(2,1)}), bf16[192,256]{1,0:T(8,128)(2,1)}) %reduce-scatter.2.cloned.1.call-update) | async-done | bytes 98320 | tf_op jit(solution)/shard_map/reduce_scatter | solution.py:267
  170.5 3.3 %all-to-all-start.3 = ((bf16[2,96,256]{2,1,0:T(8,128)(2,1)}), bf16[2,96,256]{2,1,0:T(8,128)(2,1)S(1)}, u32[]{:S(2)}, u32[]{:S(2)}) async-start(bf16[2,96,256]{2,1,0:T(8,128)(2,1)} %bitcast.30), calls=%async_computation.4 | async-start | bytes 196608 | tf_op jit(solution)/shard_map/all_to_all | solution.py:294
  173.8 2.0 %reduce_sum.25 = bf16[192,384]{1,0:T(8,128)(2,1)S(1)} reduce(bf16[16,192,384]{2,1,0:T(8,128)(2,1)} %all_to_all.21, bf16[]{:T(256)} %constant.50.clone.1), dimensions={0}, to_apply=%region_2.3 | reduce | flops 1105920 | bytes 2506754 | tf_op jit(solution)/shard_map/reduce_sum | solution.py:293
  175.8 0.7 slice.41
  176.5 1.6 all-to-all-done.3
  (27 shorter events, 3.3 us)
Async XLA Ops:
  7.2 6.2 %copy-start.3 = (bf16[3072,288]{0,1:T(8,128)(2,1)S(1)}, bf16[3072,288]{0,1:T(8,128)(2,1)}, u32[]{:S(2)}) copy-start(bf16[3072,288]{0,1:T(8,128)(2,1)} %param.5) | copy-start | bytes 5308420
  8.9 8.2 %all-to-all-start = ((bf16[2,2,96,256]{3,2,1,0:T(8,128)(2,1)}), bf16[2,2,96,256]{3,2,1,0:T(8,128)(2,1)S(1)}, u32[]{:S(2)}, u32[]{:S(2)}) async-start(bf16[2,2,96,256]{3,2,1,0:T(8,128)(2,1)} %bitcast.9), calls=%async_computation | async-start | bytes 393216 | tf_op jit(solution)/shard_map/all_to_all | solution.py:207
  12.3 86.8 %all-gather.2.cloned.1.call-start = ((), (), s32[]{:S(2)}) async-start(), calls=%async_computation.6 | async-start | bytes 1671168 | tf_op jit(solution)/shard_map/all_gather | solution.py:220
  17.8 152.7 %reduce-scatter.2.cloned.1.call-start = ((), (), s32[]{:S(2)}) async-start(), calls=%async_computation.5 | async-start | bytes 1671168 | tf_op jit(solution)/shard_map/reduce_scatter | solution.py:267
  17.9 32.5 %collective-permute-start = (bf16[192,3072]{1,0:T(8,128)(2,1)S(1)}, bf16[192,3072]{1,0:T(8,128)(2,1)S(1)}, u32[]{:S(2)}, u32[]{:S(2)}) collective-permute-start(bf16[192,3072]{1,0:T(8,128)(2,1)S(1)} %pad_maximum_fusion), channel_id=1, source_target_pairs={{0,1},{1,0},{2,3},{3,2},{4,5},{5,4},{6,7},{7,6},{8,9},{9,8},{10,11... | collective-permute-start | bytes 3538952 | tf_op jit(solution)/shard_map/ppermute | solution.py:221
  50.3 35.7 %copy-start = (bf16[768,256]{1,0:T(8,128)(2,1)}, bf16[768,256]{1,0:T(8,128)(2,1)S(1)}, u32[]{:S(2)}) copy-start(bf16[768,256]{1,0:T(8,128)(2,1)S(1)} %all_gather.6.refs_0_) | copy-start | bytes 1179652
  50.4 35.7 %copy-start.1 = (bf16[192,3072]{1,0:T(8,128)(2,1)}, bf16[192,3072]{1,0:T(8,128)(2,1)S(1)}, u32[]{:S(2)}) copy-start(bf16[192,3072]{1,0:T(8,128)(2,1)S(1)} %collective-permute-done.refs_7_.refs_9_) | copy-start | bytes 3538948
  50.4 35.6 %collective-permute-start.5 = (bf16[192,3072]{1,0:T(8,128)(2,1)S(1)}, bf16[192,3072]{1,0:T(8,128)(2,1)S(1)}, u32[]{:S(2)}, u32[]{:S(2)}) collective-permute-start(bf16[192,3072]{1,0:T(8,128)(2,1)S(1)} %collective-permute-done.refs_7_.refs_9_), channel_id=1, source_target_pairs={{0,32},{32,0},{1,33},{33,1},{2,34},{34,2},{3,35},{35,3},{4,36},{36... | collective-permute-start | bytes 3538952 | tf_op jit(solution)/shard_map/ppermute | solution.py:224
  52.3 33.7 %collective-permute-start.2 = (bf16[768,256]{1,0:T(8,128)(2,1)S(1)}, bf16[768,256]{1,0:T(8,128)(2,1)S(1)}, u32[]{:S(2)}, u32[]{:S(2)}) collective-permute-start(bf16[768,256]{1,0:T(8,128)(2,1)S(1)} %all_gather.6.refs_0_), channel_id=1, source_target_pairs={{0,2},{2,4},{4,6},{6,8},{8,10},{10,12},{12,14},{14,16},{16,18},{18... | collective-permute-start | bytes 1179656 | tf_op jit(solution)/shard_map/ppermute | solution.py:182
  55.1 30.9 %collective-permute-start.1 = (bf16[768,256]{1,0:T(8,128)(2,1)S(1)}, bf16[768,256]{1,0:T(8,128)(2,1)}, u32[]{:S(2)}, u32[]{:S(2)}) collective-permute-start(bf16[768,256]{1,0:T(8,128)(2,1)S(1)} %all_gather.6.refs_0_), channel_id=1, source_target_pairs={{0,30},{2,0},{4,2},{6,4},{8,6},{10,8},{12,10},{14,12},{16,14},{18,... | collective-permute-start | bytes 1179656 | tf_op jit(solution)/shard_map/ppermute | solution.py:182
  61.6 24.4 %collective-permute-start.4 = (bf16[384,256]{1,0:T(8,128)(2,1)S(1)}, bf16[384,256]{1,0:T(8,128)(2,1)}, u32[]{:S(2)}, u32[]{:S(2)}) collective-permute-start(bf16[384,256]{1,0:T(8,128)(2,1)S(1)} %get-tuple-element.31), channel_id=1, source_target_pairs={{0,28},{2,30},{4,0},{6,2},{8,4},{10,6},{12,8},{14,10},{16,12},{18,... | collective-permute-start | bytes 589832 | tf_op jit(solution)/shard_map/ppermute | solution.py:182
  66.0 20.0 %collective-permute-start.3 = (bf16[384,256]{1,0:T(8,128)(2,1)S(1)}, bf16[384,256]{1,0:T(8,128)(2,1)}, u32[]{:S(2)}, u32[]{:S(2)}) collective-permute-start(bf16[384,256]{1,0:T(8,128)(2,1)S(1)} %get-tuple-element.32), channel_id=1, source_target_pairs={{0,4},{2,6},{4,8},{6,10},{8,12},{10,14},{12,16},{14,18},{16,20},{1... | collective-permute-start | bytes 589832 | tf_op jit(solution)/shard_map/ppermute | solution.py:182
  86.0 0.7 copy-start.5
  86.0 1.1 copy-start.2
  170.5 7.6 %all-to-all-start.3 = ((bf16[2,96,256]{2,1,0:T(8,128)(2,1)}), bf16[2,96,256]{2,1,0:T(8,128)(2,1)S(1)}, u32[]{:S(2)}, u32[]{:S(2)}) async-start(bf16[2,96,256]{2,1,0:T(8,128)(2,1)} %bitcast.30), calls=%async_computation.4 | async-start | bytes 196608 | tf_op jit(solution)/shard_map/all_to_all | solution.py:294
  175.8 2.9 %copy-start.4 = (bf16[192,384]{1,0:T(8,128)(2,1)}, bf16[192,384]{1,0:T(8,128)(2,1)S(1)}, u32[]{:S(2)}) copy-start(bf16[192,384]{1,0:T(8,128)(2,1)S(1)} %reduce_sum.25) | copy-start | bytes 442372
Sparse Core Ops, SparseCore 0:
  17.9 81.1 all-gather.1
  101.9 68.5 reduce-scatter.1

commit v9 on v5

--- a/solution.py
+++ b/solution.py
@@ -70,18 +70,20 @@
     block = features // (4 * GROUP)
     core = place[4]
     thirds, quarter = 3 * head // 2, head // 2
+    half = block // 2
     rows_in = []
     for ref, (which, first, count) in zip(sets, SETS):
-        for n in range(count):
-            at = aligned((GROUP * (first + n) + place[which]) * block, block)
-            rows_in.append((ref.at[pl.ds(block * n, block)], raw.at[at]))
+        for n in range(2 * count):
+            at = (GROUP * (first + n // 2) + place[which]) * block + place[5 + n % 2] * half
+            rows_in.append((ref.at[pl.ds(half * n, half)], raw.at[aligned(at, half)]))
     rows_in = start_all(rows_in, sems)
-    weights_in = [(qkv_own, qkv.at[0]), (out_own, out.at[0])]
+    weights_in = [(qkv_own, qkv.at[0])]
     for source, at in partner_pieces(mine, theirs, core, 0, thirds):
         weights_in.append((source, qkv.at[1, at]))
+    weights_in.append((out_own, out.at[0]))
     for source, at in partner_pieces(mine, theirs, core, thirds, quarter):
         weights_in.append((source, out.at[1, at]))
-    weights_in = start_all(weights_in, sems, 16)
+    weights_in = start_all(weights_in, sems, 32)
     wait_all(rows_in)
 
     def rows_of(n):
@@ -96,10 +98,10 @@
     scale = lax.rsqrt(jnp.sum(variance, 0, keepdims=True) / features + epsilon)
     for n in blocks:
         normed[block * n : block * (n + 1), :] = ((rows_of(n) - mean) * scale).astype(low)
-    results_out = start_all([(normed, results[0])], sems, 22)
-    wait_all(weights_in)
+    wait_all(weights_in[:3])
+    both = contract(qkv[...].reshape(6 * head, features), normed[...], 1, 0).astype(low)
     for slot in range(2):
-        projected = contract(qkv[slot], normed[...], 1, 0).astype(low)
+        projected = both[3 * head * slot : 3 * head * (slot + 1)]
         query_norm, query_inv = normalize_first(projected[:head].astype(wide))
         key_norm, key_inv = normalize_first(projected[head : 2 * head].astype(wide))
         values = projected[2 * head :]
@@ -113,14 +115,16 @@
         inverses[slot, 1:2, :] = key_inv
         value[slot] = values
         heads[slot] = contract(values, attend.astype(low), 1, 0).astype(low)
-    results_out += start_all(list(zip(kept[1:], results[1:])), sems, 23)
+    results_out = start_all(list(zip(kept[1:], results[1:])), sems, 39)
+    results_out += start_all([(normed, results[0])], sems, 38)
+    wait_all(weights_in[3:])
     both_heads = heads[...].reshape(2 * head, PATCHES)
     step = 768
     for n, start in enumerate(range(0, features, step)):
         both = out[:, :, start : start + step].reshape(2 * head, step)
         branch[start : start + step, :] = contract(both, both_heads, 0, 0).astype(low)
         part = pl.ds(start, step)
-        results_out += start_all([(branch.at[part], branch_result.at[part])], sems, 29 + n)
+        results_out += start_all([(branch.at[part], branch_result.at[part])], sems, 45 + n)
     wait_all(results_out)
 
 
@@ -131,15 +135,17 @@
     normed, attention, query, key, inverses, value, heads = kept
     core = place[4]
     thirds, quarter = 3 * head // 2, head // 2
-    first_in = [(cotangent_in, cotangent), (out_own, out.at[0])]
+    first_in = [(cotangent_in.at[:, n], cotangent.at[:, place[5 + n]]) for n in range(2)]
+    first_in.append((out_own, out.at[0]))
     for source, at in partner_pieces(mine, theirs, core, thirds, quarter):
         first_in.append((source, out.at[1, at]))
     first_in = start_all(first_in, sems)
-    kept_in = start_all(list(zip(results[1:], kept[1:])) + [(results[0], normed)], sems, 4)
+    kept_in = start_all(list(zip(results[1:], kept[1:])) + [(results[0], normed)], sems, 5)
     wait_all(first_in)
     scaling = head ** (-0.5)
     cores, _, chips, rows, columns = shares.shape
-    grads = [contract(out[slot], cotangent[...], 1, 0).astype(low) for slot in range(2)]
+    cotangent = cotangent[...].reshape(normed.shape)
+    grads = [contract(out[slot], cotangent, 1, 0).astype(low) for slot in range(2)]
     wait_all(kept_in[:-1])
     rights = []
     for slot, grad in enumerate(grads):
@@ -201,8 +207,12 @@
         ]
     ).astype(jnp.int32)
 
-    stacked = jnp.stack([activations, d_branch]).reshape(2, part, images, PATCHES)
-    mixed = lax.all_to_all(stacked.transpose(2, 0, 1, 3), "xl", 0, 0, tiled=True)
+    def exchange(values):
+        kept_image = lax.dynamic_slice_in_dim(values, xl_at * PATCHES, PATCHES, 1)
+        other_image = lax.dynamic_slice_in_dim(values, (1 - xl_at) * PATCHES, PATCHES, 1)
+        return jnp.concatenate([kept_image, lax.ppermute(other_image, "xl", swap)], 0)
+
+    cot_block, act_block = exchange(d_branch), exchange(activations)
 
     qkv_own, out_own = w_qkv.T, w_out.T
     thirds, quarter = 3 * head // 2, head // 2
@@ -213,15 +223,14 @@
         ],
         0,
     )
-    mine, mixed = lax.optimization_barrier((mine, mixed))
-    chunk = xl * part
-    cotangent = lax.all_gather(mixed[:, 1].reshape(chunk, PATCHES), Z, axis=0, tiled=True)
+    mine, cot_block, act_block = lax.optimization_barrier((mine, cot_block, act_block))
+    cotangent = lax.all_gather(cot_block, Z, axis=0, tiled=True)
+    cotangent = cotangent.reshape(features // (xl * part), xl, part, PATCHES)
     mine = lax.ppermute(mine, "xl", swap)
-    copies = jnp.broadcast_to(mixed[:, 0].reshape(1, chunk, PATCHES), (zh, chunk, PATCHES))
-    same = lax.all_to_all(copies, "zh", 0, 0, tiled=True).reshape(zh * chunk, PATCHES)
+    same = lax.all_gather(act_block, "zh", axis=0, tiled=True)
     mine, same = lax.optimization_barrier((mine, same))
     theirs = lax.ppermute(mine, "core", swap)
-    middle = zh * chunk // 2
+    middle = same.shape[0] // 2
     sets = (
         same,
         shift(same, -1),
@@ -255,7 +264,7 @@
             pltpu.VMEM((features, PATCHES), low),
         ]
         + [pltpu.VMEM(k.shape, k.dtype) for k in kept]
-        + [pltpu.SemaphoreType.DMA((33,))],
+        + [pltpu.SemaphoreType.DMA((49,))],
         compiler_params=pltpu.CompilerParams(vmem_limit_bytes=60 << 20),
         cost_estimate=pl.CostEstimate(
             flops=2_000_000_000, bytes_accessed=14_000_000, transcendentals=131072
@@ -272,11 +281,11 @@
         in_specs=[smem] + [hbm] * 11,
         out_specs=vmem,
         scratch_shapes=[
-            pltpu.VMEM((features, PATCHES), low),
+            pltpu.VMEM(cotangent.shape, low),
             pltpu.VMEM((2, head, features), low),
         ]
         + [pltpu.VMEM(k.shape, k.dtype) for k in kept]
-        + [pltpu.SemaphoreType.DMA((11,))],
+        + [pltpu.SemaphoreType.DMA((12,))],
         compiler_params=pltpu.CompilerParams(vmem_limit_bytes=60 << 20),
         cost_estimate=pl.CostEstimate(
             flops=1_000_000, bytes_accessed=100_000, transcendentals=0

time: 195 us -> 187 us (0.959)
  the two profiles are of different devices: /device:TPU:8 before, /device:TPU:12 now
where the time goes in v9:
time: 187 us; the launch traced here: 186 us
  blocking collectives  79.3 us (42%)
  waiting for transfers between devices  33.1 us (18%)
  starting transfers between devices  27.9 us (15%)
  Pallas kernels  18.6 us (10%)
  between operations  14.3 us (8%)
  local copies, waits for them, and re-layouts  7.01 us (4%)
  other arithmetic  6.25 us (3%)
    all_to_all x1, blocking collectives, on_device(): lax.all_to_all(pair_sum.reshape(xl * xh * y, rows, columns), ('xl', 'xh',...  35.1 us
    all_gather x1, blocking collectives, on_device(): same = lax.all_gather(act_block, 'zh', axis=0, tiled=True)  31.5 us
    ppermute x4, waiting for transfers between devices, shift(): return lax.ppermute(values, Z, [(i, (i + by) % size) for i in range(size)])  16.9 us
    ppermute x4, starting transfers between devices, shift(): return lax.ppermute(values, Z, [(i, (i + by) % size) for i in range(size)])  14 us
    all_to_all x1, blocking collectives, on_device(): pairs = lax.all_to_all(shares, 'core', 0, 0, tiled=True)  12.7 us
    reduce_scatter x1, waiting for transfers between devices, on_device(): summed = lax.psum_scatter(branch, Z, scatter_dimension=0, tiled=True)  10.3 us
    pallas_call x1, Pallas kernels, on_device(): pl.pallas_call(functools.partial(backward_kernel, head), out_shape=shape(...  9.82 us
    pallas_call x1, Pallas kernels, on_device(): pl.pallas_call(functools.partial(forward_kernel, head), out_shape=kept +...  8.81 us
  transfers between devices with their start and end apart: 11, of which 5 were waited for; matrix products, arithmetic and copies ran while one was open for 5% of the time, Pallas kernels for 10%

profile of v9, /device:TPU:12, one launch (start us, length us, event | category | flops | bytes accessed | tf_op | source)
XLA Modules:
  0.0 186.5 jit_solution(1425766648730944561)
XLA Ops:
  8.1 3.1 %collective-permute-start.1 = (bf16[96,256]{1,0:T(8,128)(2,1)S(1)}, bf16[96,256]{1,0:T(8,128)(2,1)S(1)}, u32[]{:S(2)}, u32[]{:S(2)}) collective-permute-start(bf16[96,256]{1,0:T(8,128)(2,1)S(1)} %get-tuple-element.36), channel_id=1, source_target_pairs={{0,1},{1,0},{2,3},{3,2},{4,5},{5,4},{6,7},{7,6},{8,9},{9,8},{10,11... | collective-permute-start | bytes 147464 | tf_op jit(solution)/shard_map/ppermute | solution.py:213
  11.2 0.8 constant_dynamic-slice_fusion.3
  12.0 2.7 %collective-permute-start = (bf16[96,256]{1,0:T(8,128)(2,1)S(1)}, bf16[96,256]{1,0:T(8,128)(2,1)S(1)}, u32[]{:S(2)}, u32[]{:S(2)}) collective-permute-start(bf16[96,256]{1,0:T(8,128)(2,1)S(1)} %get-tuple-element.38), channel_id=1, source_target_pairs={{0,1},{1,0},{2,3},{3,2},{4,5},{5,4},{6,7},{7,6},{8,9},{9,8},{10,11... | collective-permute-start | bytes 147464 | tf_op jit(solution)/shard_map/ppermute | solution.py:213
  14.7 1.0 dynamic-slice_bitcast_fusion.1
  15.7 1.2 dynamic-slice_bitcast_fusion
  17.1 0.9 collective-permute-done
  18.7 2.7 %collective-permute-start.2 = (bf16[192,3072]{1,0:T(8,128)(2,1)S(1)}, bf16[192,3072]{1,0:T(8,128)(2,1)S(1)}, u32[]{:S(2)}, u32[]{:S(2)}) collective-permute-start(bf16[192,3072]{1,0:T(8,128)(2,1)S(1)} %pad_maximum_fusion), channel_id=1, source_target_pairs={{0,1},{1,0},{2,3},{3,2},{4,5},{5,4},{6,7},{7,6},{8,9},{9,8},{10,11... | collective-permute-start | bytes 3538952 | tf_op jit(solution)/shard_map/ppermute | solution.py:229
  21.4 31.5 %all_gather.6.refs_0_ = bf16[768,256]{1,0:T(8,128)(2,1)S(1)} all-gather(bf16[192,256]{1,0:T(8,128)(2,1)S(1)} %pad_maximum_fusion.2), channel_id=1, replica_groups=mesh['xh'=2,'y'=4,'core'=2,'zh'=4,'zl'=4,'xl'=2] {'zh'}, dimensions={0}, use_global_device_ids=true | all-gather | bytes 491520 | tf_op jit(solution)/shard_map/all_gather | solution.py:230
  52.9 1.9 %collective-permute-start.7 = (bf16[192,3072]{1,0:T(8,128)(2,1)S(1)}, bf16[192,3072]{1,0:T(8,128)(2,1)S(1)}, u32[]{:S(2)}, u32[]{:S(2)}) collective-permute-start(bf16[192,3072]{1,0:T(8,128)(2,1)S(1)} %collective-permute-done.2.refs_7_.refs_9_), channel_id=1, source_target_pairs={{0,32},{32,0},{1,33},{33,1},{2,34},{34,2},{3,35},{35,3},{4,36},{36... | collective-permute-start | bytes 3538952 | tf_op jit(solution)/shard_map/ppermute | solution.py:232
  54.8 1.9 %collective-permute-start.4 = (bf16[768,256]{1,0:T(8,128)(2,1)S(1)}, bf16[768,256]{1,0:T(8,128)(2,1)S(1)}, u32[]{:S(2)}, u32[]{:S(2)}) collective-permute-start(bf16[768,256]{1,0:T(8,128)(2,1)S(1)} %all_gather.6.refs_0_), channel_id=1, source_target_pairs={{0,2},{2,4},{4,6},{6,8},{8,10},{10,12},{12,14},{14,16},{16,18},{18... | collective-permute-start | bytes 1179656 | tf_op jit(solution)/shard_map/ppermute | solution.py:188
  56.8 5.3 %collective-permute-start.3 = (bf16[768,256]{1,0:T(8,128)(2,1)S(1)}, bf16[768,256]{1,0:T(8,128)(2,1)}, u32[]{:S(2)}, u32[]{:S(2)}) collective-permute-start(bf16[768,256]{1,0:T(8,128)(2,1)S(1)} %all_gather.6.refs_0_), channel_id=1, source_target_pairs={{0,30},{2,0},{4,2},{6,4},{8,6},{10,8},{12,10},{14,12},{16,14},{18,... | collective-permute-start | bytes 1179656 | tf_op jit(solution)/shard_map/ppermute | solution.py:188
  62.2 4.4 %collective-permute-start.6 = (bf16[384,256]{1,0:T(8,128)(2,1)S(1)}, bf16[384,256]{1,0:T(8,128)(2,1)}, u32[]{:S(2)}, u32[]{:S(2)}) collective-permute-start(bf16[384,256]{1,0:T(8,128)(2,1)S(1)} %get-tuple-element.33), channel_id=1, source_target_pairs={{0,28},{2,30},{4,0},{6,2},{8,4},{10,6},{12,8},{14,10},{16,12},{18,... | collective-permute-start | bytes 589832 | tf_op jit(solution)/shard_map/ppermute | solution.py:188
  66.5 2.4 %collective-permute-start.5 = (bf16[384,256]{1,0:T(8,128)(2,1)S(1)}, bf16[384,256]{1,0:T(8,128)(2,1)}, u32[]{:S(2)}, u32[]{:S(2)}) collective-permute-start(bf16[384,256]{1,0:T(8,128)(2,1)S(1)} %get-tuple-element.34), channel_id=1, source_target_pairs={{0,4},{2,6},{4,8},{6,10},{8,12},{10,14},{12,16},{14,18},{16,20},{1... | collective-permute-start | bytes 589832 | tf_op jit(solution)/shard_map/ppermute | solution.py:188
  69.5 16.9 %collective-permute-done.6.refs_4_ = bf16[384,256]{1,0:T(8,128)(2,1)} collective-permute-done((bf16[384,256]{1,0:T(8,128)(2,1)S(1)}, bf16[384,256]{1,0:T(8,128)(2,1)}, u32[]{:S(2)}, u32[]{:S(2)}) %collective-permute-start.6) | collective-permute-done | bytes 196640 | tf_op jit(solution)/shard_map/ppermute | solution.py:188
  87.6 8.8 %forward.1 = (bf16[3072,256]{1,0:T(8,128)(2,1)}, f32[2,256,256]{2,1,0:T(8,128)}, f32[2,96,256]{2,1,0:T(8,128)}, f32[2,96,256]{2,1,0:T(8,128)}, f32[2,8,256]{2,1,...) custom-call(s32[7]{0:T(128)} %stack.31.place, ...), custom_call_target="tpu_custom_call" | custom-call | flops 2000000000 | bytes 14000000 | tf_op jit(solution)/shard_map/forward/pallas_call | solution.py:255
  96.4 3.4 %all-gather.2.cloned.1.call-done = bf16[3072,256]{1,0:T(8,128)(2,1)} async-done(((bf16[192,256]{1,0:T(8,128)(2,1)}), bf16[3072,256]{1,0:T(8,128)(2,1)}) %all-gather.2.cloned.1.call-update) | async-done | bytes 1572880 | tf_op jit(solution)/shard_map/all_gather | solution.py:227
  99.9 9.8 %backward.1 = bf16[2,2,8,192,384]{4,3,2,1,0:T(8,128)(2,1)} custom-call(s32[7]{0:T(128)} %stack.31.place, bf16[3072,256]{1,0:T(8,128)(2,1)} %get-tuple-element.23.refs_0_, f32[2,256,256]{2,1,0:T(8,128)} %get-tuple-element.24.refs_1_, f32[2,96,256]{2,1,0:T(8,128)} %get-tuple-element.25.refs_2_, f32[2,96,256]{2,1,0:T(8,128)} %get-tuple-element.26.refs_3_, ...), custom_call_target="tpu_custom_call" | custom-call | flops 1000000 | bytes 100000 | tf_op jit(solution)/shard_map/backward/pallas_call | solution.py:278
  109.7 12.7 %all_to_all.15 = bf16[2,2,8,192,384]{4,3,2,1,0:T(8,128)(2,1)} all-to-all(bf16[2,2,8,192,384]{4,3,2,1,0:T(8,128)(2,1)} %backward.1), channel_id=1, replica_groups=mesh['xh'=2,'y'=4,'core'=2,'zh'=4,'zl'=4,'xl'=2] {'core'}, dimensions={0} | all-to-all | bytes 9437184 | tf_op jit(solution)/shard_map/all_to_all | solution.py:295
  122.4 3.5 %reduce_sum.24 = bf16[2,8,192,384]{3,2,1,0:T(8,128)(2,1)S(1)} reduce(bf16[2,2,8,192,384]{4,3,2,1,0:T(8,128)(2,1)} %all_to_all.15, bf16[]{:T(256)} %constant.54.clone.1), dimensions={0}, to_apply=%region_1.2 | reduce | flops 1179648 | bytes 7077890 | tf_op jit(solution)/shard_map/reduce_sum | solution.py:296
  126.0 35.1 %all_to_all.16 = bf16[16,192,384]{2,1,0:T(8,128)(2,1)} all-to-all(bf16[16,192,384]{2,1,0:T(8,128)(2,1)S(1)} %bitcast.20), channel_id=1, replica_groups=mesh['xh'=2,'y'=4,'core'=2,'zh'=4,'zl'=4,'xl'=2] {'xl','xh','y'}, dimensions={0} | all-to-all | bytes 4718592 | tf_op jit(solution)/shard_map/all_to_all | solution.py:297
  161.0 10.3 %reduce-scatter.2.cloned.1.call-done = bf16[192,256]{1,0:T(8,128)(2,1)} async-done(((bf16[3072,256]{1,0:T(8,128)(2,1)}), bf16[192,256]{1,0:T(8,128)(2,1)}) %reduce-scatter.2.cloned.1.call-update) | async-done | bytes 98320 | tf_op jit(solution)/shard_map/reduce_scatter | solution.py:275
  171.4 3.3 %all-to-all-start.2 = ((bf16[2,96,256]{2,1,0:T(8,128)(2,1)}), bf16[2,96,256]{2,1,0:T(8,128)(2,1)S(1)}, u32[]{:S(2)}, u32[]{:S(2)}) async-start(bf16[2,96,256]{2,1,0:T(8,128)(2,1)} %bitcast.27), calls=%async_computation.3 | async-start | bytes 196608 | tf_op jit(solution)/shard_map/all_to_all | solution.py:302
  174.7 2.0 %reduce_sum.25 = bf16[192,384]{1,0:T(8,128)(2,1)S(1)} reduce(bf16[16,192,384]{2,1,0:T(8,128)(2,1)} %all_to_all.16, bf16[]{:T(256)} %constant.54.clone.1), dimensions={0}, to_apply=%region_2.3 | reduce | flops 1105920 | bytes 2506754 | tf_op jit(solution)/shard_map/reduce_sum | solution.py:301
  177.4 1.6 all-to-all-done.2
  (28 shorter events, 4.8 us)
Async XLA Ops:
  7.2 92.7 %all-gather.2.cloned.1.call-start = ((), (), s32[]{:S(2)}) async-start(), calls=%async_computation.5 | async-start | bytes 1671168 | tf_op jit(solution)/shard_map/all_gather | solution.py:227
  8.1 9.0 %collective-permute-start.1 = (bf16[96,256]{1,0:T(8,128)(2,1)S(1)}, bf16[96,256]{1,0:T(8,128)(2,1)S(1)}, u32[]{:S(2)}, u32[]{:S(2)}) collective-permute-start(bf16[96,256]{1,0:T(8,128)(2,1)S(1)} %get-tuple-element.36), channel_id=1, source_target_pairs={{0,1},{1,0},{2,3},{3,2},{4,5},{5,4},{6,7},{7,6},{8,9},{9,8},{10,11... | collective-permute-start | bytes 147464 | tf_op jit(solution)/shard_map/ppermute | solution.py:213
  12.0 6.0 %collective-permute-start = (bf16[96,256]{1,0:T(8,128)(2,1)S(1)}, bf16[96,256]{1,0:T(8,128)(2,1)S(1)}, u32[]{:S(2)}, u32[]{:S(2)}) collective-permute-start(bf16[96,256]{1,0:T(8,128)(2,1)S(1)} %get-tuple-element.38), channel_id=1, source_target_pairs={{0,1},{1,0},{2,3},{3,2},{4,5},{5,4},{6,7},{7,6},{8,9},{9,8},{10,11... | collective-permute-start | bytes 147464 | tf_op jit(solution)/shard_map/ppermute | solution.py:213
  18.6 152.7 %reduce-scatter.2.cloned.1.call-start = ((), (), s32[]{:S(2)}) async-start(), calls=%async_computation.4 | async-start | bytes 1671168 | tf_op jit(solution)/shard_map/reduce_scatter | solution.py:275
  18.7 34.2 %collective-permute-start.2 = (bf16[192,3072]{1,0:T(8,128)(2,1)S(1)}, bf16[192,3072]{1,0:T(8,128)(2,1)S(1)}, u32[]{:S(2)}, u32[]{:S(2)}) collective-permute-start(bf16[192,3072]{1,0:T(8,128)(2,1)S(1)} %pad_maximum_fusion), channel_id=1, source_target_pairs={{0,1},{1,0},{2,3},{3,2},{4,5},{5,4},{6,7},{7,6},{8,9},{9,8},{10,11... | collective-permute-start | bytes 3538952 | tf_op jit(solution)/shard_map/ppermute | solution.py:229
  52.9 33.5 %copy-start = (bf16[768,256]{1,0:T(8,128)(2,1)}, bf16[768,256]{1,0:T(8,128)(2,1)S(1)}, u32[]{:S(2)}) copy-start(bf16[768,256]{1,0:T(8,128)(2,1)S(1)} %all_gather.6.refs_0_) | copy-start | bytes 1179652
  52.9 33.5 %copy-start.1 = (bf16[192,3072]{1,0:T(8,128)(2,1)}, bf16[192,3072]{1,0:T(8,128)(2,1)S(1)}, u32[]{:S(2)}) copy-start(bf16[192,3072]{1,0:T(8,128)(2,1)S(1)} %collective-permute-done.2.refs_7_.refs_9_) | copy-start | bytes 3538948
  52.9 33.5 %collective-permute-start.7 = (bf16[192,3072]{1,0:T(8,128)(2,1)S(1)}, bf16[192,3072]{1,0:T(8,128)(2,1)S(1)}, u32[]{:S(2)}, u32[]{:S(2)}) collective-permute-start(bf16[192,3072]{1,0:T(8,128)(2,1)S(1)} %collective-permute-done.2.refs_7_.refs_9_), channel_id=1, source_target_pairs={{0,32},{32,0},{1,33},{33,1},{2,34},{34,2},{3,35},{35,3},{4,36},{36... | collective-permute-start | bytes 3538952 | tf_op jit(solution)/shard_map/ppermute | solution.py:232
  54.8 31.6 %collective-permute-start.4 = (bf16[768,256]{1,0:T(8,128)(2,1)S(1)}, bf16[768,256]{1,0:T(8,128)(2,1)S(1)}, u32[]{:S(2)}, u32[]{:S(2)}) collective-permute-start(bf16[768,256]{1,0:T(8,128)(2,1)S(1)} %all_gather.6.refs_0_), channel_id=1, source_target_pairs={{0,2},{2,4},{4,6},{6,8},{8,10},{10,12},{12,14},{14,16},{16,18},{18... | collective-permute-start | bytes 1179656 | tf_op jit(solution)/shard_map/ppermute | solution.py:188
  56.8 29.6 %collective-permute-start.3 = (bf16[768,256]{1,0:T(8,128)(2,1)S(1)}, bf16[768,256]{1,0:T(8,128)(2,1)}, u32[]{:S(2)}, u32[]{:S(2)}) collective-permute-start(bf16[768,256]{1,0:T(8,128)(2,1)S(1)} %all_gather.6.refs_0_), channel_id=1, source_target_pairs={{0,30},{2,0},{4,2},{6,4},{8,6},{10,8},{12,10},{14,12},{16,14},{18,... | collective-permute-start | bytes 1179656 | tf_op jit(solution)/shard_map/ppermute | solution.py:188
  62.2 24.3 %collective-permute-start.6 = (bf16[384,256]{1,0:T(8,128)(2,1)S(1)}, bf16[384,256]{1,0:T(8,128)(2,1)}, u32[]{:S(2)}, u32[]{:S(2)}) collective-permute-start(bf16[384,256]{1,0:T(8,128)(2,1)S(1)} %get-tuple-element.33), channel_id=1, source_target_pairs={{0,28},{2,30},{4,0},{6,2},{8,4},{10,6},{12,8},{14,10},{16,12},{18,... | collective-permute-start | bytes 589832 | tf_op jit(solution)/shard_map/ppermute | solution.py:188
  66.5 19.9 %collective-permute-start.5 = (bf16[384,256]{1,0:T(8,128)(2,1)S(1)}, bf16[384,256]{1,0:T(8,128)(2,1)}, u32[]{:S(2)}, u32[]{:S(2)}) collective-permute-start(bf16[384,256]{1,0:T(8,128)(2,1)S(1)} %get-tuple-element.34), channel_id=1, source_target_pairs={{0,4},{2,6},{4,8},{6,10},{8,12},{10,14},{12,16},{14,18},{16,20},{1... | collective-permute-start | bytes 589832 | tf_op jit(solution)/shard_map/ppermute | solution.py:188
  86.4 0.8 copy-start.4
  86.4 1.2 copy-start.2
  171.4 7.6 %all-to-all-start.2 = ((bf16[2,96,256]{2,1,0:T(8,128)(2,1)}), bf16[2,96,256]{2,1,0:T(8,128)(2,1)S(1)}, u32[]{:S(2)}, u32[]{:S(2)}) async-start(bf16[2,96,256]{2,1,0:T(8,128)(2,1)} %bitcast.27), calls=%async_computation.3 | async-start | bytes 196608 | tf_op jit(solution)/shard_map/all_to_all | solution.py:302
  176.7 2.9 %copy-start.3 = (bf16[192,384]{1,0:T(8,128)(2,1)}, bf16[192,384]{1,0:T(8,128)(2,1)S(1)}, u32[]{:S(2)}) copy-start(bf16[192,384]{1,0:T(8,128)(2,1)S(1)} %reduce_sum.25) | copy-start | bytes 442372
Sparse Core Ops, SparseCore 0:
  18.8 81.0 all-gather.1
  102.7 68.6 reduce-scatter.1

commit v10 on v8

--- a/solution.py
+++ b/solution.py
@@ -76,9 +76,10 @@
             at = aligned((GROUP * (first + n) + place[which]) * block, block)
             rows_in.append((ref.at[pl.ds(block * n, block)], raw.at[at]))
     rows_in = start_all(rows_in, sems)
-    weights_in = [(qkv_own, qkv.at[0]), (out_own, out.at[0])]
+    weights_in = [(qkv_own, qkv.at[0])]
     for source, at in partner_pieces(mine, theirs, core, 0, thirds):
         weights_in.append((source, qkv.at[1, at]))
+    weights_in.append((out_own, out.at[0]))
     for source, at in partner_pieces(mine, theirs, core, thirds, quarter):
         weights_in.append((source, out.at[1, at]))
     weights_in = start_all(weights_in, sems, 16)
@@ -96,10 +97,10 @@
     scale = lax.rsqrt(jnp.sum(variance, 0, keepdims=True) / features + epsilon)
     for n in blocks:
         normed[block * n : block * (n + 1), :] = ((rows_of(n) - mean) * scale).astype(low)
-    results_out = start_all([(normed, results[0])], sems, 22)
-    wait_all(weights_in)
+    wait_all(weights_in[:3])
+    both = contract(qkv[...].reshape(6 * head, features), normed[...], 1, 0).astype(low)
     for slot in range(2):
-        projected = contract(qkv[slot], normed[...], 1, 0).astype(low)
+        projected = both[3 * head * slot : 3 * head * (slot + 1)]
         query_norm, query_inv = normalize_first(projected[:head].astype(wide))
         key_norm, key_inv = normalize_first(projected[head : 2 * head].astype(wide))
         values = projected[2 * head :]
@@ -113,7 +114,9 @@
         inverses[slot, 1:2, :] = key_inv
         value[slot] = values
         heads[slot] = contract(values, attend.astype(low), 1, 0).astype(low)
-    results_out += start_all(list(zip(kept[1:], results[1:])), sems, 23)
+    results_out = start_all(list(zip(kept[1:], results[1:])), sems, 23)
+    results_out += start_all([(normed, results[0])], sems, 22)
+    wait_all(weights_in[3:])
     both_heads = heads[...].reshape(2 * head, PATCHES)
     step = 768
     for n, start in enumerate(range(0, features, step)):

time: 186 us -> 186 us (level)
  the two profiles are of different devices: /device:TPU:8 before, /device:TPU:4 now
where the time goes in v10:
time: 186 us
  blocking collectives  79.3 us (43%)
  waiting for transfers between devices  34.6 us (19%)
  starting transfers between devices  27 us (15%)
  Pallas kernels  18.5 us (10%)
  between operations  14.3 us (8%)
  other arithmetic  6.27 us (3%)
  local copies, waits for them, and re-layouts  5.86 us (3%)
    all_to_all x1, blocking collectives, on_device(): lax.all_to_all(pair_sum.reshape(xl * xh * y, rows, columns), ('xl', 'xh',...  36.2 us
    all_gather x1, blocking collectives, on_device(): lax.all_gather(mixed[:, 0].reshape(chunk, PATCHES), 'zh', axis=0, tiled=T...  30.3 us
    ppermute x4, waiting for transfers between devices, shift(): return lax.ppermute(values, Z, [(i, (i + by) % size) for i in range(size)])  17.2 us
    ppermute x4, starting transfers between devices, shift(): return lax.ppermute(values, Z, [(i, (i + by) % size) for i in range(size)])  16.1 us
    all_to_all x1, blocking collectives, on_device(): pairs = lax.all_to_all(shares, 'core', 0, 0, tiled=True)  12.8 us
    pallas_call x1, Pallas kernels, on_device(): pl.pallas_call(functools.partial(backward_kernel, head), out_shape=shape(...  9.8 us
    reduce_scatter x1, waiting for transfers between devices, on_device(): summed = lax.psum_scatter(branch, Z, scatter_dimension=0, tiled=True)  8.96 us
    pallas_call x1, Pallas kernels, on_device(): pl.pallas_call(functools.partial(forward_kernel, head), out_shape=kept +...  8.66 us
  transfers between devices with their start and end apart: 10, of which 5 were waited for; matrix products, arithmetic and copies ran while one was open for 4% of the time, Pallas kernels for 10%

profile of v10, /device:TPU:4, one launch (start us, length us, event | category | flops | bytes accessed | tf_op | source)
XLA Modules:
  0.0 185.7 jit_solution(15737860329654747469)
XLA Ops:
  7.2 1.0 fusion.2
  8.9 3.4 %all-to-all-start = ((bf16[2,2,96,256]{3,2,1,0:T(8,128)(2,1)}), bf16[2,2,96,256]{3,2,1,0:T(8,128)(2,1)S(1)}, u32[]{:S(2)}, u32[]{:S(2)}) async-start(bf16[2,2,96,256]{3,2,1,0:T(8,128)(2,1)} %bitcast.9), calls=%async_computation | async-start | bytes 393216 | tf_op jit(solution)/shard_map/all_to_all | solution.py:210
  12.4 1.0 dynamic-slice_bitcast_fusion.1
  13.5 3.6 %all-to-all-done = bf16[2,2,96,256]{3,2,1,0:T(8,128)(2,1)S(1)} async-done(((bf16[2,2,96,256]{3,2,1,0:T(8,128)(2,1)}), bf16[2,2,96,256]{3,2,1,0:T(8,128)(2,1)S(1)}, u32[]{:S(2)}, u32[]{:S(2)}) %all-to-all-start) | async-done | bytes 196640 | tf_op jit(solution)/shard_map/all_to_all | solution.py:210
  17.9 2.1 %collective-permute-start = (bf16[192,3072]{1,0:T(8,128)(2,1)S(1)}, bf16[192,3072]{1,0:T(8,128)(2,1)S(1)}, u32[]{:S(2)}, u32[]{:S(2)}) collective-permute-start(bf16[192,3072]{1,0:T(8,128)(2,1)S(1)} %pad_maximum_fusion), channel_id=1, source_target_pairs={{0,1},{1,0},{2,3},{3,2},{4,5},{5,4},{6,7},{7,6},{8,9},{9,8},{10,11... | collective-permute-start | bytes 3538952 | tf_op jit(solution)/shard_map/ppermute | solution.py:224
  20.0 30.3 %all_gather.6.refs_0_ = bf16[768,256]{1,0:T(8,128)(2,1)S(1)} all-gather(bf16[192,256]{1,0:T(8,128)(2,1)S(1)} %bitcast.28), channel_id=1, replica_groups=mesh['xh'=2,'y'=4,'core'=2,'zh'=4,'zl'=4,'xl'=2] {'zh'}, dimensions={0}, use_global_device_ids=true | all-gather | bytes 491520 | tf_op jit(solution)/shard_map/all_gather | solution.py:225
  50.2 1.9 %collective-permute-start.5 = (bf16[192,3072]{1,0:T(8,128)(2,1)S(1)}, bf16[192,3072]{1,0:T(8,128)(2,1)S(1)}, u32[]{:S(2)}, u32[]{:S(2)}) collective-permute-start(bf16[192,3072]{1,0:T(8,128)(2,1)S(1)} %collective-permute-done.refs_7_.refs_9_), channel_id=1, source_target_pairs={{0,32},{32,0},{1,33},{33,1},{2,34},{34,2},{3,35},{35,3},{4,36},{36... | collective-permute-start | bytes 3538952 | tf_op jit(solution)/shard_map/ppermute | solution.py:227
  52.2 2.9 %collective-permute-start.2 = (bf16[768,256]{1,0:T(8,128)(2,1)S(1)}, bf16[768,256]{1,0:T(8,128)(2,1)S(1)}, u32[]{:S(2)}, u32[]{:S(2)}) collective-permute-start(bf16[768,256]{1,0:T(8,128)(2,1)S(1)} %all_gather.6.refs_0_), channel_id=1, source_target_pairs={{0,2},{2,4},{4,6},{6,8},{8,10},{10,12},{12,14},{14,16},{16,18},{18... | collective-permute-start | bytes 1179656 | tf_op jit(solution)/shard_map/ppermute | solution.py:185
  55.1 6.5 %collective-permute-start.1 = (bf16[768,256]{1,0:T(8,128)(2,1)S(1)}, bf16[768,256]{1,0:T(8,128)(2,1)}, u32[]{:S(2)}, u32[]{:S(2)}) collective-permute-start(bf16[768,256]{1,0:T(8,128)(2,1)S(1)} %all_gather.6.refs_0_), channel_id=1, source_target_pairs={{0,30},{2,0},{4,2},{6,4},{8,6},{10,8},{12,10},{14,12},{16,14},{18,... | collective-permute-start | bytes 1179656 | tf_op jit(solution)/shard_map/ppermute | solution.py:185
  61.6 4.4 %collective-permute-start.4 = (bf16[384,256]{1,0:T(8,128)(2,1)S(1)}, bf16[384,256]{1,0:T(8,128)(2,1)}, u32[]{:S(2)}, u32[]{:S(2)}) collective-permute-start(bf16[384,256]{1,0:T(8,128)(2,1)S(1)} %get-tuple-element.31), channel_id=1, source_target_pairs={{0,28},{2,30},{4,0},{6,2},{8,4},{10,6},{12,8},{14,10},{16,12},{18,... | collective-permute-start | bytes 589832 | tf_op jit(solution)/shard_map/ppermute | solution.py:185
  66.0 2.4 %collective-permute-start.3 = (bf16[384,256]{1,0:T(8,128)(2,1)S(1)}, bf16[384,256]{1,0:T(8,128)(2,1)}, u32[]{:S(2)}, u32[]{:S(2)}) collective-permute-start(bf16[384,256]{1,0:T(8,128)(2,1)S(1)} %get-tuple-element.32), channel_id=1, source_target_pairs={{0,4},{2,6},{4,8},{6,10},{8,12},{10,14},{12,16},{14,18},{16,20},{1... | collective-permute-start | bytes 589832 | tf_op jit(solution)/shard_map/ppermute | solution.py:185
  69.0 17.1 %collective-permute-done.4.refs_4_ = bf16[384,256]{1,0:T(8,128)(2,1)} collective-permute-done((bf16[384,256]{1,0:T(8,128)(2,1)S(1)}, bf16[384,256]{1,0:T(8,128)(2,1)}, u32[]{:S(2)}, u32[]{:S(2)}) %collective-permute-start.4) | collective-permute-done | bytes 196640 | tf_op jit(solution)/shard_map/ppermute | solution.py:185
  86.2 0.7 copy-done.5
  87.3 8.7 %forward.1 = (bf16[3072,256]{1,0:T(8,128)(2,1)}, f32[2,256,256]{2,1,0:T(8,128)}, f32[2,96,256]{2,1,0:T(8,128)}, f32[2,96,256]{2,1,0:T(8,128)}, f32[2,8,256]{2,1,...) custom-call(s32[7]{0:T(128)} %stack.31.place, ...), custom_call_target="tpu_custom_call" | custom-call | flops 2000000000 | bytes 14000000 | tf_op jit(solution)/shard_map/forward/pallas_call | solution.py:250
  96.0 3.3 %all-gather.2.cloned.1.call-done.refs_7_ = bf16[3072,256]{1,0:T(8,128)(2,1)} async-done(((bf16[192,256]{1,0:T(8,128)(2,1)}), bf16[3072,256]{1,0:T(8,128)(2,1)}) %all-gather.2.cloned.1.call-update) | async-done | bytes 1572880 | tf_op jit(solution)/shard_map/all_gather | solution.py:223
  99.3 9.8 %backward.1 = bf16[2,2,8,192,384]{4,3,2,1,0:T(8,128)(2,1)} custom-call(s32[7]{0:T(128)} %stack.31.place, bf16[3072,256]{1,0:T(8,128)(2,1)} %get-tuple-element.22.refs_0_, f32[2,256,256]{2,1,0:T(8,128)} %get-tuple-element.23.refs_1_, f32[2,96,256]{2,1,0:T(8,128)} %get-tuple-element.24.refs_2_, f32[2,96,256]{2,1,0:T(8,128)} %get-tuple-element.25.refs_3_, ...), custom_call_target="tpu_custom_call" | custom-call | flops 1000000 | bytes 100000 | tf_op jit(solution)/shard_map/backward/pallas_call | solution.py:273
  109.1 12.8 %all_to_all.20 = bf16[2,2,8,192,384]{4,3,2,1,0:T(8,128)(2,1)} all-to-all(bf16[2,2,8,192,384]{4,3,2,1,0:T(8,128)(2,1)} %backward.1), channel_id=1, replica_groups=mesh['xh'=2,'y'=4,'core'=2,'zh'=4,'zl'=4,'xl'=2] {'core'}, dimensions={0} | all-to-all | bytes 9437184 | tf_op jit(solution)/shard_map/all_to_all | solution.py:290
  121.8 3.5 %reduce_sum.24 = bf16[2,8,192,384]{3,2,1,0:T(8,128)(2,1)S(1)} reduce(bf16[2,2,8,192,384]{4,3,2,1,0:T(8,128)(2,1)} %all_to_all.20, bf16[]{:T(256)} %constant.50.clone.1), dimensions={0}, to_apply=%region_1.2 | reduce | flops 1179648 | bytes 7077890 | tf_op jit(solution)/shard_map/reduce_sum | solution.py:291
  125.3 36.2 %all_to_all.21 = bf16[16,192,384]{2,1,0:T(8,128)(2,1)} all-to-all(bf16[16,192,384]{2,1,0:T(8,128)(2,1)S(1)} %bitcast.22), channel_id=1, replica_groups=mesh['xh'=2,'y'=4,'core'=2,'zh'=4,'zl'=4,'xl'=2] {'xl','xh','y'}, dimensions={0} | all-to-all | bytes 4718592 | tf_op jit(solution)/shard_map/all_to_all | solution.py:292
  161.6 9.0 %reduce-scatter.2.cloned.1.call-done = bf16[192,256]{1,0:T(8,128)(2,1)} async-done(((bf16[3072,256]{1,0:T(8,128)(2,1)}), bf16[192,256]{1,0:T(8,128)(2,1)}) %reduce-scatter.2.cloned.1.call-update) | async-done | bytes 98320 | tf_op jit(solution)/shard_map/reduce_scatter | solution.py:270
  170.6 3.3 %all-to-all-start.3 = ((bf16[2,96,256]{2,1,0:T(8,128)(2,1)}), bf16[2,96,256]{2,1,0:T(8,128)(2,1)S(1)}, u32[]{:S(2)}, u32[]{:S(2)}) async-start(bf16[2,96,256]{2,1,0:T(8,128)(2,1)} %bitcast.30), calls=%async_computation.4 | async-start | bytes 196608 | tf_op jit(solution)/shard_map/all_to_all | solution.py:297
  173.9 2.0 %reduce_sum.25 = bf16[192,384]{1,0:T(8,128)(2,1)S(1)} reduce(bf16[16,192,384]{2,1,0:T(8,128)(2,1)} %all_to_all.21, bf16[]{:T(256)} %constant.50.clone.1), dimensions={0}, to_apply=%region_2.3 | reduce | flops 1105920 | bytes 2506754 | tf_op jit(solution)/shard_map/reduce_sum | solution.py:296
  175.9 0.7 slice.41
  176.6 1.6 all-to-all-done.3
  (27 shorter events, 3.3 us)
Async XLA Ops:
  7.2 6.2 %copy-start.3 = (bf16[3072,288]{0,1:T(8,128)(2,1)S(1)}, bf16[3072,288]{0,1:T(8,128)(2,1)}, u32[]{:S(2)}) copy-start(bf16[3072,288]{0,1:T(8,128)(2,1)} %param.5) | copy-start | bytes 5308420
  8.9 8.2 %all-to-all-start = ((bf16[2,2,96,256]{3,2,1,0:T(8,128)(2,1)}), bf16[2,2,96,256]{3,2,1,0:T(8,128)(2,1)S(1)}, u32[]{:S(2)}, u32[]{:S(2)}) async-start(bf16[2,2,96,256]{3,2,1,0:T(8,128)(2,1)} %bitcast.9), calls=%async_computation | async-start | bytes 393216 | tf_op jit(solution)/shard_map/all_to_all | solution.py:210
  12.3 87.0 %all-gather.2.cloned.1.call-start = ((), (), s32[]{:S(2)}) async-start(), calls=%async_computation.6 | async-start | bytes 1671168 | tf_op jit(solution)/shard_map/all_gather | solution.py:223
  17.8 152.7 %reduce-scatter.2.cloned.1.call-start = ((), (), s32[]{:S(2)}) async-start(), calls=%async_computation.5 | async-start | bytes 1671168 | tf_op jit(solution)/shard_map/reduce_scatter | solution.py:270
  17.9 32.4 %collective-permute-start = (bf16[192,3072]{1,0:T(8,128)(2,1)S(1)}, bf16[192,3072]{1,0:T(8,128)(2,1)S(1)}, u32[]{:S(2)}, u32[]{:S(2)}) collective-permute-start(bf16[192,3072]{1,0:T(8,128)(2,1)S(1)} %pad_maximum_fusion), channel_id=1, source_target_pairs={{0,1},{1,0},{2,3},{3,2},{4,5},{5,4},{6,7},{7,6},{8,9},{9,8},{10,11... | collective-permute-start | bytes 3538952 | tf_op jit(solution)/shard_map/ppermute | solution.py:224
  50.2 36.0 %copy-start = (bf16[768,256]{1,0:T(8,128)(2,1)}, bf16[768,256]{1,0:T(8,128)(2,1)S(1)}, u32[]{:S(2)}) copy-start(bf16[768,256]{1,0:T(8,128)(2,1)S(1)} %all_gather.6.refs_0_) | copy-start | bytes 1179652
  50.2 36.0 %copy-start.1 = (bf16[192,3072]{1,0:T(8,128)(2,1)}, bf16[192,3072]{1,0:T(8,128)(2,1)S(1)}, u32[]{:S(2)}) copy-start(bf16[192,3072]{1,0:T(8,128)(2,1)S(1)} %collective-permute-done.refs_7_.refs_9_) | copy-start | bytes 3538948
  50.2 35.9 %collective-permute-start.5 = (bf16[192,3072]{1,0:T(8,128)(2,1)S(1)}, bf16[192,3072]{1,0:T(8,128)(2,1)S(1)}, u32[]{:S(2)}, u32[]{:S(2)}) collective-permute-start(bf16[192,3072]{1,0:T(8,128)(2,1)S(1)} %collective-permute-done.refs_7_.refs_9_), channel_id=1, source_target_pairs={{0,32},{32,0},{1,33},{33,1},{2,34},{34,2},{3,35},{35,3},{4,36},{36... | collective-permute-start | bytes 3538952 | tf_op jit(solution)/shard_map/ppermute | solution.py:227
  52.2 34.0 %collective-permute-start.2 = (bf16[768,256]{1,0:T(8,128)(2,1)S(1)}, bf16[768,256]{1,0:T(8,128)(2,1)S(1)}, u32[]{:S(2)}, u32[]{:S(2)}) collective-permute-start(bf16[768,256]{1,0:T(8,128)(2,1)S(1)} %all_gather.6.refs_0_), channel_id=1, source_target_pairs={{0,2},{2,4},{4,6},{6,8},{8,10},{10,12},{12,14},{14,16},{16,18},{18... | collective-permute-start | bytes 1179656 | tf_op jit(solution)/shard_map/ppermute | solution.py:185
  55.1 31.1 %collective-permute-start.1 = (bf16[768,256]{1,0:T(8,128)(2,1)S(1)}, bf16[768,256]{1,0:T(8,128)(2,1)}, u32[]{:S(2)}, u32[]{:S(2)}) collective-permute-start(bf16[768,256]{1,0:T(8,128)(2,1)S(1)} %all_gather.6.refs_0_), channel_id=1, source_target_pairs={{0,30},{2,0},{4,2},{6,4},{8,6},{10,8},{12,10},{14,12},{16,14},{18,... | collective-permute-start | bytes 1179656 | tf_op jit(solution)/shard_map/ppermute | solution.py:185
  61.6 24.6 %collective-permute-start.4 = (bf16[384,256]{1,0:T(8,128)(2,1)S(1)}, bf16[384,256]{1,0:T(8,128)(2,1)}, u32[]{:S(2)}, u32[]{:S(2)}) collective-permute-start(bf16[384,256]{1,0:T(8,128)(2,1)S(1)} %get-tuple-element.31), channel_id=1, source_target_pairs={{0,28},{2,30},{4,0},{6,2},{8,4},{10,6},{12,8},{14,10},{16,12},{18,... | collective-permute-start | bytes 589832 | tf_op jit(solution)/shard_map/ppermute | solution.py:185
  66.0 20.2 %collective-permute-start.3 = (bf16[384,256]{1,0:T(8,128)(2,1)S(1)}, bf16[384,256]{1,0:T(8,128)(2,1)}, u32[]{:S(2)}, u32[]{:S(2)}) collective-permute-start(bf16[384,256]{1,0:T(8,128)(2,1)S(1)} %get-tuple-element.32), channel_id=1, source_target_pairs={{0,4},{2,6},{4,8},{6,10},{8,12},{10,14},{12,16},{14,18},{16,20},{1... | collective-permute-start | bytes 589832 | tf_op jit(solution)/shard_map/ppermute | solution.py:185
  86.2 0.7 copy-start.5
  86.2 1.1 copy-start.2
  170.6 7.6 %all-to-all-start.3 = ((bf16[2,96,256]{2,1,0:T(8,128)(2,1)}), bf16[2,96,256]{2,1,0:T(8,128)(2,1)S(1)}, u32[]{:S(2)}, u32[]{:S(2)}) async-start(bf16[2,96,256]{2,1,0:T(8,128)(2,1)} %bitcast.30), calls=%async_computation.4 | async-start | bytes 196608 | tf_op jit(solution)/shard_map/all_to_all | solution.py:297
  175.9 2.9 %copy-start.4 = (bf16[192,384]{1,0:T(8,128)(2,1)}, bf16[192,384]{1,0:T(8,128)(2,1)S(1)}, u32[]{:S(2)}) copy-start(bf16[192,384]{1,0:T(8,128)(2,1)S(1)} %reduce_sum.25) | copy-start | bytes 442372
Sparse Core Ops, SparseCore 0:
  17.9 81.3 all-gather.1
  102.1 68.4 reduce-scatter.1
